TPU v7x, 32 devices: a whole 2x2x4 slice. The times are simulated.
32 devices in a mesh: seq: 2 (over x), head: 4 (over z), dp: 4 (over y, core).
Axes of the slice: x: 2, y: 2, z: 4, core: 2. Of those that a mesh axis runs over, the one named last changes fastest.
Arguments:
- layer_input: bfloat16 [4, 1024, 2048], P('dp', 'seq'), may hold values from -6 to 6
- w_query: bfloat16 [2048, 2048], P(None, 'head'), may hold values from -0.125 to 0.125
- w_key: bfloat16 [2048, 2048], P(None, 'head'), may hold values from -0.125 to 0.125
- w_value: bfloat16 [2048, 2048], P(None, 'head'), may hold values from -0.125 to 0.125
- w_out: bfloat16 [2048, 2048], P('head'), may hold values from -0.125 to 0.125
- out_grad: bfloat16 [4, 1024, 2048], P('dp', 'seq'), may hold values from -6 to 6
Outputs:
- input_grad: bfloat16 [4, 1024, 2048], P('dp', 'seq', 'head')
- grad_query: float32 [2048, 2048], P(('seq', 'dp'), 'head')
- grad_key: float32 [2048, 2048], P(('seq', 'dp'), 'head')
- grad_value: float32 [2048, 2048], P(('seq', 'dp'), 'head')
- grad_out: float32 [2048, 2048], P('head', ('seq', 'dp'))
All inputs are finite; a program needn't handle non-finite values.
Results may differ from a plain program's by a relative error of at most 0.0073.
Values sent between devices are 32-bit elements; how exact they have to be, the bound alone decides.
No kernel may reach another device: no remote copies, remote signals or barrier semaphores. Data moves between devices by JAX's collectives and lax.ppermute only.
A program may use at most 128 MiB of HBM per device.

v0:
```python
import functools

import jax
import jax.numpy as jnp
from jax import lax
from jax.experimental import pallas as pl
from jax.experimental.pallas import tpu as pltpu
from jax.sharding import PartitionSpec as P

HEAD_DIM = 128
BF16 = jnp.bfloat16
F32 = jnp.float32
MIB = 1024 * 1024
PLANNED = (2, 4, 4)
NN = ((1,), (0,))
NT = ((1,), (1,))
TN = ((0,), (0,))
ANYWHERE = pl.BlockSpec(memory_space=pl.ANY)
IN_VMEM = pl.BlockSpec(memory_space=pltpu.VMEM)
IN_SMEM = pl.BlockSpec(memory_space=pltpu.SMEM)


def dot(a, b, dims):
    return lax.dot_general(a, b, (dims, ((), ())), preferred_element_type=F32)


def shaped(shape, dtype):
    return jax.ShapeDtypeStruct(shape, dtype)


def params(mib):
    return pltpu.CompilerParams(vmem_limit_bytes=mib * MIB)


def cost(flops, size):
    return pl.CostEstimate(flops=flops, bytes_accessed=size, transcendentals=0)


class Place:
    def __init__(self, number, sizes):
        _, n_head, n_dp = sizes
        self.dp = lax.rem(number, n_dp)
        self.head = lax.rem(lax.div(number, n_dp), n_head)
        self.seq = lax.div(number, n_head * n_dp)
        self.core = lax.rem(self.dp, 2)


def position_scale(start, rows):
    positions = (start + lax.broadcasted_iota(jnp.int32, (rows, 1), 0)).astype(F32)
    return 1.0 / jnp.sqrt(HEAD_DIM * (positions + 1.0))


def project_kernel(
    number_ref, x_hbm, o_hbm, wq_hbm, wk_hbm, wv_hbm, wo_hbm,
    q_ref, k_ref, v_ref, g_ref, xo_ref, wq_ref, wk_ref, wv_ref, *rest, one_state, sizes,
):
    states, (wo_ref, sems) = rest[:-2], rest[-2:]
    rows, hd = q_ref.shape
    x_ref, o_ref = xo_ref.at[0], xo_ref.at[1]
    mid = x_ref.shape[1] // 2
    lower, upper = pl.ds(0, mid), pl.ds(mid, mid)
    parts = (
        (x_hbm.at[:, lower], x_ref.at[:, lower]),
        (wk_hbm.at[lower], wk_ref.at[lower]),
        (x_hbm.at[:, upper], x_ref.at[:, upper]),
        (wk_hbm.at[upper], wk_ref.at[upper]),
        (wv_hbm, wv_ref),
        (wq_hbm, wq_ref),
        (o_hbm, o_ref),
        (wo_hbm, wo_ref),
    )
    copies = [pltpu.make_async_copy(a, b, sems.at[i]) for i, (a, b) in enumerate(parts)]
    for c in copies[:4]:
        c.start()
    copies[0].wait()
    copies[1].wait()
    for c in copies[4:]:
        c.start()
    keys = dot(x_ref[:, lower], wk_ref[lower, :], NN)
    copies[2].wait()
    copies[3].wait()
    k_ref[...] = (keys + dot(x_ref[:, upper], wk_ref[upper, :], NN)).astype(BF16)
    copies[4].wait()
    v_ref[...] = dot(x_ref[...], wv_ref[...], NN).astype(BF16)
    copies[5].wait()
    q_ref[...] = dot(x_ref[...], wq_ref[...], NN).astype(BF16)
    copies[6].wait()
    copies[7].wait()
    seq_at = Place(number_ref[0], sizes).seq
    scale = position_scale(seq_at * rows, rows)
    g_ref[...] = (dot(o_ref[...], wo_ref[...], NT) * scale).astype(BF16)

    def state(a_ref, b_ref, out_ref):
        for h in range(hd // HEAD_DIM):
            at = pl.ds(h * HEAD_DIM, HEAD_DIM)
            out_ref[h] = dot(a_ref[:, at], b_ref[:, at], TN)

    if one_state:
        pl.when(seq_at == 0)(lambda: state(k_ref, v_ref, states[0]))
        pl.when(seq_at != 0)(lambda: state(q_ref, g_ref, states[0]))
    else:
        state(k_ref, v_ref, states[0])
        state(q_ref, g_ref, states[1])


def project(number, sizes, in_rows, grad_rows, w_query, w_key, w_value, w_out):
    rows, width = in_rows.shape
    hd = w_query.shape[1]
    one_state = sizes == PLANNED
    n_states = 1 if one_state else 2
    args = [
        pltpu.with_memory_space_constraint(a, pltpu.HBM)
        for a in (in_rows, grad_rows, w_query, w_key, w_value, w_out)
    ]
    outs = [(rows, hd)] * 4 + [(2, rows, width)] + [(width, hd)] * 3
    out_shape = [pltpu.VMEM(s, BF16) for s in outs]
    out_shape += [pltpu.VMEM((hd // HEAD_DIM, HEAD_DIM, HEAD_DIM), F32)] * n_states
    return pl.pallas_call(
        functools.partial(project_kernel, one_state=one_state, sizes=sizes),
        out_shape=out_shape,
        in_specs=[IN_SMEM] + [ANYWHERE] * 6,
        out_specs=[IN_VMEM] * len(out_shape),
        scratch_shapes=[pltpu.VMEM((hd, width), BF16), pltpu.SemaphoreType.DMA((8,))],
        compiler_params=params(16),
        cost_estimate=cost(8 * rows * width * hd, 14 * MIB),
        name="project",
    )(number, *args)


def call(kernel, name, out_shape, args, flops, after=(), place=None, in_place=False):
    n, n_after = len(args), len(after)
    numbers = [] if place is None else [place[0]]

    def body(*refs):
        first = [Place(refs[0][0], place[1])] if numbers else []
        refs = refs[len(numbers) :]
        kernel(*first, *refs[:n], *refs[n + n_after :])

    many = isinstance(out_shape, (list, tuple))
    return pl.pallas_call(
        body,
        out_shape=out_shape,
        in_specs=[IN_SMEM] * len(numbers) + [IN_VMEM] * n + [ANYWHERE] * n_after,
        out_specs=[IN_VMEM] * len(out_shape) if many else IN_VMEM,
        compiler_params=params(16),
        cost_estimate=cost(flops, 2 * MIB),
        input_output_aliases={len(numbers) + n - 1: 0} if in_place else {},
        name=name,
    )(*numbers, *args, *after)


def attend_kernel(place, q_all, k_all, v_all, g_all, *rest, which, with_state):
    state_ref, out_ref = rest[0] if with_state else None, rest[-1]
    rows, hd = q_all.shape
    half = rows // 2
    top, low = slice(0, half), slice(half, rows)

    def causal(a, b):
        r = lax.broadcasted_iota(jnp.int32, (half, half), 0)
        c = lax.broadcasted_iota(jnp.int32, (half, half), 1)
        diagonal = r >= c
        s00 = jnp.where(diagonal, dot(a[top], b[top], NT), 0.0).astype(BF16)
        s10 = dot(a[low], b[top], NT).astype(BF16)
        s11 = jnp.where(diagonal, dot(a[low], b[low], NT), 0.0).astype(BF16)
        return s00, s10, s11

    def per_head(body):
        def step(h, carry):
            at = pl.ds(pl.multiple_of(h * HEAD_DIM, HEAD_DIM), HEAD_DIM)
            state = state_ref[h].astype(BF16) if with_state else None

            def put(slot, halves, cross, dims, scale=None):
                for rows_at, value in zip((top, low), halves):
                    if with_state:
                        value = value + dot(cross[rows_at], state, dims)
                    if scale is not None:
                        value = value * scale[rows_at]
                    out_ref[slot, rows_at, at] = value.astype(BF16)

            body([r[:, at] for r in (q_all, k_all, v_all, g_all)], put)
            return carry

        lax.fori_loop(0, hd // HEAD_DIM, step, 0, unroll=2)

    def forward():
        scale = position_scale(place.seq * rows, rows)

        def body(heads, put):
            q, k, v, g = heads
            for slot, a, b, c, dims in ((0, q, k, v, NN), (1, g, v, k, NT)):
                s00, s10, s11 = causal(a, b)
                halves = (dot(s00, c[top], NN), dot(s10, c[top], NN) + dot(s11, c[low], NN))
                put(slot, halves, a, dims, scale if slot == 0 else None)

        per_head(body)

    def backward():
        def body(heads, put):
            q, k, v, g = heads
            for slot, a, b, c, dims in ((2, q, k, g, NN), (3, g, v, q, NT)):
                s00, s10, s11 = causal(a, b)
                halves = (dot(s00, c[top], TN) + dot(s10, c[low], TN), dot(s11, c[low], TN))
                put(slot, halves, b, dims)

        per_head(body)

    chosen = which(place)
    pl.when(chosen == 0)(forward)
    pl.when(chosen != 0)(backward)


def attend(place, which, q, k, v, g, state=None, into=None, after=()):
    rows, hd = q.shape
    args = [q, k, v, g] + [a for a in (state, into) if a is not None]
    return call(
        functools.partial(attend_kernel, which=which, with_state=state is not None),
        "attend",
        shaped((4, rows, hd), BF16),
        args,
        128 * rows * rows * hd,
        after,
        place,
        in_place=into is not None,
    )


def head_terms_kernel(place, d_ref, wq_ref, wk_ref, wv_ref, out_ref, *, shard):
    width = out_ref.shape[1]
    step = min(width, 256)
    start = shard(place) * width
    for i in range(width // step):
        rows = pl.ds(pl.multiple_of(start + i * step, step), step)
        out_ref[:, pl.ds(i * step, step)] = (
            dot(d_ref[1], wq_ref[rows, :], NT)
            + dot(d_ref[3], wk_ref[rows, :], NT)
            + dot(d_ref[2], wv_ref[rows, :], NT)
        )


def head_terms(place, results, weights, shard, shards, after=()):
    width, hd = weights[0].shape
    rows = results.shape[1]
    return call(
        functools.partial(head_terms_kernel, shard=shard),
        "head_terms",
        shaped((rows, width // shards), F32),
        [results, *weights],
        6 * rows * width // shards * hd,
        after,
        place,
    )


def add_kernel(*refs):
    total = refs[0][...]
    for ref in refs[1:-1]:
        total = total + ref[...]
    refs[-1][...] = total.astype(refs[-1].dtype)


def add(arrays, dtype, after=()):
    return call(add_kernel, "add", shaped(arrays[0].shape, dtype), list(arrays), 0, after)


def column_block(place, i):
    return (place.seq ^ (i // 2 % 2)) * 4 + (place.dp ^ (i % 2 * 2 + i // 4))


def fill_tiles(place, xo_ref, d_ref, pair, side, blocks, scale, added, outs):
    half = d_ref.shape[2] // 2
    block = outs[0].shape[1]
    features = pl.ds(pl.multiple_of(side * half, half), half)
    for i, b in enumerate(blocks):
        columns = pl.ds(pl.multiple_of(column_block(place, b) * block, block), block)
        for t, rows in enumerate((1 - pair, 0)):
            tile = dot(xo_ref[rows, :, columns], d_ref[2 * pair + t, :, features], TN) * scale
            for read in added:
                tile = tile + read(i, t)
            outs[i][t] = tile


def other_core_kernel(place, xo_ref, d_ref, out_ref, *, early, slot, scale):
    outs = [out_ref.at[i] for i in range(4)]
    pair, side = place.seq ^ early, 1 - place.core ^ slot
    fill_tiles(place, xo_ref, d_ref, pair, side, (4, 5, 6, 7), scale, (), outs)


def first_hop_kernel(place, xo_ref, d_ref, far_ref, out_ref, *, early, slot, scale):
    pair, side = place.seq ^ early, place.core ^ slot
    blocks = (2 - side, 3)
    outs = [out_ref.at[i] for i in range(2)]
    added = (lambda i, t: far_ref[blocks[i], t],)
    fill_tiles(place, xo_ref, d_ref, pair, side, blocks, scale, added, outs)


def second_hop_kernel(
    place, xo_ref, d_ref, far0_ref, far1_ref, over0_ref, over1_ref, keep_ref, send_ref, *, slot, scale
):
    far, over = (far0_ref, far1_ref), (over0_ref, over1_ref)
    side = place.core ^ slot
    blocks = (0, 1 + side)
    for p in (0, 1):
        added = (
            lambda i, t: jnp.where(side == 0, far[1 - p][blocks[i], t], far[p][blocks[i], t]),
            lambda i, t: over[p][i, t],
        )
        pair = place.seq ^ p ^ 1 - side
        outs = (keep_ref.at[p], send_ref.at[p])
        fill_tiles(place, xo_ref, d_ref, pair, side, blocks, scale, added, outs)


def collect_kernel(place, *refs):
    kept, moved, (out_ref, query_ref, key_ref, value_ref) = refs[:2], refs[2:4], refs[4:]
    half = query_ref.shape[1] // 2
    for side in (0, 1):
        at = pl.ds(side * half, half)

        def total(pair, t):
            p = place.seq ^ pair
            first = kept[side][p if side else 1 - p, t] + moved[side][1 - p, t]
            second = kept[1 - side][p if side else 1 - p, t] + moved[1 - side][1 - p, t]
            return jnp.where(place.core == 0, first, second)

        out_ref[at, :] = total(0, 0).T
        query_ref[:, at] = total(0, 1)
        value_ref[:, at] = total(1, 0)
        key_ref[:, at] = total(1, 1)


def collect(place, kept, moved, after):
    block, half = kept[0].shape[2:]
    tall, wide = shaped((block, 2 * half), F32), shaped((2 * half, block), F32)
    outs = [wide, tall, tall, tall]
    return call(collect_kernel, "collect", outs, [*kept, *moved], 0, after, place)


def states_before(x, axis, reverse):
    peers, here = (lax.axis_size(axis), lax.axis_index(axis))
    everything = lax.all_gather(x, axis)
    at = jnp.arange(peers)
    reached = at > here if reverse else at < here
    return jnp.sum(jnp.where(reached[:, None, None, None], everything, 0.0), axis=0)


def swap(x, axis, bit):
    return lax.ppermute(x, axis, [(i, i ^ bit) for i in range(lax.axis_size(axis))])


def local(layer_input, w_query, w_key, w_value, w_out, out_grad):
    num_rows = layer_input.shape[1]
    n_seq, n_head, n_dp = (lax.axis_size(a) for a in ("seq", "head", "dp"))
    scale = float(n_seq * n_dp * num_rows) ** -0.5

    sizes = (n_seq, n_head, n_dp)
    number = (lax.axis_index("seq") * n_head + lax.axis_index("head")) * n_dp + lax.axis_index("dp")
    number = number.astype(jnp.int32).reshape(1)
    place = (number, sizes)
    q, k, v, g, xo, *kept = project(
        number, sizes, layer_input[0], out_grad[0], w_query, w_key, w_value, w_out
    )
    weights, states = kept[:3], kept[3:]

    if sizes != PLANNED:
        prefix = states_before(states[0], "seq", False)
        suffix = states_before(states[1], "seq", True)
        d = attend(place, lambda at: 0, q, k, v, g, prefix)
        d = attend(place, lambda at: 1, q, k, v, g, suffix, d)
        terms = head_terms(place, d, weights, lambda at: 0, 1)

        def reduced(rows, d):
            return lax.psum_scatter(
                dot(rows, d, TN) * scale, ("seq", "dp"), scatter_dimension=0, tiled=True
            )

        return (
            lax.psum_scatter(terms, "head", scatter_dimension=1, tiled=True).astype(BF16)[None],
            reduced(xo[0], d[1]),
            reduced(xo[0], d[3]),
            reduced(xo[0], d[2]),
            reduced(xo[1], d[0]).T,
        )

    def term(flip, after):
        return head_terms(place, d, weights, lambda at: at.head ^ flip, n_head, after)

    def hop(array, slot, second):
        pairs = []
        for i in range(8):
            side = i % 2 ^ slot
            pairs.append((i, i ^ (4 if side == second else 2)))
        return lax.ppermute(array, ("seq", "dp"), pairs)

    block, half = xo.shape[2] // 8, q.shape[1] // 2
    tile = (2, block, half)
    flops = 4 * num_rows * block * half

    def to_core(d, early, slot, after):
        kernel = functools.partial(other_core_kernel, early=early, slot=slot, scale=scale)
        out = shaped((4, *tile), F32)
        array = call(kernel, "other_core", out, [xo, d], 4 * flops, after, place)
        return array, swap(array, "dp", 1)

    def first_hop(early, slot, after):
        kernel = functools.partial(first_hop_kernel, early=early, slot=slot, scale=scale)
        out = shaped((2, *tile), F32)
        args = [xo, d, far[early][slot]]
        array = call(kernel, "first_hop", out, args, 2 * flops, after, place)
        return array, hop(array, slot, 0)

    def second_hop(slot, over, after):
        kernel = functools.partial(second_hop_kernel, slot=slot, scale=scale)
        args = [xo, d, far[0][slot], far[1][slot], *over]
        outs = [shaped((2, *tile), F32)] * 2
        keep, leave = call(kernel, "second_hop", outs, args, 4 * flops, after, place)
        return keep, hop(leave, slot, 1)

    far = ([None, None], [None, None])
    state = swap(states[0], "seq", 1)
    early = attend(place, lambda at: at.seq, q, k, v, g)
    at, far[0][0] = to_core(early, 0, 0, [])
    at, far[0][1] = to_core(early, 0, 1, [at])
    d = attend(place, lambda at: 1 - at.seq, q, k, v, g, state, early, [at])
    at, far[1][0] = to_core(d, 1, 0, [])
    at, far[1][1] = to_core(d, 1, 1, [at])
    at, over1 = first_hop(0, 0, [at])
    at, over2 = first_hop(0, 1, [at])
    t3 = term(3, [at])
    t3_in = swap(t3, "head", 1)
    at, over3 = first_hop(1, 0, [t3])
    t1 = term(1, [at])
    t1_in = swap(t1, "head", 1)
    t2 = term(2, [t1])
    t0 = term(0, [t2])
    at, over4 = first_hop(1, 1, [t0, over1])
    t2 = add([t2, t3_in], F32, [at, over2])
    t2_in = swap(t2, "head", 2)
    keep0, moved0 = second_hop(0, (over1, over3), [t2])
    keep1, moved1 = second_hop(1, (over2, over4), [keep0])
    input_grad = add([t0, t1_in, t2_in], BF16, [keep1])
    kept, moved = (keep0, keep1), (moved0, moved1)
    grad_out, grad_query, grad_key, grad_value = collect(place, kept, moved, [])
    return (input_grad[None], grad_query, grad_key, grad_value, grad_out)


def solution(mesh):
    return jax.shard_map(
        local,
        mesh=mesh,
        in_specs=(
            P("dp", "seq", None),
            P(None, "head"),
            P(None, "head"),
            P(None, "head"),
            P("head", None),
            P("dp", "seq", None),
        ),
        out_specs=(
            P("dp", "seq", "head"),
            P(("seq", "dp"), "head"),
            P(("seq", "dp"), "head"),
            P(("seq", "dp"), "head"),
            P("head", ("seq", "dp")),
        ),
        check_vma=False,
    )
```

profile of v0, /device:TPU:0, one launch (start us, length us, event | category | flops | bytes accessed | tf_op | source)
XLA Modules:
  0.0 103.1 jit_solution(9409993900731700235)
XLA Ops:
  0.6 7.6 %project.1 = (bf16[512,512]{1,0:T(8,128)(2,1)S(1)}, bf16[512,512]{1,0:T(8,128)(2,1)S(1)}, bf16[512,512]{1,0:T(8,128)(2,1)S(1)}, bf16[512,512]{1,0:T(8,128)(2,1)S...) custom-call(s32[1]{0:T(128)} %bitcast.number_ref.refs_0_, ...), custom_call_target="tpu_custom_call" | custom-call | flops 4294967296 | bytes 14680064 | tf_op jit(solution)/shard_map/project/pallas_call | solution.py:118
  8.3 3.0 %collective-permute-start = (f32[4,128,128]{2,1,0:T(8,128)S(1)}, f32[4,128,128]{2,1,0:T(8,128)S(1)}, u32[]{:S(2)}, u32[]{:S(2)}) collective-permute-start(f32[4,128,128]{2,1,0:T(8,128)S(1)} %get-tuple-element.26), channel_id=1, source_target_pairs={{0,16},{16,0},{1,17},{17,1},{2,18},{18,2},{3,19},{19,3},{4,20},{20... | collective-permute-start | bytes 786440 | tf_op jit(solution)/shard_map/ppermute | solution.py:346
  11.3 2.6 %attend.2.refs_2_.refs_6_ = bf16[4,512,512]{2,1,0:T(8,128)(2,1)S(1)} custom-call(s32[1]{0:T(128)} %bitcast.number_ref.refs_0_, bf16[512,512]{1,0:T(8,128)(2,1)S(1)} %get-tuple-element.22.refs_1_, bf16[512,512]{1,0:T(8,128)(2,1)S(1)} %get-tuple-element.23.refs_2_, bf16[512,512]{1,0:T(8,128)(2,1)S(1)} %get-tuple-element.24.refs_3_, ...), custom_call_target="tpu_custom_call" | custom-call | flops 17179869184 | bytes 2097152 | tf_op jit(solution)/shard_map/attend/pallas_call | solution.py:140
  13.9 0.8 other_core.4.refs_3_
  14.7 0.1 collective-permute-start.3
  14.8 0.9 other_core.5.refs_7_
  15.7 0.5 collective-permute-start.2
  16.2 1.4 %collective-permute-done.refs_5_ = f32[4,128,128]{2,1,0:T(8,128)S(1)} collective-permute-done((f32[4,128,128]{2,1,0:T(8,128)S(1)}, f32[4,128,128]{2,1,0:T(8,128)S(1)}, u32[]{:S(2)}, u32[]{:S(2)}) %collective-permute-start) | collective-permute-done | bytes 262176 | tf_op jit(solution)/shard_map/ppermute | solution.py:346
  17.6 3.7 %attend.3.refs_2_.refs_1_ = bf16[4,512,512]{2,1,0:T(8,128)(2,1)S(1)} custom-call(s32[1]{0:T(128)} %bitcast.number_ref.refs_0_, bf16[512,512]{1,0:T(8,128)(2,1)S(1)} %get-tuple-element.22.refs_1_, bf16[512,512]{1,0:T(8,128)(2,1)S(1)} %get-tuple-element.23.refs_2_, bf16[512,512]{1,0:T(8,128)(2,1)S(1)} %get-tuple-element.24.refs_3_, ...), custom_call_target="tpu_custom_call", output_to_operand_aliasing={{}: (6, {})} | custom-call | flops 17179869184 | bytes 2097152 | tf_op jit(solution)/shard_map/attend/pallas_call | solution.py:140
  21.3 0.8 other_core.6.refs_3_
  22.2 0.1 collective-permute-start.1
  22.2 0.9 other_core.7.refs_4_
  23.1 0.5 collective-permute-start.6
  23.6 0.0 collective-permute-done.3.refs_3_
  23.6 0.5 first_hop.4.refs_4_
  24.2 1.2 %collective-permute-start.7 = (f32[2,2,256,256]{3,2,1,0:T(8,128)S(1)}, f32[2,2,256,256]{3,2,1,0:T(8,128)S(1)}, u32[]{:S(2)}, u32[]{:S(2)}) collective-permute-start(f32[2,2,256,256]{3,2,1,0:T(8,128)S(1)} %first_hop.4.refs_4_), channel_id=1, source_target_pairs={{0,16},{1,3},{2,18},{3,1},{16,0},{17,19},{18,2},{19,17},{4,20},{5,... | collective-permute-start | bytes 3145736 | tf_op jit(solution)/shard_map/ppermute | solution.py:391
  25.4 0.0 collective-permute-done.2.refs_3_
  25.4 0.5 first_hop.5.refs_5_
  25.9 1.6 %collective-permute-start.8 = (f32[2,2,256,256]{3,2,1,0:T(8,128)S(1)}, f32[2,2,256,256]{3,2,1,0:T(8,128)S(1)}, u32[]{:S(2)}, u32[]{:S(2)}) collective-permute-start(f32[2,2,256,256]{3,2,1,0:T(8,128)S(1)} %first_hop.5.refs_5_), channel_id=1, source_target_pairs={{0,2},{1,17},{2,0},{3,19},{16,18},{17,1},{18,16},{19,3},{4,6},{5,2... | collective-permute-start | bytes 3145736 | tf_op jit(solution)/shard_map/ppermute | solution.py:391
  27.5 1.0 head_terms.4.refs_4_
  28.5 1.7 %collective-permute-start.5 = (f32[512,512]{1,0:T(8,128)S(1)}, f32[512,512]{1,0:T(8,128)S(1)}, u32[]{:S(2)}, u32[]{:S(2)}) collective-permute-start(f32[512,512]{1,0:T(8,128)S(1)} %head_terms.4.refs_4_), channel_id=1, source_target_pairs={{0,4},{4,0},{8,12},{12,8},{1,5},{5,1},{9,13},{13,9},{2,6},{6,2},{1... | collective-permute-start | bytes 3145736 | tf_op jit(solution)/shard_map/ppermute | solution.py:346
  30.1 0.0 collective-permute-done.1.refs_3_.refs_4_
  30.1 0.5 first_hop.6.refs_5_
  30.7 1.2 %collective-permute-start.11 = (f32[2,2,256,256]{3,2,1,0:T(8,128)S(1)}, f32[2,2,256,256]{3,2,1,0:T(8,128)S(1)}, u32[]{:S(2)}, u32[]{:S(2)}) collective-permute-start(f32[2,2,256,256]{3,2,1,0:T(8,128)S(1)} %first_hop.6.refs_5_), channel_id=1, source_target_pairs={{0,16},{1,3},{2,18},{3,1},{16,0},{17,19},{18,2},{19,17},{4,20},{5,... | collective-permute-start | bytes 3145736 | tf_op jit(solution)/shard_map/ppermute | solution.py:391
  31.9 1.0 head_terms.5.refs_5_
  32.9 1.0 head_terms.6.refs_5_.refs_0_
  33.9 1.0 head_terms.7.refs_4_.refs_0_
  35.0 0.0 collective-permute-done.6.refs_3_.refs_4_
  35.0 14.1 %collective-permute-done.7.refs_5_ = f32[2,2,256,256]{3,2,1,0:T(8,128)S(1)} collective-permute-done((f32[2,2,256,256]{3,2,1,0:T(8,128)S(1)}, f32[2,2,256,256]{3,2,1,0:T(8,128)S(1)}, u32[]{:S(2)}, u32[]{:S(2)}) %collective-permute-start.7) | collective-permute-done | bytes 1048608 | tf_op jit(solution)/shard_map/ppermute | solution.py:391
  49.1 0.5 first_hop.7.refs_2_
  49.7 2.7 %collective-permute-start.10 = (f32[2,2,256,256]{3,2,1,0:T(8,128)S(1)}, f32[2,2,256,256]{3,2,1,0:T(8,128)S(1)}, u32[]{:S(2)}, u32[]{:S(2)}) collective-permute-start(f32[2,2,256,256]{3,2,1,0:T(8,128)S(1)} %first_hop.7.refs_2_), channel_id=1, source_target_pairs={{0,2},{1,17},{2,0},{3,19},{16,18},{17,1},{18,16},{19,3},{4,6},{5,2... | collective-permute-start | bytes 3145736 | tf_op jit(solution)/shard_map/ppermute | solution.py:391
  52.4 1.8 %collective-permute-start.4 = (f32[512,512]{1,0:T(8,128)S(1)}, f32[512,512]{1,0:T(8,128)S(1)}, u32[]{:S(2)}, u32[]{:S(2)}) collective-permute-start(f32[512,512]{1,0:T(8,128)S(1)} %head_terms.5.refs_5_), channel_id=1, source_target_pairs={{0,4},{4,0},{8,12},{12,8},{1,5},{5,1},{9,13},{13,9},{2,6},{6,2},{1... | collective-permute-start | bytes 3145736 | tf_op jit(solution)/shard_map/ppermute | solution.py:346
  54.1 0.5 collective-permute-done.5.refs_1_
  54.7 0.0 collective-permute-done.8.refs_3_.refs_5_
  54.7 0.2 add.10.refs_7_
  54.8 2.7 %collective-permute-start.9 = (f32[512,512]{1,0:T(8,128)S(1)}, f32[512,512]{1,0:T(8,128)S(1)}, u32[]{:S(2)}, u32[]{:S(2)}) collective-permute-start(f32[512,512]{1,0:T(8,128)S(1)} %add.10.refs_7_), channel_id=1, source_target_pairs={{0,8},{4,12},{8,0},{12,4},{1,9},{5,13},{9,1},{13,5},{2,10},{6,14},... | collective-permute-start | bytes 3145736 | tf_op jit(solution)/shard_map/ppermute | solution.py:346
  57.5 14.1 %collective-permute-done.11.refs_6_ = f32[2,2,256,256]{3,2,1,0:T(8,128)S(1)} collective-permute-done((f32[2,2,256,256]{3,2,1,0:T(8,128)S(1)}, f32[2,2,256,256]{3,2,1,0:T(8,128)S(1)}, u32[]{:S(2)}, u32[]{:S(2)}) %collective-permute-start.11) | collective-permute-done | bytes 1048608 | tf_op jit(solution)/shard_map/ppermute | solution.py:391
  71.6 1.2 %second_hop.2 = (f32[2,2,256,256]{3,2,1,0:T(8,128)S(1)}, f32[2,2,256,256]{3,2,1,0:T(8,128)S(1)}) custom-call(s32[1]{0:T(128)} %bitcast.number_ref.refs_0_, bf16[2,512,2048]{2,1,0:T(8,128)(2,1)S(1)} %get-tuple-element.27.refs_1_, bf16[4,512,512]{2,1,0:T(8,128)(2,1)S(1)} %attend.3.refs_2_.refs_1_, f32[4,2,256,256]{3,2,1,0:T(8,128)S(1)} %collective-permute-done.3.refs_3_, ...), custom_call_target="tpu_custom_call" | custom-call | flops 536870912 | bytes 2097152 | tf_op jit(solution)/shard_map/second_hop/pallas_call | solution.py:140
  72.8 2.5 %collective-permute-start.12 = (f32[2,2,256,256]{3,2,1,0:T(8,128)S(1)}, f32[2,2,256,256]{3,2,1,0:T(8,128)S(1)}, u32[]{:S(2)}, u32[]{:S(2)}) collective-permute-start(f32[2,2,256,256]{3,2,1,0:T(8,128)S(1)} %get-tuple-element.33), channel_id=1, source_target_pairs={{0,2},{1,17},{2,0},{3,19},{16,18},{17,1},{18,16},{19,3},{4,6},{5,2... | collective-permute-start | bytes 3145736 | tf_op jit(solution)/shard_map/ppermute | solution.py:391
  75.3 0.0 collective-permute-done.10.refs_6_
  75.3 1.2 %second_hop.3 = (f32[2,2,256,256]{3,2,1,0:T(8,128)S(1)}, f32[2,2,256,256]{3,2,1,0:T(8,128)S(1)}) custom-call(s32[1]{0:T(128)} %bitcast.number_ref.refs_0_, bf16[2,512,2048]{2,1,0:T(8,128)(2,1)S(1)} %get-tuple-element.27.refs_1_, bf16[4,512,512]{2,1,0:T(8,128)(2,1)S(1)} %attend.3.refs_2_.refs_1_, f32[4,2,256,256]{3,2,1,0:T(8,128)S(1)} %collective-permute-done.2.refs_3_, ...), custom_call_target="tpu_custom_call" | custom-call | flops 536870912 | bytes 2097152 | tf_op jit(solution)/shard_map/second_hop/pallas_call | solution.py:140
  76.5 1.4 %collective-permute-start.13 = (f32[2,2,256,256]{3,2,1,0:T(8,128)S(1)}, f32[2,2,256,256]{3,2,1,0:T(8,128)S(1)}, u32[]{:S(2)}, u32[]{:S(2)}) collective-permute-start(f32[2,2,256,256]{3,2,1,0:T(8,128)S(1)} %get-tuple-element.34), channel_id=1, source_target_pairs={{0,16},{1,3},{2,18},{3,1},{16,0},{17,19},{18,2},{19,17},{4,20},{5,... | collective-permute-start | bytes 3145736 | tf_op jit(solution)/shard_map/ppermute | solution.py:391
  77.9 19.9 %collective-permute-done.4.refs_1_ = f32[512,512]{1,0:T(8,128)S(1)} collective-permute-done((f32[512,512]{1,0:T(8,128)S(1)}, f32[512,512]{1,0:T(8,128)S(1)}, u32[]{:S(2)}, u32[]{:S(2)}) %collective-permute-start.4) | collective-permute-done | bytes 1048608 | tf_op jit(solution)/shard_map/ppermute | solution.py:346
  97.9 2.5 %collective-permute-done.9.refs_2_ = f32[512,512]{1,0:T(8,128)S(1)} collective-permute-done((f32[512,512]{1,0:T(8,128)S(1)}, f32[512,512]{1,0:T(8,128)S(1)}, u32[]{:S(2)}, u32[]{:S(2)}) %collective-permute-start.9) | collective-permute-done | bytes 1048608 | tf_op jit(solution)/shard_map/ppermute | solution.py:346
  100.4 1.1 %add.11 = bf16[512,512]{1,0:T(8,128)(2,1)} custom-call(f32[512,512]{1,0:T(8,128)S(1)} %head_terms.7.refs_4_.refs_0_, f32[512,512]{1,0:T(8,128)S(1)} %collective-permute-done.4.refs_1_, f32[512,512]{1,0:T(8,128)S(1)} %collective-permute-done.9.refs_2_, f32[2,2,256,256]{3,2,1,0:T(8,128)S(1)} %get-tuple-element.32.refs_3_.refs_2_), custom_call_target="tpu_custom_call" | custom-call | bytes 2097152 | tf_op jit(solution)/shard_map/add/pallas_call | solution.py:140
  101.4 0.0 collective-permute-done.12.refs_3_
  101.4 0.0 collective-permute-done.13.refs_4_
  101.4 1.6 %collect.1 = (f32[512,256]{1,0:T(8,128)}, f32[256,512]{1,0:T(8,128)}, f32[256,512]{1,0:T(8,128)}, f32[256,512]{1,0:T(8,128)}) custom-call(s32[1]{0:T(128)} %bitcast.number_ref.refs_0_, f32[2,2,256,256]{3,2,1,0:T(8,128)S(1)} %get-tuple-element.31.refs_7_.refs_1_, f32[2,2,256,256]{3,2,1,0:T(8,128)S(1)} %get-tuple-element.32.refs_3_.refs_2_, ...), custom_call_target="tpu_custom_call" | custom-call | bytes 2097152 | tf_op jit(solution)/shard_map/collect/pallas_call | solution.py:140
Async XLA Ops:
  8.3 9.3 %collective-permute-start = (f32[4,128,128]{2,1,0:T(8,128)S(1)}, f32[4,128,128]{2,1,0:T(8,128)S(1)}, u32[]{:S(2)}, u32[]{:S(2)}) collective-permute-start(f32[4,128,128]{2,1,0:T(8,128)S(1)} %get-tuple-element.26), channel_id=1, source_target_pairs={{0,16},{16,0},{1,17},{17,1},{2,18},{18,2},{3,19},{19,3},{4,20},{20... | collective-permute-start | bytes 786440 | tf_op jit(solution)/shard_map/ppermute | solution.py:346
  14.7 8.9 %collective-permute-start.3 = (f32[4,2,256,256]{3,2,1,0:T(8,128)S(1)}, f32[4,2,256,256]{3,2,1,0:T(8,128)S(1)}, u32[]{:S(2)}, u32[]{:S(2)}) collective-permute-start(f32[4,2,256,256]{3,2,1,0:T(8,128)S(1)} %other_core.4.refs_3_), channel_id=1, source_target_pairs={{0,1},{1,0},{2,3},{3,2},{4,5},{5,4},{6,7},{7,6},{8,9},{9,8},{10,11... | collective-permute-start | bytes 6291464 | tf_op jit(solution)/shard_map/ppermute | solution.py:346
  15.7 9.7 %collective-permute-start.2 = (f32[4,2,256,256]{3,2,1,0:T(8,128)S(1)}, f32[4,2,256,256]{3,2,1,0:T(8,128)S(1)}, u32[]{:S(2)}, u32[]{:S(2)}) collective-permute-start(f32[4,2,256,256]{3,2,1,0:T(8,128)S(1)} %other_core.5.refs_7_), channel_id=1, source_target_pairs={{0,1},{1,0},{2,3},{3,2},{4,5},{5,4},{6,7},{7,6},{8,9},{9,8},{10,11... | collective-permute-start | bytes 6291464 | tf_op jit(solution)/shard_map/ppermute | solution.py:346
  22.2 8.0 %collective-permute-start.1 = (f32[4,2,256,256]{3,2,1,0:T(8,128)S(1)}, f32[4,2,256,256]{3,2,1,0:T(8,128)S(1)}, u32[]{:S(2)}, u32[]{:S(2)}) collective-permute-start(f32[4,2,256,256]{3,2,1,0:T(8,128)S(1)} %other_core.6.refs_3_), channel_id=1, source_target_pairs={{0,1},{1,0},{2,3},{3,2},{4,5},{5,4},{6,7},{7,6},{8,9},{9,8},{10,11... | collective-permute-start | bytes 6291464 | tf_op jit(solution)/shard_map/ppermute | solution.py:346
  23.1 11.9 %collective-permute-start.6 = (f32[4,2,256,256]{3,2,1,0:T(8,128)S(1)}, f32[4,2,256,256]{3,2,1,0:T(8,128)S(1)}, u32[]{:S(2)}, u32[]{:S(2)}) collective-permute-start(f32[4,2,256,256]{3,2,1,0:T(8,128)S(1)} %other_core.7.refs_4_), channel_id=1, source_target_pairs={{0,1},{1,0},{2,3},{3,2},{4,5},{5,4},{6,7},{7,6},{8,9},{9,8},{10,11... | collective-permute-start | bytes 6291464 | tf_op jit(solution)/shard_map/ppermute | solution.py:346
  24.2 24.9 %collective-permute-start.7 = (f32[2,2,256,256]{3,2,1,0:T(8,128)S(1)}, f32[2,2,256,256]{3,2,1,0:T(8,128)S(1)}, u32[]{:S(2)}, u32[]{:S(2)}) collective-permute-start(f32[2,2,256,256]{3,2,1,0:T(8,128)S(1)} %first_hop.4.refs_4_), channel_id=1, source_target_pairs={{0,16},{1,3},{2,18},{3,1},{16,0},{17,19},{18,2},{19,17},{4,20},{5,... | collective-permute-start | bytes 3145736 | tf_op jit(solution)/shard_map/ppermute | solution.py:391
  25.9 28.7 %collective-permute-start.8 = (f32[2,2,256,256]{3,2,1,0:T(8,128)S(1)}, f32[2,2,256,256]{3,2,1,0:T(8,128)S(1)}, u32[]{:S(2)}, u32[]{:S(2)}) collective-permute-start(f32[2,2,256,256]{3,2,1,0:T(8,128)S(1)} %first_hop.5.refs_5_), channel_id=1, source_target_pairs={{0,2},{1,17},{2,0},{3,19},{16,18},{17,1},{18,16},{19,3},{4,6},{5,2... | collective-permute-start | bytes 3145736 | tf_op jit(solution)/shard_map/ppermute | solution.py:391
  28.5 26.2 %collective-permute-start.5 = (f32[512,512]{1,0:T(8,128)S(1)}, f32[512,512]{1,0:T(8,128)S(1)}, u32[]{:S(2)}, u32[]{:S(2)}) collective-permute-start(f32[512,512]{1,0:T(8,128)S(1)} %head_terms.4.refs_4_), channel_id=1, source_target_pairs={{0,4},{4,0},{8,12},{12,8},{1,5},{5,1},{9,13},{13,9},{2,6},{6,2},{1... | collective-permute-start | bytes 3145736 | tf_op jit(solution)/shard_map/ppermute | solution.py:346
  30.7 40.9 %collective-permute-start.11 = (f32[2,2,256,256]{3,2,1,0:T(8,128)S(1)}, f32[2,2,256,256]{3,2,1,0:T(8,128)S(1)}, u32[]{:S(2)}, u32[]{:S(2)}) collective-permute-start(f32[2,2,256,256]{3,2,1,0:T(8,128)S(1)} %first_hop.6.refs_5_), channel_id=1, source_target_pairs={{0,16},{1,3},{2,18},{3,1},{16,0},{17,19},{18,2},{19,17},{4,20},{5,... | collective-permute-start | bytes 3145736 | tf_op jit(solution)/shard_map/ppermute | solution.py:391
  49.7 25.6 %collective-permute-start.10 = (f32[2,2,256,256]{3,2,1,0:T(8,128)S(1)}, f32[2,2,256,256]{3,2,1,0:T(8,128)S(1)}, u32[]{:S(2)}, u32[]{:S(2)}) collective-permute-start(f32[2,2,256,256]{3,2,1,0:T(8,128)S(1)} %first_hop.7.refs_2_), channel_id=1, source_target_pairs={{0,2},{1,17},{2,0},{3,19},{16,18},{17,1},{18,16},{19,3},{4,6},{5,2... | collective-permute-start | bytes 3145736 | tf_op jit(solution)/shard_map/ppermute | solution.py:391
  52.4 45.5 %collective-permute-start.4 = (f32[512,512]{1,0:T(8,128)S(1)}, f32[512,512]{1,0:T(8,128)S(1)}, u32[]{:S(2)}, u32[]{:S(2)}) collective-permute-start(f32[512,512]{1,0:T(8,128)S(1)} %head_terms.5.refs_5_), channel_id=1, source_target_pairs={{0,4},{4,0},{8,12},{12,8},{1,5},{5,1},{9,13},{13,9},{2,6},{6,2},{1... | collective-permute-start | bytes 3145736 | tf_op jit(solution)/shard_map/ppermute | solution.py:346
  54.8 45.6 %collective-permute-start.9 = (f32[512,512]{1,0:T(8,128)S(1)}, f32[512,512]{1,0:T(8,128)S(1)}, u32[]{:S(2)}, u32[]{:S(2)}) collective-permute-start(f32[512,512]{1,0:T(8,128)S(1)} %add.10.refs_7_), channel_id=1, source_target_pairs={{0,8},{4,12},{8,0},{12,4},{1,9},{5,13},{9,1},{13,5},{2,10},{6,14},... | collective-permute-start | bytes 3145736 | tf_op jit(solution)/shard_map/ppermute | solution.py:346
  72.8 28.6 %collective-permute-start.12 = (f32[2,2,256,256]{3,2,1,0:T(8,128)S(1)}, f32[2,2,256,256]{3,2,1,0:T(8,128)S(1)}, u32[]{:S(2)}, u32[]{:S(2)}) collective-permute-start(f32[2,2,256,256]{3,2,1,0:T(8,128)S(1)} %get-tuple-element.33), channel_id=1, source_target_pairs={{0,2},{1,17},{2,0},{3,19},{16,18},{17,1},{18,16},{19,3},{4,6},{5,2... | collective-permute-start | bytes 3145736 | tf_op jit(solution)/shard_map/ppermute | solution.py:391
  76.5 24.9 %collective-permute-start.13 = (f32[2,2,256,256]{3,2,1,0:T(8,128)S(1)}, f32[2,2,256,256]{3,2,1,0:T(8,128)S(1)}, u32[]{:S(2)}, u32[]{:S(2)}) collective-permute-start(f32[2,2,256,256]{3,2,1,0:T(8,128)S(1)} %get-tuple-element.34), channel_id=1, source_target_pairs={{0,16},{1,3},{2,18},{3,1},{16,0},{17,19},{18,2},{19,17},{4,20},{5,... | collective-permute-start | bytes 3145736 | tf_op jit(solution)/shard_map/ppermute | solution.py:391
where the time goes:
time: 103 us
  waiting for transfers between devices  52.6 us (51%)
  Pallas kernels  28.8 us (28%)
  starting transfers between devices  20.9 us (20%)
    ppermute x6, waiting for transfers between devices, hop(): return lax.ppermute(array, ('seq', 'dp'), pairs)  28.3 us
    ppermute x8, waiting for transfers between devices, swap(): lax.ppermute(x, axis, [(i, i ^ bit) for i in range(lax.axis_size(axis))])  24.3 us
    pallas_call x19, Pallas kernels, call(): pl.pallas_call(body, out_shape=out_shape, in_specs=[IN_SMEM] * len(number...  21.2 us
    ppermute x6, starting transfers between devices, hop(): return lax.ppermute(array, ('seq', 'dp'), pairs)  10.6 us
    ppermute x8, starting transfers between devices, swap(): lax.ppermute(x, axis, [(i, i ^ bit) for i in range(lax.axis_size(axis))])  10.3 us
    pallas_call x1, Pallas kernels, project(): pl.pallas_call(functools.partial(project_kernel, one_state=one_state, siz...  7.61 us
  transfers between devices with their start and end apart: 14, of which 6 were waited for; matrix products, arithmetic and copies ran while one was open for 0% of the time, Pallas kernels for 19%

commit v1 on v0

v1 whole, which is shorter than its diff:
```python
import functools

import jax
import jax.numpy as jnp
from jax import lax
from jax.experimental import pallas as pl
from jax.experimental.pallas import tpu as pltpu
from jax.sharding import PartitionSpec as P

HEAD_DIM = 128
BF16 = jnp.bfloat16
F32 = jnp.float32
MIB = 1024 * 1024
PLANNED = (2, 4, 4)
NN = ((1,), (0,))
NT = ((1,), (1,))
TN = ((0,), (0,))
ANYWHERE = pl.BlockSpec(memory_space=pl.ANY)
IN_VMEM = pl.BlockSpec(memory_space=pltpu.VMEM)
IN_SMEM = pl.BlockSpec(memory_space=pltpu.SMEM)


def dot(a, b, dims):
    return lax.dot_general(a, b, (dims, ((), ())), preferred_element_type=F32)


def shaped(shape, dtype):
    return jax.ShapeDtypeStruct(shape, dtype)


def params(mib):
    return pltpu.CompilerParams(vmem_limit_bytes=mib * MIB)


def cost(flops, size):
    return pl.CostEstimate(flops=flops, bytes_accessed=size, transcendentals=0)


class Place:
    def __init__(self, number, sizes):
        _, n_head, n_dp = sizes
        self.dp = lax.rem(number, n_dp)
        self.head = lax.rem(lax.div(number, n_dp), n_head)
        self.seq = lax.div(number, n_head * n_dp)
        self.core = lax.rem(self.dp, 2)


def position_scale(start, rows):
    positions = (start + lax.broadcasted_iota(jnp.int32, (rows, 1), 0)).astype(F32)
    return 1.0 / jnp.sqrt(HEAD_DIM * (positions + 1.0))


def project_part(place, part, xo_ref, wq_ref, wk_ref, wv_ref, wo_ref, out_ref, state_ref, arrived):
    rows, width = xo_ref.shape[1:]
    x_ref, o_ref = xo_ref.at[0], xo_ref.at[1]
    lower, upper = pl.ds(0, width // 2), pl.ds(width // 2, width // 2)

    def first(slot, w_ref):
        arrived(0)
        product = dot(x_ref[:, lower], w_ref[lower, :], NN)
        arrived(1)
        out_ref[slot] = (product + dot(x_ref[:, upper], w_ref[upper, :], NN)).astype(BF16)
        arrived(2)

    def state(slot):
        if state_ref is not None:
            for h in range(state_ref.shape[0]):
                at = pl.ds(h * HEAD_DIM, HEAD_DIM)
                state_ref[h] = dot(out_ref[slot, :, at], out_ref[slot + 1, :, at], TN)

    if part == 0:
        first(0, wk_ref)
        out_ref[1] = dot(x_ref[...], wv_ref[...], NN).astype(BF16)
    else:
        first(2, wq_ref)
        scale = position_scale(place.seq * rows, rows)
        out_ref[3] = (dot(o_ref[...], wo_ref[...], NT) * scale).astype(BF16)
    state(2 * part)


def load_kernel(
    number_ref, x_hbm, o_hbm, wq_hbm, wk_hbm, wv_hbm, wo_hbm,
    out_ref, state_ref, xo_ref, wq_ref, wk_ref, wv_ref, wo_ref, sems, *, sizes, which,
):
    place = Place(number_ref[0], sizes)
    mid = xo_ref.shape[2] // 2
    lower, upper = pl.ds(0, mid), pl.ds(mid, mid)
    x_ref, o_ref = xo_ref.at[0], xo_ref.at[1]

    def run(part):
        w_hbm, w_ref = ((wk_hbm, wk_ref), (wq_hbm, wq_ref))[part]
        v, q, k = (wv_hbm, wv_ref), (wq_hbm, wq_ref), (wk_hbm, wk_ref)
        o, w_o = (o_hbm, o_ref), (wo_hbm, wo_ref)
        pairs = [
            (x_hbm.at[:, lower], x_ref.at[:, lower]),
            (w_hbm.at[lower], w_ref.at[lower]),
            (x_hbm.at[:, upper], x_ref.at[:, upper]),
            (w_hbm.at[upper], w_ref.at[upper]),
            *((v, q, o, w_o) if part == 0 else (o, w_o, k, v)),
        ]
        copies = [pltpu.make_async_copy(a, b, sems.at[i]) for i, (a, b) in enumerate(pairs)]
        needed = (2, 4, 5 if part == 0 else 6)
        for c in copies[:4]:
            c.start()

        def arrived(stage):
            for c in copies[needed[stage - 1] if stage else 0 : needed[stage]]:
                c.wait()
            if stage == 0:
                for c in copies[4:]:
                    c.start()

        project_part(
            place, part, xo_ref, wq_ref, wk_ref, wv_ref, wo_ref, out_ref, state_ref, arrived
        )
        for c in copies[needed[2] :]:
            c.wait()

    chosen = which(place)
    pl.when(chosen == 0)(lambda: run(0))
    pl.when(chosen != 0)(lambda: run(1))


def load(place, which, in_rows, grad_rows, w_query, w_key, w_value, w_out):
    number, sizes = place
    rows, width = in_rows.shape
    hd = w_query.shape[1]
    args = [
        pltpu.with_memory_space_constraint(a, pltpu.HBM)
        for a in (in_rows, grad_rows, w_query, w_key, w_value, w_out)
    ]
    out_shape = [
        pltpu.VMEM((4, rows, hd), BF16),
        pltpu.VMEM((hd // HEAD_DIM, HEAD_DIM, HEAD_DIM), F32),
        pltpu.VMEM((2, rows, width), BF16),
        *[pltpu.VMEM((width, hd), BF16)] * 3,
        pltpu.VMEM((hd, width), BF16),
    ]
    return pl.pallas_call(
        functools.partial(load_kernel, sizes=sizes, which=which),
        out_shape=out_shape,
        in_specs=[IN_SMEM] + [ANYWHERE] * 6,
        out_specs=[IN_VMEM] * len(out_shape),
        scratch_shapes=[pltpu.SemaphoreType.DMA((8,))],
        compiler_params=params(16),
        cost_estimate=cost(4 * rows * width * hd, 14 * MIB),
        name="load",
    )(number, *args)


def project_kernel(place, part_ref, xo_ref, wq_ref, wk_ref, wv_ref, wo_ref, out_ref, *states, which):
    state_ref = states[0] if states else None

    def run(part):
        other = 2 - 2 * part
        out_ref[other : other + 2] = part_ref[other : other + 2]
        project_part(
            place, part, xo_ref, wq_ref, wk_ref, wv_ref, wo_ref, out_ref, state_ref, lambda stage: None
        )

    chosen = which(place)
    pl.when(chosen == 0)(lambda: run(0))
    pl.when(chosen != 0)(lambda: run(1))


def project(place, which, part, xo, weights, w_out, with_state):
    rows, width = xo.shape[1:]
    hd = part.shape[2]
    out = [shaped(part.shape, BF16)]
    if with_state:
        out.append(shaped((hd // HEAD_DIM, HEAD_DIM, HEAD_DIM), F32))
    kernel = functools.partial(project_kernel, which=which)
    args = [part, xo, *weights, w_out]
    return call(kernel, "project", out, args, 4 * rows * width * hd, (), place)


def call(kernel, name, out_shape, args, flops, after=(), place=None):
    n, n_after = len(args), len(after)
    numbers = [] if place is None else [place[0]]

    def body(*refs):
        first = [Place(refs[0][0], place[1])] if numbers else []
        refs = refs[len(numbers) :]
        kernel(*first, *refs[:n], *refs[n + n_after :])

    many = isinstance(out_shape, (list, tuple))
    return pl.pallas_call(
        body,
        out_shape=out_shape,
        in_specs=[IN_SMEM] * len(numbers) + [IN_VMEM] * n + [ANYWHERE] * n_after,
        out_specs=[IN_VMEM] * len(out_shape) if many else IN_VMEM,
        compiler_params=params(16),
        cost_estimate=cost(flops, 2 * MIB),
        name=name,
    )(*numbers, *args, *after)


def attend_kernel(place, in_ref, *rest, which, again):
    if again:
        state_ref, part_ref, scores_ref, out_ref = rest
    else:
        out_ref, scores_ref = rest
    rows, hd = in_ref.shape[1:]
    half = rows // 2
    top, low = slice(0, half), slice(half, rows)

    def causal(h, n, a, b):
        if not again:
            r = lax.broadcasted_iota(jnp.int32, (half, half), 0)
            c = lax.broadcasted_iota(jnp.int32, (half, half), 1)
            diagonal = r >= c
            scores_ref[h, n] = jnp.where(diagonal, dot(a[top], b[top], NT), 0.0).astype(BF16)
            scores_ref[h, n + 1] = dot(a[low], b[top], NT).astype(BF16)
            scores_ref[h, n + 2] = jnp.where(diagonal, dot(a[low], b[low], NT), 0.0).astype(BF16)
        return [scores_ref[h, n + i] for i in range(3)]

    def per_head(body):
        def step(h, carry):
            at = pl.ds(pl.multiple_of(h * HEAD_DIM, HEAD_DIM), HEAD_DIM)
            state = state_ref[h].astype(BF16) if again else None

            def put(slot, halves, cross, dims, scale=None):
                added = dot(cross, state, dims) if again else None
                for rows_at, value in zip((top, low), halves):
                    if again:
                        value = value + added[rows_at]
                    if scale is not None:
                        value = value * scale[rows_at]
                    out_ref[slot, rows_at, at] = value.astype(BF16)

            body(h, [in_ref[slot, :, at] for slot in range(4)], put)
            return carry

        lax.fori_loop(0, hd // HEAD_DIM, step, 0, unroll=2)

    def forward():
        scale = position_scale(place.seq * rows, rows)

        def body(h, heads, put):
            k, v, q, g = heads
            for slot, a, b, c, dims in ((0, q, k, v, NN), (1, g, v, k, NT)):
                s00, s10, s11 = causal(h, 3 * slot, a, b)
                halves = (dot(s00, c[top], NN), dot(s10, c[top], NN) + dot(s11, c[low], NN))
                put(slot, halves, a, dims, scale if slot == 0 else None)

        per_head(body)

    def backward():
        def body(h, heads, put):
            k, v, q, g = heads
            for slot, a, b, c, dims in ((2, q, k, g, NN), (3, g, v, q, NT)):
                s00, s10, s11 = causal(h, 3 * slot - 6, a, b)
                halves = (dot(s00, c[top], TN) + dot(s10, c[low], TN), dot(s11, c[low], TN))
                put(slot, halves, b, dims)

        per_head(body)

    chosen = which(place)
    if again:
        for t in (0, 1):
            out_ref[2 - 2 * chosen + t] = part_ref[2 - 2 * chosen + t]
    pl.when(chosen == 0)(forward)
    pl.when(chosen != 0)(backward)


def attend(place, which, projected, more=(), after=()):
    rows, hd = projected.shape[1:]
    out = shaped((4, rows, hd), BF16)
    scores = shaped((hd // HEAD_DIM, 6, rows // 2, rows // 2), BF16)
    kernel = functools.partial(attend_kernel, which=which, again=bool(more))
    outs = out if more else [out, scores]
    return call(kernel, "attend", outs, [projected, *more], 128 * rows * rows * hd, after, place)


def head_terms_kernel(place, d_ref, wq_ref, wk_ref, wv_ref, out_ref, *, shard):
    width = out_ref.shape[1]
    step = min(width, 256)
    start = shard(place) * width
    for i in range(width // step):
        rows = pl.ds(pl.multiple_of(start + i * step, step), step)
        out_ref[:, pl.ds(i * step, step)] = (
            dot(d_ref[1], wq_ref[rows, :], NT)
            + dot(d_ref[3], wk_ref[rows, :], NT)
            + dot(d_ref[2], wv_ref[rows, :], NT)
        )


def head_terms(place, results, weights, shard, shards, after=()):
    width, hd = weights[0].shape
    rows = results.shape[1]
    return call(
        functools.partial(head_terms_kernel, shard=shard),
        "head_terms",
        shaped((rows, width // shards), F32),
        [results, *weights],
        6 * rows * width // shards * hd,
        after,
        place,
    )


def add_kernel(*refs):
    total = refs[0][...]
    for ref in refs[1:-1]:
        total = total + ref[...]
    refs[-1][...] = total.astype(refs[-1].dtype)


def add(arrays, dtype, after=()):
    return call(add_kernel, "add", shaped(arrays[0].shape, dtype), list(arrays), 0, after)


def column_block(place, i):
    return (place.seq ^ (i // 2 % 2)) * 4 + (place.dp ^ (i % 2 * 2 + i // 4))


def fill_tiles(place, xo_ref, d_ref, pair, side, blocks, scale, added, outs):
    half = d_ref.shape[2] // 2
    block = outs[0].shape[1]
    features = pl.ds(pl.multiple_of(side * half, half), half)
    for i, b in enumerate(blocks):
        columns = pl.ds(pl.multiple_of(column_block(place, b) * block, block), block)
        for t, rows in enumerate((1 - pair, 0)):
            tile = dot(xo_ref[rows, :, columns], d_ref[2 * pair + t, :, features], TN) * scale
            for read in added:
                tile = tile + read(i, t)
            outs[i][t] = tile


def other_core_kernel(place, xo_ref, d_ref, out_ref, *, early, slot, scale):
    outs = [out_ref.at[i] for i in range(4)]
    pair, side = place.seq ^ early, 1 - place.core ^ slot
    fill_tiles(place, xo_ref, d_ref, pair, side, (4, 5, 6, 7), scale, (), outs)


def first_hop_kernel(place, xo_ref, d_ref, far_ref, out_ref, *, early, slot, scale):
    pair, side = place.seq ^ early, place.core ^ slot
    blocks = (2 - side, 3)
    outs = [out_ref.at[i] for i in range(2)]
    added = (lambda i, t: far_ref[blocks[i], t],)
    fill_tiles(place, xo_ref, d_ref, pair, side, blocks, scale, added, outs)


def second_hop_kernel(
    place, xo_ref, d_ref, far0_ref, far1_ref, over0_ref, over1_ref, keep_ref, send_ref,
    *, slot, scale,
):
    over = (over0_ref, over1_ref)
    side = place.core ^ slot
    blocks = (0, 1 + side)

    def far(p, i, t):
        return (far0_ref, far1_ref)[p][blocks[i], t]

    for p in (0, 1):
        added = (
            lambda i, t: jnp.where(side == 0, far(1 - p, i, t), far(p, i, t)),
            lambda i, t: over[p][i, t],
        )
        pair = place.seq ^ p ^ 1 - side
        outs = (keep_ref.at[p], send_ref.at[p])
        fill_tiles(place, xo_ref, d_ref, pair, side, blocks, scale, added, outs)


def settle_kernel(place, kept_ref, moved_ref, out_ref, *, slot):
    side = place.core ^ slot
    for p in (0, 1):
        for t in (0, 1):
            out_ref[p, t] = kept_ref[p ^ 1 - side, t] + moved_ref[1 - p, t]


def finish_kernel(place, *refs):
    line, (sums_ref, kept_ref, moved_ref) = refs[:3], refs[3:6]
    input_ref, out_ref, query_ref, key_ref, value_ref = refs[6:]
    half = query_ref.shape[1] // 2
    input_ref[...] = (line[0][...] + line[1][...] + line[2][...]).astype(BF16)
    for side in (0, 1):
        at = pl.ds(side * half, half)

        def total(pair, t):
            p = place.seq ^ pair
            late = kept_ref[p ^ 1 - side, t] + moved_ref[1 - p, t]
            return jnp.where(place.core == side, sums_ref[p, t], late)

        out_ref[at, :] = total(0, 0).T
        query_ref[:, at] = total(0, 1)
        value_ref[:, at] = total(1, 0)
        key_ref[:, at] = total(1, 1)


def finish(place, line, sums, kept, moved):
    block, half = kept.shape[2:]
    tall, wide = shaped((block, 2 * half), F32), shaped((2 * half, block), F32)
    outs = [shaped(line[0].shape, BF16), wide, tall, tall, tall]
    return call(finish_kernel, "finish", outs, [*line, sums, kept, moved], 0, (), place)


def states_before(x, axis, reverse):
    peers, here = (lax.axis_size(axis), lax.axis_index(axis))
    everything = lax.all_gather(x, axis)
    at = jnp.arange(peers)
    reached = at > here if reverse else at < here
    return jnp.sum(jnp.where(reached[:, None, None, None], everything, 0.0), axis=0)


def swap(x, axis, bit):
    return lax.ppermute(x, axis, [(i, i ^ bit) for i in range(lax.axis_size(axis))])


def local(layer_input, w_query, w_key, w_value, w_out, out_grad):
    num_rows = layer_input.shape[1]
    n_seq, n_head, n_dp = (lax.axis_size(a) for a in ("seq", "head", "dp"))
    scale = float(n_seq * n_dp * num_rows) ** -0.5

    sizes = (n_seq, n_head, n_dp)
    number = (lax.axis_index("seq") * n_head + lax.axis_index("head")) * n_dp + lax.axis_index("dp")
    number = number.astype(jnp.int32).reshape(1)
    place = (number, sizes)
    arrays = (layer_input[0], out_grad[0], w_query, w_key, w_value, w_out)
    planned = sizes == PLANNED
    part = (lambda at: at.seq) if planned else (lambda at: 0)
    projected, state, xo, *weights, wo = load(place, part, *arrays)
    if planned:
        state = swap(state, "seq", 1)
    projected, *more = project(
        place, lambda at: 1 - part(at), projected, xo, weights, wo, not planned
    )

    if not planned:
        prefix = states_before(state, "seq", False)
        suffix = states_before(more[0], "seq", True)
        d, scores = attend(place, lambda at: 0, projected)
        d = attend(place, lambda at: 0, projected, (prefix, d, scores))
        d = attend(place, lambda at: 1, projected, (suffix, d, scores))
        terms = head_terms(place, d, weights, lambda at: 0, 1)

        def reduced(rows, d):
            return lax.psum_scatter(
                dot(rows, d, TN) * scale, ("seq", "dp"), scatter_dimension=0, tiled=True
            )

        return (
            lax.psum_scatter(terms, "head", scatter_dimension=1, tiled=True).astype(BF16)[None],
            reduced(xo[0], d[1]),
            reduced(xo[0], d[3]),
            reduced(xo[0], d[2]),
            reduced(xo[1], d[0]).T,
        )

    def term(flip, after):
        return head_terms(place, d, weights, lambda at: at.head ^ flip, n_head, after)

    def hop(array, slot, second):
        pairs = []
        for i in range(8):
            side = i % 2 ^ slot
            pairs.append((i, i ^ (4 if side == second else 2)))
        return lax.ppermute(array, ("seq", "dp"), pairs)

    block, half = xo.shape[2] // 8, projected.shape[2] // 2
    tile = (2, block, half)
    flops = 4 * num_rows * block * half

    def to_core(d, early, slot, after):
        kernel = functools.partial(other_core_kernel, early=early, slot=slot, scale=scale)
        out = shaped((4, *tile), F32)
        array = call(kernel, "other_core", out, [xo, d], 4 * flops, after, place)
        return array, swap(array, "dp", 1)

    def first_hop(early, slot, after):
        kernel = functools.partial(first_hop_kernel, early=early, slot=slot, scale=scale)
        out = shaped((2, *tile), F32)
        args = [xo, d, far[early][slot]]
        array = call(kernel, "first_hop", out, args, 2 * flops, after, place)
        return array, hop(array, slot, 0)

    def second_hop(slot, over, after):
        kernel = functools.partial(second_hop_kernel, slot=slot, scale=scale)
        outs = [shaped((2, *tile), F32)] * 2
        args = [xo, d, far[0][slot], far[1][slot], *over]
        keep, leave = call(kernel, "second_hop", outs, args, 4 * flops, after, place)
        return keep, hop(leave, slot, 1)

    early, scores = attend(place, lambda at: at.seq, projected)
    far = ([None, None], [None, None])
    at, far[0][0] = to_core(early, 0, 0, [])
    at, far[0][1] = to_core(early, 0, 1, [at])
    d = attend(place, lambda at: 1 - at.seq, projected, (state, early, scores), [at])
    at, far[1][0] = to_core(d, 1, 0, [])
    at, far[1][1] = to_core(d, 1, 1, [at])
    at, over1 = first_hop(0, 0, [at])
    t3 = term(3, [at])
    t3_in = swap(t3, "head", 1)
    at, over2 = first_hop(0, 1, [t3])
    at, over3 = first_hop(1, 0, [at])
    at, over4 = first_hop(1, 1, [at])
    t2 = term(2, [at])
    t0 = term(0, [t2])
    t1 = term(1, [t0, over1])
    t1_in = swap(t1, "head", 1)
    t2 = add([t2, t3_in], F32, [t1])
    t2_in = swap(t2, "head", 2)
    keep0, moved0 = second_hop(0, (over1, over3), [t2, over2])
    keep1, moved1 = second_hop(1, (over2, over4), [keep0])
    settle = functools.partial(settle_kernel, slot=0)
    sums = call(settle, "settle", shaped(keep0.shape, F32), [keep0, moved0], 0, [keep1], place)
    outs = finish(place, (t0, t1_in, t2_in), sums, keep1, moved1)
    input_grad, grad_out, grad_query, grad_key, grad_value = outs
    return (input_grad[None], grad_query, grad_key, grad_value, grad_out)


def solution(mesh):
    return jax.shard_map(
        local,
        mesh=mesh,
        in_specs=(
            P("dp", "seq", None),
            P(None, "head"),
            P(None, "head"),
            P(None, "head"),
            P("head", None),
            P("dp", "seq", None),
        ),
        out_specs=(
            P("dp", "seq", "head"),
            P(("seq", "dp"), "head"),
            P(("seq", "dp"), "head"),
            P(("seq", "dp"), "head"),
            P("head", ("seq", "dp")),
        ),
        check_vma=False,
    )
```

time: 103 us -> 99.1 us (0.962)
  Pallas kernels: 28.8 us -> 25.9 us
    ppermute x8, waiting for transfers between devices: 24.3 us -> 6.38 us  [swap(): lax.ppermute(x, axis, [(i, i ^ bit) for i in range(lax.axis_size(axis))])]
    ppermute x6, waiting for transfers between devices: 28.3 us -> 45.5 us  [hop(): return lax.ppermute(array, ('seq', 'dp'), pairs)]
    pallas_call x1, Pallas kernels: 7.61 us -> 5.2 us  [load(): pl.pallas_call(functools.partial(load_kernel, sizes=sizes, which=which),...]
    ppermute x6, starting transfers between devices: 10.6 us -> 8.39 us  [hop(): return lax.ppermute(array, ('seq', 'dp'), pairs)]
    ppermute x8, starting transfers between devices: 10.3 us -> 11.9 us  [swap(): lax.ppermute(x, axis, [(i, i ^ bit) for i in range(lax.axis_size(axis))])]
    pallas_call x19 -> x20, Pallas kernels: 21.2 us -> 20.8 us  [call(): pl.pallas_call(body, out_shape=out_shape, in_specs=[IN_SMEM] * len(number...]
  transfers between devices with their start and end apart: 14 -> 14, of which waited for: 6 -> 5; matrix products, arithmetic and copies ran while one was open for 0% -> 0% of each run, Pallas kernels for 19% -> 19%
where the time goes in v1:
time: 99.1 us; the launch traced here: 98.9 us
  waiting for transfers between devices  51.9 us (52%)
  Pallas kernels  25.9 us (26%)
  starting transfers between devices  20.3 us (20%)
    ppermute x6, waiting for transfers between devices, hop(): return lax.ppermute(array, ('seq', 'dp'), pairs)  45.5 us
    pallas_call x20, Pallas kernels, call(): pl.pallas_call(body, out_shape=out_shape, in_specs=[IN_SMEM] * len(number...  20.8 us
    ppermute x8, starting transfers between devices, swap(): lax.ppermute(x, axis, [(i, i ^ bit) for i in range(lax.axis_size(axis))])  11.9 us
    ppermute x6, starting transfers between devices, hop(): return lax.ppermute(array, ('seq', 'dp'), pairs)  8.39 us
    ppermute x8, waiting for transfers between devices, swap(): lax.ppermute(x, axis, [(i, i ^ bit) for i in range(lax.axis_size(axis))])  6.38 us
    pallas_call x1, Pallas kernels, load(): pl.pallas_call(functools.partial(load_kernel, sizes=sizes, which=which),...  5.2 us
  transfers between devices with their start and end apart: 14, of which 5 were waited for; matrix products, arithmetic and copies ran while one was open for 0% of the time, Pallas kernels for 19%

profile of v1, /device:TPU:0, one launch (start us, length us, event | category | flops | bytes accessed | tf_op | source)
XLA Modules:
  0.0 98.9 jit_solution(14594235216423530385)
XLA Ops:
  0.6 5.2 %load.1 = (bf16[4,512,512]{2,1,0:T(8,128)(2,1)S(1)}, f32[4,128,128]{2,1,0:T(8,128)S(1)}, bf16[2,512,2048]{2,1,0:T(8,128)(2,1)S(1)}, bf16[2048,512]{1,0:T(8,128)(...) custom-call(s32[1]{0:T(128)} %bitcast.number_ref.refs_0_, ...), custom_call_target="tpu_custom_call" | custom-call | flops 2147483648 | bytes 14680064 | tf_op jit(solution)/shard_map/load/pallas_call | solution.py:139
  5.8 3.4 %collective-permute-start = (f32[4,128,128]{2,1,0:T(8,128)S(1)}, f32[4,128,128]{2,1,0:T(8,128)S(1)}, u32[]{:S(2)}, u32[]{:S(2)}) collective-permute-start(f32[4,128,128]{2,1,0:T(8,128)S(1)} %get-tuple-element.29), channel_id=1, source_target_pairs={{0,16},{16,0},{1,17},{17,1},{2,18},{18,2},{3,19},{19,3},{4,20},{20... | collective-permute-start | bytes 786440 | tf_op jit(solution)/shard_map/ppermute | solution.py:407
  9.2 2.4 %project.1.refs_1_ = bf16[4,512,512]{2,1,0:T(8,128)(2,1)S(1)} custom-call(s32[1]{0:T(128)} %bitcast.number_ref.refs_0_, bf16[4,512,512]{2,1,0:T(8,128)(2,1)S(1)} %get-tuple-element.23.refs_1_, bf16[2,512,2048]{2,1,0:T(8,128)(2,1)S(1)} %get-tuple-element.24.refs_2_.refs_1_, bf16[2048,512]{1,0:T(8,128)(2,1)S(1)} %get-tuple-element.25.refs_3_.refs_2_, ...), custom_call_target="tpu_custom_call" | custom-call | flops 2147483648 | bytes 2097152 | tf_op jit(solution)/shard_map/project/pallas_call | solution.py:187
  11.6 2.6 %attend.2 = (bf16[4,512,512]{2,1,0:T(8,128)(2,1)S(1)}, bf16[4,6,256,256]{3,2,1,0:T(8,128)(2,1)S(1)}) custom-call(s32[1]{0:T(128)} %bitcast.number_ref.refs_0_, bf16[4,512,512]{2,1,0:T(8,128)(2,1)S(1)} %project.1.refs_1_), custom_call_target="tpu_custom_call" | custom-call | flops 17179869184 | bytes 2097152 | tf_op jit(solution)/shard_map/attend/pallas_call | solution.py:187
  14.2 0.8 other_core.4.refs_3_
  15.1 0.1 collective-permute-start.4
  15.2 0.9 other_core.5.refs_5_
  16.0 0.5 collective-permute-start.3
  16.6 0.0 collective-permute-done.refs_2_
  16.6 1.8 %attend.3.refs_2_.refs_1_ = bf16[4,512,512]{2,1,0:T(8,128)(2,1)S(1)} custom-call(s32[1]{0:T(128)} %bitcast.number_ref.refs_0_, bf16[4,512,512]{2,1,0:T(8,128)(2,1)S(1)} %project.1.refs_1_, f32[4,128,128]{2,1,0:T(8,128)S(1)} %collective-permute-done.refs_2_, bf16[4,512,512]{2,1,0:T(8,128)(2,1)S(1)} %get-tuple-element.30.refs_2_.refs_3_, ...), custom_call_target="tpu_custom_call" | custom-call | flops 17179869184 | bytes 2097152 | tf_op jit(solution)/shard_map/attend/pallas_call | solution.py:187
  18.4 0.8 other_core.6.refs_3_
  19.2 0.1 collective-permute-start.2
  19.3 0.9 other_core.7.refs_4_
  20.2 0.5 collective-permute-start.1
  20.7 0.0 collective-permute-done.4.refs_3_
  20.7 0.5 first_hop.4.refs_5_
  21.2 0.9 collective-permute-start.5
  22.1 1.0 %head_terms.4.refs_4_ = f32[512,512]{1,0:T(8,128)S(1)} custom-call(s32[1]{0:T(128)} %bitcast.number_ref.refs_0_, bf16[4,512,512]{2,1,0:T(8,128)(2,1)S(1)} %attend.3.refs_2_.refs_1_, bf16[2048,512]{1,0:T(8,128)(2,1)S(1)} %get-tuple-element.25.refs_3_.refs_2_, bf16[2048,512]{1,0:T(8,128)(2,1)S(1)} %get-tuple-element.26.refs_4_.refs_3_, ...), custom_call_target="tpu_custom_call" | custom-call | flops 805306368 | bytes 2097152 | tf_op jit(solution)/shard_map/head_terms/pallas_call | solution.py:187
  23.2 1.8 %collective-permute-start.7 = (f32[512,512]{1,0:T(8,128)S(1)}, f32[512,512]{1,0:T(8,128)S(1)}, u32[]{:S(2)}, u32[]{:S(2)}) collective-permute-start(f32[512,512]{1,0:T(8,128)S(1)} %head_terms.4.refs_4_), channel_id=1, source_target_pairs={{0,4},{4,0},{8,12},{12,8},{1,5},{5,1},{9,13},{13,9},{2,6},{6,2},{1... | collective-permute-start | bytes 3145736 | tf_op jit(solution)/shard_map/ppermute | solution.py:407
  24.9 0.0 collective-permute-done.3.refs_3_
  24.9 0.5 first_hop.5.refs_4_
  25.5 1.6 %collective-permute-start.10 = (f32[2,2,256,256]{3,2,1,0:T(8,128)S(1)}, f32[2,2,256,256]{3,2,1,0:T(8,128)S(1)}, u32[]{:S(2)}, u32[]{:S(2)}) collective-permute-start(f32[2,2,256,256]{3,2,1,0:T(8,128)S(1)} %first_hop.5.refs_4_), channel_id=1, source_target_pairs={{0,2},{1,17},{2,0},{3,19},{16,18},{17,1},{18,16},{19,3},{4,6},{5,2... | collective-permute-start | bytes 3145736 | tf_op jit(solution)/shard_map/ppermute | solution.py:458
  27.0 0.0 collective-permute-done.2.refs_3_.refs_4_
  27.0 0.5 first_hop.6.refs_4_
  27.6 1.2 %collective-permute-start.9 = (f32[2,2,256,256]{3,2,1,0:T(8,128)S(1)}, f32[2,2,256,256]{3,2,1,0:T(8,128)S(1)}, u32[]{:S(2)}, u32[]{:S(2)}) collective-permute-start(f32[2,2,256,256]{3,2,1,0:T(8,128)S(1)} %first_hop.6.refs_4_), channel_id=1, source_target_pairs={{0,16},{1,3},{2,18},{3,1},{16,0},{17,19},{18,2},{19,17},{4,20},{5,... | collective-permute-start | bytes 3145736 | tf_op jit(solution)/shard_map/ppermute | solution.py:458
  28.7 0.5 first_hop.7.refs_5_
  29.3 1.2 %collective-permute-start.12 = (f32[2,2,256,256]{3,2,1,0:T(8,128)S(1)}, f32[2,2,256,256]{3,2,1,0:T(8,128)S(1)}, u32[]{:S(2)}, u32[]{:S(2)}) collective-permute-start(f32[2,2,256,256]{3,2,1,0:T(8,128)S(1)} %first_hop.7.refs_5_), channel_id=1, source_target_pairs={{0,2},{1,17},{2,0},{3,19},{16,18},{17,1},{18,16},{19,3},{4,6},{5,2... | collective-permute-start | bytes 3145736 | tf_op jit(solution)/shard_map/ppermute | solution.py:458
  30.5 1.0 %head_terms.5.refs_5_.refs_0_ = f32[512,512]{1,0:T(8,128)S(1)} custom-call(s32[1]{0:T(128)} %bitcast.number_ref.refs_0_, bf16[4,512,512]{2,1,0:T(8,128)(2,1)S(1)} %attend.3.refs_2_.refs_1_, bf16[2048,512]{1,0:T(8,128)(2,1)S(1)} %get-tuple-element.25.refs_3_.refs_2_, bf16[2048,512]{1,0:T(8,128)(2,1)S(1)} %get-tuple-element.26.refs_4_.refs_3_, ...), custom_call_target="tpu_custom_call" | custom-call | flops 805306368 | bytes 2097152 | tf_op jit(solution)/shard_map/head_terms/pallas_call | solution.py:187
  31.5 1.0 %head_terms.6.refs_5_.refs_1_ = f32[512,512]{1,0:T(8,128)S(1)} custom-call(s32[1]{0:T(128)} %bitcast.number_ref.refs_0_, bf16[4,512,512]{2,1,0:T(8,128)(2,1)S(1)} %attend.3.refs_2_.refs_1_, bf16[2048,512]{1,0:T(8,128)(2,1)S(1)} %get-tuple-element.25.refs_3_.refs_2_, bf16[2048,512]{1,0:T(8,128)(2,1)S(1)} %get-tuple-element.26.refs_4_.refs_3_, ...), custom_call_target="tpu_custom_call" | custom-call | flops 805306368 | bytes 2097152 | tf_op jit(solution)/shard_map/head_terms/pallas_call | solution.py:187
  32.5 11.4 %collective-permute-done.5.refs_6_.refs_5_ = f32[2,2,256,256]{3,2,1,0:T(8,128)S(1)} collective-permute-done((f32[2,2,256,256]{3,2,1,0:T(8,128)S(1)}, f32[2,2,256,256]{3,2,1,0:T(8,128)S(1)}, u32[]{:S(2)}, u32[]{:S(2)}) %collective-permute-start.5) | collective-permute-done | bytes 1048608 | tf_op jit(solution)/shard_map/ppermute | solution.py:458
  43.9 1.0 %head_terms.7.refs_2_ = f32[512,512]{1,0:T(8,128)S(1)} custom-call(s32[1]{0:T(128)} %bitcast.number_ref.refs_0_, bf16[4,512,512]{2,1,0:T(8,128)(2,1)S(1)} %attend.3.refs_2_.refs_1_, bf16[2048,512]{1,0:T(8,128)(2,1)S(1)} %get-tuple-element.25.refs_3_.refs_2_, bf16[2048,512]{1,0:T(8,128)(2,1)S(1)} %get-tuple-element.26.refs_4_.refs_3_, ...), custom_call_target="tpu_custom_call" | custom-call | flops 805306368 | bytes 2097152 | tf_op jit(solution)/shard_map/head_terms/pallas_call | solution.py:187
  44.9 2.8 %collective-permute-start.6 = (f32[512,512]{1,0:T(8,128)S(1)}, f32[512,512]{1,0:T(8,128)S(1)}, u32[]{:S(2)}, u32[]{:S(2)}) collective-permute-start(f32[512,512]{1,0:T(8,128)S(1)} %head_terms.7.refs_2_), channel_id=1, source_target_pairs={{0,4},{4,0},{8,12},{12,8},{1,5},{5,1},{9,13},{13,9},{2,6},{6,2},{1... | collective-permute-start | bytes 3145736 | tf_op jit(solution)/shard_map/ppermute | solution.py:407
  47.7 1.5 %collective-permute-done.7.refs_1_ = f32[512,512]{1,0:T(8,128)S(1)} collective-permute-done((f32[512,512]{1,0:T(8,128)S(1)}, f32[512,512]{1,0:T(8,128)S(1)}, u32[]{:S(2)}, u32[]{:S(2)}) %collective-permute-start.7) | collective-permute-done | bytes 1048608 | tf_op jit(solution)/shard_map/ppermute | solution.py:407
  49.2 0.2 add.9.refs_7_
  49.3 2.8 %collective-permute-start.8 = (f32[512,512]{1,0:T(8,128)S(1)}, f32[512,512]{1,0:T(8,128)S(1)}, u32[]{:S(2)}, u32[]{:S(2)}) collective-permute-start(f32[512,512]{1,0:T(8,128)S(1)} %add.9.refs_7_), channel_id=1, source_target_pairs={{0,8},{4,12},{8,0},{12,4},{1,9},{5,13},{9,1},{13,5},{2,10},{6,14},... | collective-permute-start | bytes 3145736 | tf_op jit(solution)/shard_map/ppermute | solution.py:407
  52.1 0.0 collective-permute-done.10.refs_8_.refs_5_
  52.1 14.3 %collective-permute-done.9.refs_6_ = f32[2,2,256,256]{3,2,1,0:T(8,128)S(1)} collective-permute-done((f32[2,2,256,256]{3,2,1,0:T(8,128)S(1)}, f32[2,2,256,256]{3,2,1,0:T(8,128)S(1)}, u32[]{:S(2)}, u32[]{:S(2)}) %collective-permute-start.9) | collective-permute-done | bytes 1048608 | tf_op jit(solution)/shard_map/ppermute | solution.py:458
  66.4 1.2 %second_hop.2 = (f32[2,2,256,256]{3,2,1,0:T(8,128)S(1)}, f32[2,2,256,256]{3,2,1,0:T(8,128)S(1)}) custom-call(s32[1]{0:T(128)} %bitcast.number_ref.refs_0_, bf16[2,512,2048]{2,1,0:T(8,128)(2,1)S(1)} %get-tuple-element.24.refs_2_.refs_1_, bf16[4,512,512]{2,1,0:T(8,128)(2,1)S(1)} %attend.3.refs_2_.refs_1_, ...), custom_call_target="tpu_custom_call" | custom-call | flops 536870912 | bytes 2097152 | tf_op jit(solution)/shard_map/second_hop/pallas_call | solution.py:187
  67.6 2.6 %collective-permute-start.11 = (f32[2,2,256,256]{3,2,1,0:T(8,128)S(1)}, f32[2,2,256,256]{3,2,1,0:T(8,128)S(1)}, u32[]{:S(2)}, u32[]{:S(2)}) collective-permute-start(f32[2,2,256,256]{3,2,1,0:T(8,128)S(1)} %get-tuple-element.33), channel_id=1, source_target_pairs={{0,2},{1,17},{2,0},{3,19},{16,18},{17,1},{18,16},{19,3},{4,6},{5,2... | collective-permute-start | bytes 3145736 | tf_op jit(solution)/shard_map/ppermute | solution.py:458
  70.2 0.0 collective-permute-done.12.refs_6_
  70.2 1.2 %second_hop.3 = (f32[2,2,256,256]{3,2,1,0:T(8,128)S(1)}, f32[2,2,256,256]{3,2,1,0:T(8,128)S(1)}) custom-call(s32[1]{0:T(128)} %bitcast.number_ref.refs_0_, bf16[2,512,2048]{2,1,0:T(8,128)(2,1)S(1)} %get-tuple-element.24.refs_2_.refs_1_, bf16[4,512,512]{2,1,0:T(8,128)(2,1)S(1)} %attend.3.refs_2_.refs_1_, ...), custom_call_target="tpu_custom_call" | custom-call | flops 536870912 | bytes 2097152 | tf_op jit(solution)/shard_map/second_hop/pallas_call | solution.py:187
  71.4 1.0 collective-permute-start.13
  72.4 19.8 %collective-permute-done.11.refs_2_ = f32[2,2,256,256]{3,2,1,0:T(8,128)S(1)} collective-permute-done((f32[2,2,256,256]{3,2,1,0:T(8,128)S(1)}, f32[2,2,256,256]{3,2,1,0:T(8,128)S(1)}, u32[]{:S(2)}, u32[]{:S(2)}) %collective-permute-start.11) | collective-permute-done | bytes 1048608 | tf_op jit(solution)/shard_map/ppermute | solution.py:458
  92.2 0.1 settle.1.refs_4_
  92.3 4.9 %collective-permute-done.8.refs_3_ = f32[512,512]{1,0:T(8,128)S(1)} collective-permute-done((f32[512,512]{1,0:T(8,128)S(1)}, f32[512,512]{1,0:T(8,128)S(1)}, u32[]{:S(2)}, u32[]{:S(2)}) %collective-permute-start.8) | collective-permute-done | bytes 1048608 | tf_op jit(solution)/shard_map/ppermute | solution.py:407
  97.2 0.0 collective-permute-done.6.refs_2_
  97.2 0.0 collective-permute-done.13.refs_6_
  97.2 1.7 %finish.1 = (bf16[512,512]{1,0:T(8,128)(2,1)}, f32[512,256]{1,0:T(8,128)}, f32[256,512]{1,0:T(8,128)}, f32[256,512]{1,0:T(8,128)}, f32[256,512]{1,0:T(8,128)}) custom-call(s32[1]{0:T(128)} %bitcast.number_ref.refs_0_, f32[512,512]{1,0:T(8,128)S(1)} %head_terms.6.refs_5_.refs_1_, f32[512,512]{1,0:T(8,128)S(1)} %collective-permute-done.6.refs_2_, ...), custom_call_target="tpu_custom_call" | custom-call | bytes 2097152 | tf_op jit(solution)/shard_map/finish/pallas_call | solution.py:187
  (1 shorter events, 0.0 us)
Async XLA Ops:
  5.8 10.7 %collective-permute-start = (f32[4,128,128]{2,1,0:T(8,128)S(1)}, f32[4,128,128]{2,1,0:T(8,128)S(1)}, u32[]{:S(2)}, u32[]{:S(2)}) collective-permute-start(f32[4,128,128]{2,1,0:T(8,128)S(1)} %get-tuple-element.29), channel_id=1, source_target_pairs={{0,16},{16,0},{1,17},{17,1},{2,18},{18,2},{3,19},{19,3},{4,20},{20... | collective-permute-start | bytes 786440 | tf_op jit(solution)/shard_map/ppermute | solution.py:407
  15.1 5.6 %collective-permute-start.4 = (f32[4,2,256,256]{3,2,1,0:T(8,128)S(1)}, f32[4,2,256,256]{3,2,1,0:T(8,128)S(1)}, u32[]{:S(2)}, u32[]{:S(2)}) collective-permute-start(f32[4,2,256,256]{3,2,1,0:T(8,128)S(1)} %other_core.4.refs_3_), channel_id=1, source_target_pairs={{0,1},{1,0},{2,3},{3,2},{4,5},{5,4},{6,7},{7,6},{8,9},{9,8},{10,11... | collective-permute-start | bytes 6291464 | tf_op jit(solution)/shard_map/ppermute | solution.py:407
  16.0 8.9 %collective-permute-start.3 = (f32[4,2,256,256]{3,2,1,0:T(8,128)S(1)}, f32[4,2,256,256]{3,2,1,0:T(8,128)S(1)}, u32[]{:S(2)}, u32[]{:S(2)}) collective-permute-start(f32[4,2,256,256]{3,2,1,0:T(8,128)S(1)} %other_core.5.refs_5_), channel_id=1, source_target_pairs={{0,1},{1,0},{2,3},{3,2},{4,5},{5,4},{6,7},{7,6},{8,9},{9,8},{10,11... | collective-permute-start | bytes 6291464 | tf_op jit(solution)/shard_map/ppermute | solution.py:407
  19.2 7.8 %collective-permute-start.2 = (f32[4,2,256,256]{3,2,1,0:T(8,128)S(1)}, f32[4,2,256,256]{3,2,1,0:T(8,128)S(1)}, u32[]{:S(2)}, u32[]{:S(2)}) collective-permute-start(f32[4,2,256,256]{3,2,1,0:T(8,128)S(1)} %other_core.6.refs_3_), channel_id=1, source_target_pairs={{0,1},{1,0},{2,3},{3,2},{4,5},{5,4},{6,7},{7,6},{8,9},{9,8},{10,11... | collective-permute-start | bytes 6291464 | tf_op jit(solution)/shard_map/ppermute | solution.py:407
  20.2 8.5 %collective-permute-start.1 = (f32[4,2,256,256]{3,2,1,0:T(8,128)S(1)}, f32[4,2,256,256]{3,2,1,0:T(8,128)S(1)}, u32[]{:S(2)}, u32[]{:S(2)}) collective-permute-start(f32[4,2,256,256]{3,2,1,0:T(8,128)S(1)} %other_core.7.refs_4_), channel_id=1, source_target_pairs={{0,1},{1,0},{2,3},{3,2},{4,5},{5,4},{6,7},{7,6},{8,9},{9,8},{10,11... | collective-permute-start | bytes 6291464 | tf_op jit(solution)/shard_map/ppermute | solution.py:407
  21.2 22.7 %collective-permute-start.5 = (f32[2,2,256,256]{3,2,1,0:T(8,128)S(1)}, f32[2,2,256,256]{3,2,1,0:T(8,128)S(1)}, u32[]{:S(2)}, u32[]{:S(2)}) collective-permute-start(f32[2,2,256,256]{3,2,1,0:T(8,128)S(1)} %first_hop.4.refs_5_), channel_id=1, source_target_pairs={{0,16},{1,3},{2,18},{3,1},{16,0},{17,19},{18,2},{19,17},{4,20},{5,... | collective-permute-start | bytes 3145736 | tf_op jit(solution)/shard_map/ppermute | solution.py:458
  23.2 26.0 %collective-permute-start.7 = (f32[512,512]{1,0:T(8,128)S(1)}, f32[512,512]{1,0:T(8,128)S(1)}, u32[]{:S(2)}, u32[]{:S(2)}) collective-permute-start(f32[512,512]{1,0:T(8,128)S(1)} %head_terms.4.refs_4_), channel_id=1, source_target_pairs={{0,4},{4,0},{8,12},{12,8},{1,5},{5,1},{9,13},{13,9},{2,6},{6,2},{1... | collective-permute-start | bytes 3145736 | tf_op jit(solution)/shard_map/ppermute | solution.py:407
  25.5 26.7 %collective-permute-start.10 = (f32[2,2,256,256]{3,2,1,0:T(8,128)S(1)}, f32[2,2,256,256]{3,2,1,0:T(8,128)S(1)}, u32[]{:S(2)}, u32[]{:S(2)}) collective-permute-start(f32[2,2,256,256]{3,2,1,0:T(8,128)S(1)} %first_hop.5.refs_4_), channel_id=1, source_target_pairs={{0,2},{1,17},{2,0},{3,19},{16,18},{17,1},{18,16},{19,3},{4,6},{5,2... | collective-permute-start | bytes 3145736 | tf_op jit(solution)/shard_map/ppermute | solution.py:458
  27.6 38.8 %collective-permute-start.9 = (f32[2,2,256,256]{3,2,1,0:T(8,128)S(1)}, f32[2,2,256,256]{3,2,1,0:T(8,128)S(1)}, u32[]{:S(2)}, u32[]{:S(2)}) collective-permute-start(f32[2,2,256,256]{3,2,1,0:T(8,128)S(1)} %first_hop.6.refs_4_), channel_id=1, source_target_pairs={{0,16},{1,3},{2,18},{3,1},{16,0},{17,19},{18,2},{19,17},{4,20},{5,... | collective-permute-start | bytes 3145736 | tf_op jit(solution)/shard_map/ppermute | solution.py:458
  29.3 41.0 %collective-permute-start.12 = (f32[2,2,256,256]{3,2,1,0:T(8,128)S(1)}, f32[2,2,256,256]{3,2,1,0:T(8,128)S(1)}, u32[]{:S(2)}, u32[]{:S(2)}) collective-permute-start(f32[2,2,256,256]{3,2,1,0:T(8,128)S(1)} %first_hop.7.refs_5_), channel_id=1, source_target_pairs={{0,2},{1,17},{2,0},{3,19},{16,18},{17,1},{18,16},{19,3},{4,6},{5,2... | collective-permute-start | bytes 3145736 | tf_op jit(solution)/shard_map/ppermute | solution.py:458
  44.9 52.3 %collective-permute-start.6 = (f32[512,512]{1,0:T(8,128)S(1)}, f32[512,512]{1,0:T(8,128)S(1)}, u32[]{:S(2)}, u32[]{:S(2)}) collective-permute-start(f32[512,512]{1,0:T(8,128)S(1)} %head_terms.7.refs_2_), channel_id=1, source_target_pairs={{0,4},{4,0},{8,12},{12,8},{1,5},{5,1},{9,13},{13,9},{2,6},{6,2},{1... | collective-permute-start | bytes 3145736 | tf_op jit(solution)/shard_map/ppermute | solution.py:407
  49.3 47.9 %collective-permute-start.8 = (f32[512,512]{1,0:T(8,128)S(1)}, f32[512,512]{1,0:T(8,128)S(1)}, u32[]{:S(2)}, u32[]{:S(2)}) collective-permute-start(f32[512,512]{1,0:T(8,128)S(1)} %add.9.refs_7_), channel_id=1, source_target_pairs={{0,8},{4,12},{8,0},{12,4},{1,9},{5,13},{9,1},{13,5},{2,10},{6,14},... | collective-permute-start | bytes 3145736 | tf_op jit(solution)/shard_map/ppermute | solution.py:407
  67.6 24.6 %collective-permute-start.11 = (f32[2,2,256,256]{3,2,1,0:T(8,128)S(1)}, f32[2,2,256,256]{3,2,1,0:T(8,128)S(1)}, u32[]{:S(2)}, u32[]{:S(2)}) collective-permute-start(f32[2,2,256,256]{3,2,1,0:T(8,128)S(1)} %get-tuple-element.33), channel_id=1, source_target_pairs={{0,2},{1,17},{2,0},{3,19},{16,18},{17,1},{18,16},{19,3},{4,6},{5,2... | collective-permute-start | bytes 3145736 | tf_op jit(solution)/shard_map/ppermute | solution.py:458
  71.4 25.8 %collective-permute-start.13 = (f32[2,2,256,256]{3,2,1,0:T(8,128)S(1)}, f32[2,2,256,256]{3,2,1,0:T(8,128)S(1)}, u32[]{:S(2)}, u32[]{:S(2)}) collective-permute-start(f32[2,2,256,256]{3,2,1,0:T(8,128)S(1)} %get-tuple-element.35), channel_id=1, source_target_pairs={{0,16},{1,3},{2,18},{3,1},{16,0},{17,19},{18,2},{19,17},{4,20},{5,... | collective-permute-start | bytes 3145736 | tf_op jit(solution)/shard_map/ppermute | solution.py:458

commit v2 on v1

--- a/solution.py
+++ b/solution.py
@@ -231,7 +231,7 @@
             body(h, [in_ref[slot, :, at] for slot in range(4)], put)
             return carry
 
-        lax.fori_loop(0, hd // HEAD_DIM, step, 0, unroll=2)
+        lax.fori_loop(0, hd // HEAD_DIM, step, 0, unroll=True)
 
     def forward():
         scale = position_scale(place.seq * rows, rows)
@@ -333,6 +333,21 @@
     fill_tiles(place, xo_ref, d_ref, pair, side, (4, 5, 6, 7), scale, (), outs)
 
 
+def other_core_both_kernel(place, xo_ref, d_ref, *out_refs, early, scale):
+    pair = place.seq ^ early
+    half = d_ref.shape[2] // 2
+    block = out_refs[0].shape[2]
+    sides = (1 - place.core, place.core)
+    for t, rows in enumerate((1 - pair, 0)):
+        features = [pl.ds(pl.multiple_of(side * half, half), half) for side in sides]
+        d = jnp.concatenate([d_ref[2 * pair + t, :, at] for at in features], axis=1)
+        for i in range(4):
+            columns = pl.ds(pl.multiple_of(column_block(place, 4 + i) * block, block), block)
+            tile = dot(xo_ref[rows, :, columns], d, TN) * scale
+            out_refs[0][i, t] = tile[:, :half]
+            out_refs[1][i, t] = tile[:, half:]
+
+
 def first_hop_kernel(place, xo_ref, d_ref, far_ref, out_ref, *, early, slot, scale):
     pair, side = place.seq ^ early, place.core ^ slot
     blocks = (2 - side, 3)
@@ -362,37 +377,67 @@
         fill_tiles(place, xo_ref, d_ref, pair, side, blocks, scale, added, outs)
 
 
-def settle_kernel(place, kept_ref, moved_ref, out_ref, *, slot):
+def put_side(place, slot, kept_ref, moved_ref, part_ref, out_refs, sems):
     side = place.core ^ slot
-    for p in (0, 1):
-        for t in (0, 1):
-            out_ref[p, t] = kept_ref[p ^ 1 - side, t] + moved_ref[1 - p, t]
-
-
-def finish_kernel(place, *refs):
-    line, (sums_ref, kept_ref, moved_ref) = refs[:3], refs[3:6]
-    input_ref, out_ref, query_ref, key_ref, value_ref = refs[6:]
-    half = query_ref.shape[1] // 2
+    half = part_ref.shape[1]
+    at = pl.ds(pl.multiple_of(side * half, half), half)
+    copies = []
+    for i, (pair, t) in enumerate(((0, 1), (1, 1), (1, 0), (0, 0))):
+        p = place.seq ^ pair
+        total = kept_ref[p ^ 1 - side, t] + moved_ref[1 - p, t]
+        part_ref[i] = total if i < 3 else total.T
+        out = out_refs[i].at[:, at] if i < 3 else out_refs[i].at[at]
+        copies.append(pltpu.make_async_copy(part_ref.at[i], out, sems.at[i]))
+        copies[-1].start()
+    return copies
+
+
+def settle_kernel(number_ref, kept_ref, moved_ref, after_ref, *rest, sizes):
+    out_refs, (part_ref, sems) = rest[:4], rest[4:]
+    place = Place(number_ref[0], sizes)
+    for c in put_side(place, 0, kept_ref, moved_ref, part_ref, out_refs, sems):
+        c.wait()
+
+
+def finish_kernel(number_ref, *refs, sizes):
+    line, (kept_ref, moved_ref) = refs[:3], refs[3:5]
+    input_out, out_refs, (part_ref, input_ref, sems) = refs[9], refs[10:14], refs[14:]
+    place = Place(number_ref[0], sizes)
     input_ref[...] = (line[0][...] + line[1][...] + line[2][...]).astype(BF16)
-    for side in (0, 1):
-        at = pl.ds(side * half, half)
-
-        def total(pair, t):
-            p = place.seq ^ pair
-            late = kept_ref[p ^ 1 - side, t] + moved_ref[1 - p, t]
-            return jnp.where(place.core == side, sums_ref[p, t], late)
-
-        out_ref[at, :] = total(0, 0).T
-        query_ref[:, at] = total(0, 1)
-        value_ref[:, at] = total(1, 0)
-        key_ref[:, at] = total(1, 1)
-
-
-def finish(place, line, sums, kept, moved):
-    block, half = kept.shape[2:]
-    tall, wide = shaped((block, 2 * half), F32), shaped((2 * half, block), F32)
-    outs = [shaped(line[0].shape, BF16), wide, tall, tall, tall]
-    return call(finish_kernel, "finish", outs, [*line, sums, kept, moved], 0, (), place)
+    last = pltpu.make_async_copy(input_ref, input_out, sems.at[4])
+    last.start()
+    for c in put_side(place, 1, kept_ref, moved_ref, part_ref, out_refs, sems):
+        c.wait()
+    last.wait()
+
+
+def finish(place, line, kept, moved):
+    number, sizes = place
+    block, half = kept[0].shape[2:]
+    tall, wide = pltpu.HBM((block, 2 * half), F32), pltpu.HBM((2 * half, block), F32)
+    grads = [tall, tall, tall, wide]
+    parts = pltpu.VMEM((4, block, half), F32)
+    sides = pl.pallas_call(
+        functools.partial(settle_kernel, sizes=sizes),
+        out_shape=grads,
+        in_specs=[IN_SMEM, IN_VMEM, IN_VMEM, ANYWHERE],
+        out_specs=[ANYWHERE] * 4,
+        scratch_shapes=[parts, pltpu.SemaphoreType.DMA((4,))],
+        compiler_params=params(16),
+        cost_estimate=cost(0, 2 * MIB),
+        name="settle",
+    )(number, kept[0], moved[0], kept[1])
+    return pl.pallas_call(
+        functools.partial(finish_kernel, sizes=sizes),
+        out_shape=[pltpu.HBM(line[0].shape, BF16), *grads],
+        in_specs=[IN_SMEM] + [IN_VMEM] * 5 + [ANYWHERE] * 4,
+        out_specs=[ANYWHERE] * 5,
+        input_output_aliases={6 + i: 1 + i for i in range(4)},
+        scratch_shapes=[parts, pltpu.VMEM(line[0].shape, BF16), pltpu.SemaphoreType.DMA((5,))],
+        compiler_params=params(16),
+        cost_estimate=cost(0, 2 * MIB),
+        name="finish",
+    )(number, *line, kept[1], moved[1], *sides)
 
 
 def states_before(x, axis, reverse):
@@ -467,6 +512,12 @@
         array = call(kernel, "other_core", out, [xo, d], 4 * flops, after, place)
         return array, swap(array, "dp", 1)
 
+    def both_to_core(d, early, after):
+        kernel = functools.partial(other_core_both_kernel, early=early, scale=scale)
+        outs = [shaped((4, *tile), F32)] * 2
+        arrays = call(kernel, "other_core_both", outs, [xo, d], 8 * flops, after, place)
+        return arrays[0], [swap(array, "dp", 1) for array in arrays]
+
     def first_hop(early, slot, after):
         kernel = functools.partial(first_hop_kernel, early=early, slot=slot, scale=scale)
         out = shaped((2, *tile), F32)
@@ -486,8 +537,7 @@
     at, far[0][0] = to_core(early, 0, 0, [])
     at, far[0][1] = to_core(early, 0, 1, [at])
     d = attend(place, lambda at: 1 - at.seq, projected, (state, early, scores), [at])
-    at, far[1][0] = to_core(d, 1, 0, [])
-    at, far[1][1] = to_core(d, 1, 1, [at])
+    at, far[1][:] = both_to_core(d, 1, [])
     at, over1 = first_hop(0, 0, [at])
     t3 = term(3, [at])
     t3_in = swap(t3, "head", 1)
@@ -502,10 +552,8 @@
     t2_in = swap(t2, "head", 2)
     keep0, moved0 = second_hop(0, (over1, over3), [t2, over2])
     keep1, moved1 = second_hop(1, (over2, over4), [keep0])
-    settle = functools.partial(settle_kernel, slot=0)
-    sums = call(settle, "settle", shaped(keep0.shape, F32), [keep0, moved0], 0, [keep1], place)
-    outs = finish(place, (t0, t1_in, t2_in), sums, keep1, moved1)
-    input_grad, grad_out, grad_query, grad_key, grad_value = outs
+    outs = finish(place, (t0, t1_in, t2_in), (keep0, keep1), (moved0, moved1))
+    input_grad, grad_query, grad_key, grad_value, grad_out = outs
     return (input_grad[None], grad_query, grad_key, grad_value, grad_out)
 
 

time: 99.1 us -> 97.9 us (0.988)
  waiting for transfers between devices: 51.9 us -> 50.4 us
    pallas_call x20 -> x17, Pallas kernels: 20.8 us -> 18 us  [call(): pl.pallas_call(body, out_shape=out_shape, in_specs=[IN_SMEM] * len(number...]
    pallas_call x0 -> x2, Pallas kernels: none -> 2.49 us  [the longest x1 1.45 us: finish(): pl.pallas_call(functools.partial(finish_kernel, sizes=sizes), out_shape=[...]
  transfers between devices with their start and end apart: 14 -> 14, of which waited for: 5 -> 6; matrix products, arithmetic and copies ran while one was open for 0% -> 0% of each run, Pallas kernels for 19% -> 19%
where the time goes in v2:
time: 97.9 us; the launch traced here: 97.8 us
  waiting for transfers between devices  50.4 us (51%)
  Pallas kernels  25.7 us (26%)
  starting transfers between devices  20.7 us (21%)
    ppermute x6, waiting for transfers between devices, hop(): return lax.ppermute(array, ('seq', 'dp'), pairs)  44.7 us
    pallas_call x17, Pallas kernels, call(): pl.pallas_call(body, out_shape=out_shape, in_specs=[IN_SMEM] * len(number...  18 us
    ppermute x8, starting transfers between devices, swap(): lax.ppermute(x, axis, [(i, i ^ bit) for i in range(lax.axis_size(axis))])  11.9 us
    ppermute x6, starting transfers between devices, hop(): return lax.ppermute(array, ('seq', 'dp'), pairs)  8.82 us
    ppermute x8, waiting for transfers between devices, swap(): lax.ppermute(x, axis, [(i, i ^ bit) for i in range(lax.axis_size(axis))])  5.75 us
    pallas_call x1, Pallas kernels, load(): pl.pallas_call(functools.partial(load_kernel, sizes=sizes, which=which),...  5.2 us
  transfers between devices with their start and end apart: 14, of which 6 were waited for; matrix products, arithmetic and copies ran while one was open for 0% of the time, Pallas kernels for 19%

profile of v2, /device:TPU:0, one launch (start us, length us, event | category | flops | bytes accessed | tf_op | source)
XLA Modules:
  0.0 97.8 jit_solution(9860230902861634469)
XLA Ops:
  0.6 5.2 %load.1 = (bf16[4,512,512]{2,1,0:T(8,128)(2,1)S(1)}, f32[4,128,128]{2,1,0:T(8,128)S(1)}, bf16[2,512,2048]{2,1,0:T(8,128)(2,1)S(1)}, bf16[2048,512]{1,0:T(8,128)(...) custom-call(s32[1]{0:T(128)} %bitcast.number_ref.refs_0_, ...), custom_call_target="tpu_custom_call" | custom-call | flops 2147483648 | bytes 14680064 | tf_op jit(solution)/shard_map/load/pallas_call | solution.py:139
  5.8 3.4 %collective-permute-start = (f32[4,128,128]{2,1,0:T(8,128)S(1)}, f32[4,128,128]{2,1,0:T(8,128)S(1)}, u32[]{:S(2)}, u32[]{:S(2)}) collective-permute-start(f32[4,128,128]{2,1,0:T(8,128)S(1)} %get-tuple-element.35), channel_id=1, source_target_pairs={{0,16},{16,0},{1,17},{17,1},{2,18},{18,2},{3,19},{19,3},{4,20},{20... | collective-permute-start | bytes 786440 | tf_op jit(solution)/shard_map/ppermute | solution.py:452
  9.2 2.4 %project.1.refs_1_ = bf16[4,512,512]{2,1,0:T(8,128)(2,1)S(1)} custom-call(s32[1]{0:T(128)} %bitcast.number_ref.refs_0_, bf16[4,512,512]{2,1,0:T(8,128)(2,1)S(1)} %get-tuple-element.29.refs_1_, bf16[2,512,2048]{2,1,0:T(8,128)(2,1)S(1)} %get-tuple-element.30.refs_2_.refs_1_, bf16[2048,512]{1,0:T(8,128)(2,1)S(1)} %get-tuple-element.31.refs_3_.refs_2_, ...), custom_call_target="tpu_custom_call" | custom-call | flops 2147483648 | bytes 2097152 | tf_op jit(solution)/shard_map/project/pallas_call | solution.py:187
  11.6 2.5 %attend.2 = (bf16[4,512,512]{2,1,0:T(8,128)(2,1)S(1)}, bf16[4,6,256,256]{3,2,1,0:T(8,128)(2,1)S(1)}) custom-call(s32[1]{0:T(128)} %bitcast.number_ref.refs_0_, bf16[4,512,512]{2,1,0:T(8,128)(2,1)S(1)} %project.1.refs_1_), custom_call_target="tpu_custom_call" | custom-call | flops 17179869184 | bytes 2097152 | tf_op jit(solution)/shard_map/attend/pallas_call | solution.py:187
  14.1 0.8 other_core.2.refs_3_
  14.9 0.1 collective-permute-start.4
  15.0 0.9 other_core.3.refs_5_
  15.9 0.5 collective-permute-start.3
  16.4 0.0 collective-permute-done.refs_2_
  16.4 1.4 %attend.3.refs_2_.refs_1_ = bf16[4,512,512]{2,1,0:T(8,128)(2,1)S(1)} custom-call(s32[1]{0:T(128)} %bitcast.number_ref.refs_0_, bf16[4,512,512]{2,1,0:T(8,128)(2,1)S(1)} %project.1.refs_1_, f32[4,128,128]{2,1,0:T(8,128)S(1)} %collective-permute-done.refs_2_, bf16[4,512,512]{2,1,0:T(8,128)(2,1)S(1)} %get-tuple-element.36.refs_2_.refs_3_, ...), custom_call_target="tpu_custom_call" | custom-call | flops 17179869184 | bytes 2097152 | tf_op jit(solution)/shard_map/attend/pallas_call | solution.py:187
  17.8 1.3 %other_core_both.1 = (f32[4,2,256,256]{3,2,1,0:T(8,128)S(1)}, f32[4,2,256,256]{3,2,1,0:T(8,128)S(1)}) custom-call(s32[1]{0:T(128)} %bitcast.number_ref.refs_0_, bf16[2,512,2048]{2,1,0:T(8,128)(2,1)S(1)} %get-tuple-element.30.refs_2_.refs_1_, bf16[4,512,512]{2,1,0:T(8,128)(2,1)S(1)} %attend.3.refs_2_.refs_1_), custom_call_target="tpu_custom_call" | custom-call | flops 1073741824 | bytes 2097152 | tf_op jit(solution)/shard_map/other_core_both/pallas_call | solution.py:187
  19.1 0.1 collective-permute-start.2
  19.2 0.5 collective-permute-start.1
  19.7 0.0 collective-permute-done.4.refs_3_
  19.7 0.5 first_hop.4.refs_5_
  20.3 0.9 collective-permute-start.5
  21.2 1.0 %head_terms.4.refs_4_ = f32[512,512]{1,0:T(8,128)S(1)} custom-call(s32[1]{0:T(128)} %bitcast.number_ref.refs_0_, bf16[4,512,512]{2,1,0:T(8,128)(2,1)S(1)} %attend.3.refs_2_.refs_1_, bf16[2048,512]{1,0:T(8,128)(2,1)S(1)} %get-tuple-element.31.refs_3_.refs_2_, bf16[2048,512]{1,0:T(8,128)(2,1)S(1)} %get-tuple-element.32.refs_4_.refs_3_, ...), custom_call_target="tpu_custom_call" | custom-call | flops 805306368 | bytes 2097152 | tf_op jit(solution)/shard_map/head_terms/pallas_call | solution.py:187
  22.2 1.8 %collective-permute-start.7 = (f32[512,512]{1,0:T(8,128)S(1)}, f32[512,512]{1,0:T(8,128)S(1)}, u32[]{:S(2)}, u32[]{:S(2)}) collective-permute-start(f32[512,512]{1,0:T(8,128)S(1)} %head_terms.4.refs_4_), channel_id=1, source_target_pairs={{0,4},{4,0},{8,12},{12,8},{1,5},{5,1},{9,13},{13,9},{2,6},{6,2},{1... | collective-permute-start | bytes 3145736 | tf_op jit(solution)/shard_map/ppermute | solution.py:452
  24.0 0.0 collective-permute-done.3.refs_3_
  24.0 0.5 first_hop.5.refs_4_
  24.5 1.6 %collective-permute-start.9 = (f32[2,2,256,256]{3,2,1,0:T(8,128)S(1)}, f32[2,2,256,256]{3,2,1,0:T(8,128)S(1)}, u32[]{:S(2)}, u32[]{:S(2)}) collective-permute-start(f32[2,2,256,256]{3,2,1,0:T(8,128)S(1)} %first_hop.5.refs_4_), channel_id=1, source_target_pairs={{0,2},{1,17},{2,0},{3,19},{16,18},{17,1},{18,16},{19,3},{4,6},{5,2... | collective-permute-start | bytes 3145736 | tf_op jit(solution)/shard_map/ppermute | solution.py:503
  26.1 0.0 collective-permute-done.2.refs_3_.refs_4_
  26.1 0.5 first_hop.6.refs_4_
  26.7 1.1 %collective-permute-start.11 = (f32[2,2,256,256]{3,2,1,0:T(8,128)S(1)}, f32[2,2,256,256]{3,2,1,0:T(8,128)S(1)}, u32[]{:S(2)}, u32[]{:S(2)}) collective-permute-start(f32[2,2,256,256]{3,2,1,0:T(8,128)S(1)} %first_hop.6.refs_4_), channel_id=1, source_target_pairs={{0,16},{1,3},{2,18},{3,1},{16,0},{17,19},{18,2},{19,17},{4,20},{5,... | collective-permute-start | bytes 3145736 | tf_op jit(solution)/shard_map/ppermute | solution.py:503
  27.8 0.4 collective-permute-done.1.refs_3_.refs_4_
  28.2 0.5 first_hop.7.refs_5_
  28.7 1.6 %collective-permute-start.10 = (f32[2,2,256,256]{3,2,1,0:T(8,128)S(1)}, f32[2,2,256,256]{3,2,1,0:T(8,128)S(1)}, u32[]{:S(2)}, u32[]{:S(2)}) collective-permute-start(f32[2,2,256,256]{3,2,1,0:T(8,128)S(1)} %first_hop.7.refs_5_), channel_id=1, source_target_pairs={{0,2},{1,17},{2,0},{3,19},{16,18},{17,1},{18,16},{19,3},{4,6},{5,2... | collective-permute-start | bytes 3145736 | tf_op jit(solution)/shard_map/ppermute | solution.py:503
  30.3 1.0 %head_terms.5.refs_5_.refs_0_ = f32[512,512]{1,0:T(8,128)S(1)} custom-call(s32[1]{0:T(128)} %bitcast.number_ref.refs_0_, bf16[4,512,512]{2,1,0:T(8,128)(2,1)S(1)} %attend.3.refs_2_.refs_1_, bf16[2048,512]{1,0:T(8,128)(2,1)S(1)} %get-tuple-element.31.refs_3_.refs_2_, bf16[2048,512]{1,0:T(8,128)(2,1)S(1)} %get-tuple-element.32.refs_4_.refs_3_, ...), custom_call_target="tpu_custom_call" | custom-call | flops 805306368 | bytes 2097152 | tf_op jit(solution)/shard_map/head_terms/pallas_call | solution.py:187
  31.3 1.0 %head_terms.6.refs_5_.refs_0_ = f32[512,512]{1,0:T(8,128)S(1)} custom-call(s32[1]{0:T(128)} %bitcast.number_ref.refs_0_, bf16[4,512,512]{2,1,0:T(8,128)(2,1)S(1)} %attend.3.refs_2_.refs_1_, bf16[2048,512]{1,0:T(8,128)(2,1)S(1)} %get-tuple-element.31.refs_3_.refs_2_, bf16[2048,512]{1,0:T(8,128)(2,1)S(1)} %get-tuple-element.32.refs_4_.refs_3_, ...), custom_call_target="tpu_custom_call" | custom-call | flops 805306368 | bytes 2097152 | tf_op jit(solution)/shard_map/head_terms/pallas_call | solution.py:187
  32.3 10.6 %collective-permute-done.5.refs_6_.refs_5_ = f32[2,2,256,256]{3,2,1,0:T(8,128)S(1)} collective-permute-done((f32[2,2,256,256]{3,2,1,0:T(8,128)S(1)}, f32[2,2,256,256]{3,2,1,0:T(8,128)S(1)}, u32[]{:S(2)}, u32[]{:S(2)}) %collective-permute-start.5) | collective-permute-done | bytes 1048608 | tf_op jit(solution)/shard_map/ppermute | solution.py:503
  43.0 1.0 %head_terms.7.refs_2_ = f32[512,512]{1,0:T(8,128)S(1)} custom-call(s32[1]{0:T(128)} %bitcast.number_ref.refs_0_, bf16[4,512,512]{2,1,0:T(8,128)(2,1)S(1)} %attend.3.refs_2_.refs_1_, bf16[2048,512]{1,0:T(8,128)(2,1)S(1)} %get-tuple-element.31.refs_3_.refs_2_, bf16[2048,512]{1,0:T(8,128)(2,1)S(1)} %get-tuple-element.32.refs_4_.refs_3_, ...), custom_call_target="tpu_custom_call" | custom-call | flops 805306368 | bytes 2097152 | tf_op jit(solution)/shard_map/head_terms/pallas_call | solution.py:187
  44.0 2.8 %collective-permute-start.6 = (f32[512,512]{1,0:T(8,128)S(1)}, f32[512,512]{1,0:T(8,128)S(1)}, u32[]{:S(2)}, u32[]{:S(2)}) collective-permute-start(f32[512,512]{1,0:T(8,128)S(1)} %head_terms.7.refs_2_), channel_id=1, source_target_pairs={{0,4},{4,0},{8,12},{12,8},{1,5},{5,1},{9,13},{13,9},{2,6},{6,2},{1... | collective-permute-start | bytes 3145736 | tf_op jit(solution)/shard_map/ppermute | solution.py:452
  46.7 1.5 %collective-permute-done.7.refs_1_ = f32[512,512]{1,0:T(8,128)S(1)} collective-permute-done((f32[512,512]{1,0:T(8,128)S(1)}, f32[512,512]{1,0:T(8,128)S(1)}, u32[]{:S(2)}, u32[]{:S(2)}) %collective-permute-start.7) | collective-permute-done | bytes 1048608 | tf_op jit(solution)/shard_map/ppermute | solution.py:452
  48.2 0.2 add.9.refs_7_
  48.4 2.8 %collective-permute-start.8 = (f32[512,512]{1,0:T(8,128)S(1)}, f32[512,512]{1,0:T(8,128)S(1)}, u32[]{:S(2)}, u32[]{:S(2)}) collective-permute-start(f32[512,512]{1,0:T(8,128)S(1)} %add.9.refs_7_), channel_id=1, source_target_pairs={{0,8},{4,12},{8,0},{12,4},{1,9},{5,13},{9,1},{13,5},{2,10},{6,14},... | collective-permute-start | bytes 3145736 | tf_op jit(solution)/shard_map/ppermute | solution.py:452
  51.2 0.0 collective-permute-done.9.refs_8_.refs_5_
  51.2 14.3 %collective-permute-done.11.refs_6_ = f32[2,2,256,256]{3,2,1,0:T(8,128)S(1)} collective-permute-done((f32[2,2,256,256]{3,2,1,0:T(8,128)S(1)}, f32[2,2,256,256]{3,2,1,0:T(8,128)S(1)}, u32[]{:S(2)}, u32[]{:S(2)}) %collective-permute-start.11) | collective-permute-done | bytes 1048608 | tf_op jit(solution)/shard_map/ppermute | solution.py:503
  65.5 1.2 %second_hop.2 = (f32[2,2,256,256]{3,2,1,0:T(8,128)S(1)}, f32[2,2,256,256]{3,2,1,0:T(8,128)S(1)}) custom-call(s32[1]{0:T(128)} %bitcast.number_ref.refs_0_, bf16[2,512,2048]{2,1,0:T(8,128)(2,1)S(1)} %get-tuple-element.30.refs_2_.refs_1_, bf16[4,512,512]{2,1,0:T(8,128)(2,1)S(1)} %attend.3.refs_2_.refs_1_, ...), custom_call_target="tpu_custom_call" | custom-call | flops 536870912 | bytes 2097152 | tf_op jit(solution)/shard_map/second_hop/pallas_call | solution.py:187
  66.7 2.6 %collective-permute-start.13 = (f32[2,2,256,256]{3,2,1,0:T(8,128)S(1)}, f32[2,2,256,256]{3,2,1,0:T(8,128)S(1)}, u32[]{:S(2)}, u32[]{:S(2)}) collective-permute-start(f32[2,2,256,256]{3,2,1,0:T(8,128)S(1)} %get-tuple-element.43), channel_id=1, source_target_pairs={{0,2},{1,17},{2,0},{3,19},{16,18},{17,1},{18,16},{19,3},{4,6},{5,2... | collective-permute-start | bytes 3145736 | tf_op jit(solution)/shard_map/ppermute | solution.py:503
  69.3 0.0 collective-permute-done.10.refs_6_
  69.3 1.2 %second_hop.3 = (f32[2,2,256,256]{3,2,1,0:T(8,128)S(1)}, f32[2,2,256,256]{3,2,1,0:T(8,128)S(1)}) custom-call(s32[1]{0:T(128)} %bitcast.number_ref.refs_0_, bf16[2,512,2048]{2,1,0:T(8,128)(2,1)S(1)} %get-tuple-element.30.refs_2_.refs_1_, bf16[4,512,512]{2,1,0:T(8,128)(2,1)S(1)} %attend.3.refs_2_.refs_1_, ...), custom_call_target="tpu_custom_call" | custom-call | flops 536870912 | bytes 2097152 | tf_op jit(solution)/shard_map/second_hop/pallas_call | solution.py:187
  70.5 1.0 %collective-permute-start.12 = (f32[2,2,256,256]{3,2,1,0:T(8,128)S(1)}, f32[2,2,256,256]{3,2,1,0:T(8,128)S(1)}, u32[]{:S(2)}, u32[]{:S(2)}) collective-permute-start(f32[2,2,256,256]{3,2,1,0:T(8,128)S(1)} %get-tuple-element.42), channel_id=1, source_target_pairs={{0,16},{1,3},{2,18},{3,1},{16,0},{17,19},{18,2},{19,17},{4,20},{5,... | collective-permute-start | bytes 3145736 | tf_op jit(solution)/shard_map/ppermute | solution.py:503
  71.5 19.8 %collective-permute-done.13.moved_ref = f32[2,2,256,256]{3,2,1,0:T(8,128)S(1)} collective-permute-done((f32[2,2,256,256]{3,2,1,0:T(8,128)S(1)}, f32[2,2,256,256]{3,2,1,0:T(8,128)S(1)}, u32[]{:S(2)}, u32[]{:S(2)}) %collective-permute-start.13) | collective-permute-done | bytes 1048608 | tf_op jit(solution)/shard_map/ppermute | solution.py:503
  91.3 1.0 %settle.1 = (f32[256,512]{1,0:T(8,128)}, f32[256,512]{1,0:T(8,128)}, f32[256,512]{1,0:T(8,128)}, f32[512,256]{1,0:T(8,128)}) custom-call(s32[1]{0:T(128)} %bitcast.number_ref.refs_0_, f32[2,2,256,256]{3,2,1,0:T(8,128)S(1)} %get-tuple-element.40.refs_7_.kept_ref, f32[2,2,256,256]{3,2,1,0:T(8,128)S(1)} %collective-permute-done.13.moved_ref, ...), custom_call_target="tpu_custom_call" | custom-call | bytes 2097152 | tf_op jit(solution)/shard_map/settle/pallas_call | solution.py:420
  92.3 3.8 %collective-permute-done.8.refs_2_ = f32[512,512]{1,0:T(8,128)S(1)} collective-permute-done((f32[512,512]{1,0:T(8,128)S(1)}, f32[512,512]{1,0:T(8,128)S(1)}, u32[]{:S(2)}, u32[]{:S(2)}) %collective-permute-start.8) | collective-permute-done | bytes 1048608 | tf_op jit(solution)/shard_map/ppermute | solution.py:452
  96.1 0.0 collective-permute-done.6.refs_1_
  96.2 0.0 collective-permute-done.12.refs_4_
  96.2 1.5 %finish.1 = (bf16[512,512]{1,0:T(8,128)(2,1)}, f32[256,512]{1,0:T(8,128)}, f32[256,512]{1,0:T(8,128)}, f32[256,512]{1,0:T(8,128)}, f32[512,256]{1,0:T(8,128)}) custom-call(s32[1]{0:T(128)} %bitcast.number_ref.refs_0_, f32[512,512]{1,0:T(8,128)S(1)} %head_terms.6.refs_5_.refs_0_, ...), custom_call_target="tpu_custom_call", output_to_operand_aliasing={{1}: (6, {}), {2}: (7, {}), {3}: (8, {}), {4}: (9, {})} | custom-call | bytes 2097152 | tf_op jit(solution)/shard_map/finish/pallas_call | solution.py:430
Async XLA Ops:
  5.8 10.6 %collective-permute-start = (f32[4,128,128]{2,1,0:T(8,128)S(1)}, f32[4,128,128]{2,1,0:T(8,128)S(1)}, u32[]{:S(2)}, u32[]{:S(2)}) collective-permute-start(f32[4,128,128]{2,1,0:T(8,128)S(1)} %get-tuple-element.35), channel_id=1, source_target_pairs={{0,16},{16,0},{1,17},{17,1},{2,18},{18,2},{3,19},{19,3},{4,20},{20... | collective-permute-start | bytes 786440 | tf_op jit(solution)/shard_map/ppermute | solution.py:452
  14.9 4.8 %collective-permute-start.4 = (f32[4,2,256,256]{3,2,1,0:T(8,128)S(1)}, f32[4,2,256,256]{3,2,1,0:T(8,128)S(1)}, u32[]{:S(2)}, u32[]{:S(2)}) collective-permute-start(f32[4,2,256,256]{3,2,1,0:T(8,128)S(1)} %other_core.2.refs_3_), channel_id=1, source_target_pairs={{0,1},{1,0},{2,3},{3,2},{4,5},{5,4},{6,7},{7,6},{8,9},{9,8},{10,11... | collective-permute-start | bytes 6291464 | tf_op jit(solution)/shard_map/ppermute | solution.py:452
  15.9 8.1 %collective-permute-start.3 = (f32[4,2,256,256]{3,2,1,0:T(8,128)S(1)}, f32[4,2,256,256]{3,2,1,0:T(8,128)S(1)}, u32[]{:S(2)}, u32[]{:S(2)}) collective-permute-start(f32[4,2,256,256]{3,2,1,0:T(8,128)S(1)} %other_core.3.refs_5_), channel_id=1, source_target_pairs={{0,1},{1,0},{2,3},{3,2},{4,5},{5,4},{6,7},{7,6},{8,9},{9,8},{10,11... | collective-permute-start | bytes 6291464 | tf_op jit(solution)/shard_map/ppermute | solution.py:452
  19.1 7.0 %collective-permute-start.2 = (f32[4,2,256,256]{3,2,1,0:T(8,128)S(1)}, f32[4,2,256,256]{3,2,1,0:T(8,128)S(1)}, u32[]{:S(2)}, u32[]{:S(2)}) collective-permute-start(f32[4,2,256,256]{3,2,1,0:T(8,128)S(1)} %get-tuple-element.39.refs_4_), channel_id=1, source_target_pairs={{0,1},{1,0},{2,3},{3,2},{4,5},{5,4},{6,7},{7,6},{8,9},{9,8},{10,11... | collective-permute-start | bytes 6291464 | tf_op jit(solution)/shard_map/ppermute | solution.py:452
  19.2 8.9 %collective-permute-start.1 = (f32[4,2,256,256]{3,2,1,0:T(8,128)S(1)}, f32[4,2,256,256]{3,2,1,0:T(8,128)S(1)}, u32[]{:S(2)}, u32[]{:S(2)}) collective-permute-start(f32[4,2,256,256]{3,2,1,0:T(8,128)S(1)} %get-tuple-element.38), channel_id=1, source_target_pairs={{0,1},{1,0},{2,3},{3,2},{4,5},{5,4},{6,7},{7,6},{8,9},{9,8},{10,11... | collective-permute-start | bytes 6291464 | tf_op jit(solution)/shard_map/ppermute | solution.py:452
  20.3 22.7 %collective-permute-start.5 = (f32[2,2,256,256]{3,2,1,0:T(8,128)S(1)}, f32[2,2,256,256]{3,2,1,0:T(8,128)S(1)}, u32[]{:S(2)}, u32[]{:S(2)}) collective-permute-start(f32[2,2,256,256]{3,2,1,0:T(8,128)S(1)} %first_hop.4.refs_5_), channel_id=1, source_target_pairs={{0,16},{1,3},{2,18},{3,1},{16,0},{17,19},{18,2},{19,17},{4,20},{5,... | collective-permute-start | bytes 3145736 | tf_op jit(solution)/shard_map/ppermute | solution.py:503
  22.2 26.0 %collective-permute-start.7 = (f32[512,512]{1,0:T(8,128)S(1)}, f32[512,512]{1,0:T(8,128)S(1)}, u32[]{:S(2)}, u32[]{:S(2)}) collective-permute-start(f32[512,512]{1,0:T(8,128)S(1)} %head_terms.4.refs_4_), channel_id=1, source_target_pairs={{0,4},{4,0},{8,12},{12,8},{1,5},{5,1},{9,13},{13,9},{2,6},{6,2},{1... | collective-permute-start | bytes 3145736 | tf_op jit(solution)/shard_map/ppermute | solution.py:452
  24.5 26.7 %collective-permute-start.9 = (f32[2,2,256,256]{3,2,1,0:T(8,128)S(1)}, f32[2,2,256,256]{3,2,1,0:T(8,128)S(1)}, u32[]{:S(2)}, u32[]{:S(2)}) collective-permute-start(f32[2,2,256,256]{3,2,1,0:T(8,128)S(1)} %first_hop.5.refs_4_), channel_id=1, source_target_pairs={{0,2},{1,17},{2,0},{3,19},{16,18},{17,1},{18,16},{19,3},{4,6},{5,2... | collective-permute-start | bytes 3145736 | tf_op jit(solution)/shard_map/ppermute | solution.py:503
  26.7 38.8 %collective-permute-start.11 = (f32[2,2,256,256]{3,2,1,0:T(8,128)S(1)}, f32[2,2,256,256]{3,2,1,0:T(8,128)S(1)}, u32[]{:S(2)}, u32[]{:S(2)}) collective-permute-start(f32[2,2,256,256]{3,2,1,0:T(8,128)S(1)} %first_hop.6.refs_4_), channel_id=1, source_target_pairs={{0,16},{1,3},{2,18},{3,1},{16,0},{17,19},{18,2},{19,17},{4,20},{5,... | collective-permute-start | bytes 3145736 | tf_op jit(solution)/shard_map/ppermute | solution.py:503
  28.7 40.6 %collective-permute-start.10 = (f32[2,2,256,256]{3,2,1,0:T(8,128)S(1)}, f32[2,2,256,256]{3,2,1,0:T(8,128)S(1)}, u32[]{:S(2)}, u32[]{:S(2)}) collective-permute-start(f32[2,2,256,256]{3,2,1,0:T(8,128)S(1)} %first_hop.7.refs_5_), channel_id=1, source_target_pairs={{0,2},{1,17},{2,0},{3,19},{16,18},{17,1},{18,16},{19,3},{4,6},{5,2... | collective-permute-start | bytes 3145736 | tf_op jit(solution)/shard_map/ppermute | solution.py:503
  44.0 52.2 %collective-permute-start.6 = (f32[512,512]{1,0:T(8,128)S(1)}, f32[512,512]{1,0:T(8,128)S(1)}, u32[]{:S(2)}, u32[]{:S(2)}) collective-permute-start(f32[512,512]{1,0:T(8,128)S(1)} %head_terms.7.refs_2_), channel_id=1, source_target_pairs={{0,4},{4,0},{8,12},{12,8},{1,5},{5,1},{9,13},{13,9},{2,6},{6,2},{1... | collective-permute-start | bytes 3145736 | tf_op jit(solution)/shard_map/ppermute | solution.py:452
  48.4 47.8 %collective-permute-start.8 = (f32[512,512]{1,0:T(8,128)S(1)}, f32[512,512]{1,0:T(8,128)S(1)}, u32[]{:S(2)}, u32[]{:S(2)}) collective-permute-start(f32[512,512]{1,0:T(8,128)S(1)} %add.9.refs_7_), channel_id=1, source_target_pairs={{0,8},{4,12},{8,0},{12,4},{1,9},{5,13},{9,1},{13,5},{2,10},{6,14},... | collective-permute-start | bytes 3145736 | tf_op jit(solution)/shard_map/ppermute | solution.py:452
  66.7 24.6 %collective-permute-start.13 = (f32[2,2,256,256]{3,2,1,0:T(8,128)S(1)}, f32[2,2,256,256]{3,2,1,0:T(8,128)S(1)}, u32[]{:S(2)}, u32[]{:S(2)}) collective-permute-start(f32[2,2,256,256]{3,2,1,0:T(8,128)S(1)} %get-tuple-element.43), channel_id=1, source_target_pairs={{0,2},{1,17},{2,0},{3,19},{16,18},{17,1},{18,16},{19,3},{4,6},{5,2... | collective-permute-start | bytes 3145736 | tf_op jit(solution)/shard_map/ppermute | solution.py:503
  70.5 25.7 %collective-permute-start.12 = (f32[2,2,256,256]{3,2,1,0:T(8,128)S(1)}, f32[2,2,256,256]{3,2,1,0:T(8,128)S(1)}, u32[]{:S(2)}, u32[]{:S(2)}) collective-permute-start(f32[2,2,256,256]{3,2,1,0:T(8,128)S(1)} %get-tuple-element.42), channel_id=1, source_target_pairs={{0,16},{1,3},{2,18},{3,1},{16,0},{17,19},{18,2},{19,17},{4,20},{5,... | collective-permute-start | bytes 3145736 | tf_op jit(solution)/shard_map/ppermute | solution.py:503

commit v3 on v2

--- a/solution.py
+++ b/solution.py
@@ -55,27 +55,27 @@
     x_ref, o_ref = xo_ref.at[0], xo_ref.at[1]
     lower, upper = pl.ds(0, width // 2), pl.ds(width // 2, width // 2)
 
-    def first(slot, w_ref):
+    def first(w_ref):
         arrived(0)
         product = dot(x_ref[:, lower], w_ref[lower, :], NN)
         arrived(1)
-        out_ref[slot] = (product + dot(x_ref[:, upper], w_ref[upper, :], NN)).astype(BF16)
+        out_ref[0] = (product + dot(x_ref[:, upper], w_ref[upper, :], NN)).astype(BF16)
         arrived(2)
 
-    def state(slot):
+    def state():
         if state_ref is not None:
             for h in range(state_ref.shape[0]):
                 at = pl.ds(h * HEAD_DIM, HEAD_DIM)
-                state_ref[h] = dot(out_ref[slot, :, at], out_ref[slot + 1, :, at], TN)
+                state_ref[h] = dot(out_ref[0, :, at], out_ref[1, :, at], TN)
 
     if part == 0:
-        first(0, wk_ref)
+        first(wk_ref)
         out_ref[1] = dot(x_ref[...], wv_ref[...], NN).astype(BF16)
     else:
-        first(2, wq_ref)
+        first(wq_ref)
         scale = position_scale(place.seq * rows, rows)
-        out_ref[3] = (dot(o_ref[...], wo_ref[...], NT) * scale).astype(BF16)
-    state(2 * part)
+        out_ref[1] = (dot(o_ref[...], wo_ref[...], NT) * scale).astype(BF16)
+    state()
 
 
 def load_kernel(
@@ -130,7 +130,7 @@
         for a in (in_rows, grad_rows, w_query, w_key, w_value, w_out)
     ]
     out_shape = [
-        pltpu.VMEM((4, rows, hd), BF16),
+        pltpu.VMEM((2, rows, hd), BF16),
         pltpu.VMEM((hd // HEAD_DIM, HEAD_DIM, HEAD_DIM), F32),
         pltpu.VMEM((2, rows, width), BF16),
         *[pltpu.VMEM((width, hd), BF16)] * 3,
@@ -148,12 +148,10 @@
     )(number, *args)
 
 
-def project_kernel(place, part_ref, xo_ref, wq_ref, wk_ref, wv_ref, wo_ref, out_ref, *states, which):
+def project_kernel(place, xo_ref, wq_ref, wk_ref, wv_ref, wo_ref, out_ref, *states, which):
     state_ref = states[0] if states else None
 
     def run(part):
-        other = 2 - 2 * part
-        out_ref[other : other + 2] = part_ref[other : other + 2]
         project_part(
             place, part, xo_ref, wq_ref, wk_ref, wv_ref, wo_ref, out_ref, state_ref, lambda stage: None
         )
@@ -163,14 +161,14 @@
     pl.when(chosen != 0)(lambda: run(1))
 
 
-def project(place, which, part, xo, weights, w_out, with_state):
+def project(place, which, xo, weights, w_out, with_state):
     rows, width = xo.shape[1:]
-    hd = part.shape[2]
-    out = [shaped(part.shape, BF16)]
+    hd = w_out.shape[0]
+    out = [shaped((2, rows, hd), BF16)]
     if with_state:
         out.append(shaped((hd // HEAD_DIM, HEAD_DIM, HEAD_DIM), F32))
     kernel = functools.partial(project_kernel, which=which)
-    args = [part, xo, *weights, w_out]
+    args = [xo, *weights, w_out]
     return call(kernel, "project", out, args, 4 * rows * width * hd, (), place)
 
 
@@ -195,12 +193,13 @@
     )(*numbers, *args, *after)
 
 
-def attend_kernel(place, in_ref, *rest, which, again):
+def attend_kernel(place, *refs, which, part_of, again):
+    in_refs, rest = refs[:2], refs[2:]
     if again:
         state_ref, part_ref, scores_ref, out_ref = rest
     else:
         out_ref, scores_ref = rest
-    rows, hd = in_ref.shape[1:]
+    rows, hd = out_ref.shape[1:]
     half = rows // 2
     top, low = slice(0, half), slice(half, rows)
 
@@ -214,7 +213,9 @@
             scores_ref[h, n + 2] = jnp.where(diagonal, dot(a[low], b[low], NT), 0.0).astype(BF16)
         return [scores_ref[h, n + i] for i in range(3)]
 
-    def per_head(body):
+    def per_head(body, part):
+        k_v, q_g = in_refs[part], in_refs[1 - part]
+
         def step(h, carry):
             at = pl.ds(pl.multiple_of(h * HEAD_DIM, HEAD_DIM), HEAD_DIM)
             state = state_ref[h].astype(BF16) if again else None
@@ -228,7 +229,7 @@
                         value = value * scale[rows_at]
                     out_ref[slot, rows_at, at] = value.astype(BF16)
 
-            body(h, [in_ref[slot, :, at] for slot in range(4)], put)
+            body(h, [ref[i, :, at] for ref in (k_v, q_g) for i in (0, 1)], put)
             return carry
 
         lax.fori_loop(0, hd // HEAD_DIM, step, 0, unroll=True)
@@ -243,7 +244,7 @@
                 halves = (dot(s00, c[top], NN), dot(s10, c[top], NN) + dot(s11, c[low], NN))
                 put(slot, halves, a, dims, scale if slot == 0 else None)
 
-        per_head(body)
+        per_head(body, part_of(0))
 
     def backward():
         def body(h, heads, put):
@@ -253,7 +254,7 @@
                 halves = (dot(s00, c[top], TN) + dot(s10, c[low], TN), dot(s11, c[low], TN))
                 put(slot, halves, b, dims)
 
-        per_head(body)
+        per_head(body, part_of(1))
 
     chosen = which(place)
     if again:
@@ -263,13 +264,13 @@
     pl.when(chosen != 0)(backward)
 
 
-def attend(place, which, projected, more=(), after=()):
-    rows, hd = projected.shape[1:]
+def attend(place, which, part_of, projected, more=(), after=()):
+    rows, hd = projected[0].shape[1:]
     out = shaped((4, rows, hd), BF16)
     scores = shaped((hd // HEAD_DIM, 6, rows // 2, rows // 2), BF16)
-    kernel = functools.partial(attend_kernel, which=which, again=bool(more))
+    kernel = functools.partial(attend_kernel, which=which, part_of=part_of, again=bool(more))
     outs = out if more else [out, scores]
-    return call(kernel, "attend", outs, [projected, *more], 128 * rows * rows * hd, after, place)
+    return call(kernel, "attend", outs, [*projected, *more], 128 * rows * rows * hd, after, place)
 
 
 def head_terms_kernel(place, d_ref, wq_ref, wk_ref, wv_ref, out_ref, *, shard):
@@ -467,16 +468,15 @@
     projected, state, xo, *weights, wo = load(place, part, *arrays)
     if planned:
         state = swap(state, "seq", 1)
-    projected, *more = project(
-        place, lambda at: 1 - part(at), projected, xo, weights, wo, not planned
-    )
+    other, *more = project(place, lambda at: 1 - part(at), xo, weights, wo, not planned)
+    projected = (projected, other)
 
     if not planned:
         prefix = states_before(state, "seq", False)
         suffix = states_before(more[0], "seq", True)
-        d, scores = attend(place, lambda at: 0, projected)
-        d = attend(place, lambda at: 0, projected, (prefix, d, scores))
-        d = attend(place, lambda at: 1, projected, (suffix, d, scores))
+        d, scores = attend(place, lambda at: 0, lambda which: 0, projected)
+        d = attend(place, lambda at: 0, lambda which: 0, projected, (prefix, d, scores))
+        d = attend(place, lambda at: 1, lambda which: 0, projected, (suffix, d, scores))
         terms = head_terms(place, d, weights, lambda at: 0, 1)
 
         def reduced(rows, d):
@@ -502,7 +502,7 @@
             pairs.append((i, i ^ (4 if side == second else 2)))
         return lax.ppermute(array, ("seq", "dp"), pairs)
 
-    block, half = xo.shape[2] // 8, projected.shape[2] // 2
+    block, half = xo.shape[2] // 8, projected[0].shape[2] // 2
     tile = (2, block, half)
     flops = 4 * num_rows * block * half
 
@@ -532,11 +532,11 @@
         keep, leave = call(kernel, "second_hop", outs, args, 4 * flops, after, place)
         return keep, hop(leave, slot, 1)
 
-    early, scores = attend(place, lambda at: at.seq, projected)
+    early, scores = attend(place, lambda at: at.seq, lambda which: which, projected)
     far = ([None, None], [None, None])
     at, far[0][0] = to_core(early, 0, 0, [])
     at, far[0][1] = to_core(early, 0, 1, [at])
-    d = attend(place, lambda at: 1 - at.seq, projected, (state, early, scores), [at])
+    d = attend(place, lambda at: 1 - at.seq, lambda which: 1 - which, projected, (state, early, scores), [at])
     at, far[1][:] = both_to_core(d, 1, [])
     at, over1 = first_hop(0, 0, [at])
     t3 = term(3, [at])

time: 97.9 us -> 97.7 us (level)
  no operation moved by 1% of the time
where the time goes in v3:
time: 97.7 us; the launch traced here: 97.6 us
  waiting for transfers between devices  50.4 us (52%)
  Pallas kernels  25.6 us (26%)
  starting transfers between devices  20.6 us (21%)
    ppermute x6, waiting for transfers between devices, hop(): return lax.ppermute(array, ('seq', 'dp'), pairs)  44.7 us
    pallas_call x17, Pallas kernels, call(): pl.pallas_call(body, out_shape=out_shape, in_specs=[IN_SMEM] * len(number...  17.9 us
    ppermute x8, starting transfers between devices, swap(): lax.ppermute(x, axis, [(i, i ^ bit) for i in range(lax.axis_size(axis))])  11.7 us
    ppermute x6, starting transfers between devices, hop(): return lax.ppermute(array, ('seq', 'dp'), pairs)  8.88 us
    ppermute x8, waiting for transfers between devices, swap(): lax.ppermute(x, axis, [(i, i ^ bit) for i in range(lax.axis_size(axis))])  5.75 us
    pallas_call x1, Pallas kernels, load(): pl.pallas_call(functools.partial(load_kernel, sizes=sizes, which=which),...  5.2 us
  transfers between devices with their start and end apart: 14, of which 6 were waited for; matrix products, arithmetic and copies ran while one was open for 0% of the time, Pallas kernels for 19%

profile of v3, /device:TPU:0, one launch (start us, length us, event | category | flops | bytes accessed | tf_op | source)
XLA Modules:
  0.0 97.6 jit_solution(15134819977022415071)
XLA Ops:
  0.6 5.2 %load.1 = (bf16[2,512,512]{2,1,0:T(8,128)(2,1)S(1)}, f32[4,128,128]{2,1,0:T(8,128)S(1)}, bf16[2,512,2048]{2,1,0:T(8,128)(2,1)S(1)}, bf16[2048,512]{1,0:T(8,128)(...) custom-call(s32[1]{0:T(128)} %bitcast.number_ref.refs_0_, ...), custom_call_target="tpu_custom_call" | custom-call | flops 2147483648 | bytes 14680064 | tf_op jit(solution)/shard_map/load/pallas_call | solution.py:139
  5.8 3.4 %collective-permute-start = (f32[4,128,128]{2,1,0:T(8,128)S(1)}, f32[4,128,128]{2,1,0:T(8,128)S(1)}, u32[]{:S(2)}, u32[]{:S(2)}) collective-permute-start(f32[4,128,128]{2,1,0:T(8,128)S(1)} %get-tuple-element.35), channel_id=1, source_target_pairs={{0,16},{16,0},{1,17},{17,1},{2,18},{18,2},{3,19},{19,3},{4,20},{20... | collective-permute-start | bytes 786440 | tf_op jit(solution)/shard_map/ppermute | solution.py:453
  9.2 2.3 %project.1.refs_2_ = bf16[2,512,512]{2,1,0:T(8,128)(2,1)S(1)} custom-call(s32[1]{0:T(128)} %bitcast.number_ref.refs_0_, bf16[2,512,2048]{2,1,0:T(8,128)(2,1)S(1)} %get-tuple-element.30.refs_1_, bf16[2048,512]{1,0:T(8,128)(2,1)S(1)} %get-tuple-element.31.refs_2_, bf16[2048,512]{1,0:T(8,128)(2,1)S(1)} %get-tuple-element.32.refs_3_, ...), custom_call_target="tpu_custom_call" | custom-call | flops 2147483648 | bytes 2097152 | tf_op jit(solution)/shard_map/project/pallas_call | solution.py:185
  11.6 2.5 %attend.2 = (bf16[4,512,512]{2,1,0:T(8,128)(2,1)S(1)}, bf16[4,6,256,256]{3,2,1,0:T(8,128)(2,1)S(1)}) custom-call(s32[1]{0:T(128)} %bitcast.number_ref.refs_0_, bf16[2,512,512]{2,1,0:T(8,128)(2,1)S(1)} %get-tuple-element.29.refs_1_, bf16[2,512,512]{2,1,0:T(8,128)(2,1)S(1)} %project.1.refs_2_), custom_call_target="tpu_custom_call" | custom-call | flops 17179869184 | bytes 2097152 | tf_op jit(solution)/shard_map/attend/pallas_call | solution.py:185
  14.0 0.8 other_core.2.refs_3_
  14.9 0.1 collective-permute-start.4
  15.0 0.9 other_core.3.refs_6_
  15.8 0.5 collective-permute-start.3
  16.4 0.0 collective-permute-done.refs_3_
  16.4 1.4 %attend.3.refs_2_.refs_1_ = bf16[4,512,512]{2,1,0:T(8,128)(2,1)S(1)} custom-call(s32[1]{0:T(128)} %bitcast.number_ref.refs_0_, bf16[2,512,512]{2,1,0:T(8,128)(2,1)S(1)} %get-tuple-element.29.refs_1_, bf16[2,512,512]{2,1,0:T(8,128)(2,1)S(1)} %project.1.refs_2_, f32[4,128,128]{2,1,0:T(8,128)S(1)} %collective-permute-done.refs_3_, ...), custom_call_target="tpu_custom_call" | custom-call | flops 17179869184 | bytes 2097152 | tf_op jit(solution)/shard_map/attend/pallas_call | solution.py:185
  17.8 1.3 %other_core_both.1 = (f32[4,2,256,256]{3,2,1,0:T(8,128)S(1)}, f32[4,2,256,256]{3,2,1,0:T(8,128)S(1)}) custom-call(s32[1]{0:T(128)} %bitcast.number_ref.refs_0_, bf16[2,512,2048]{2,1,0:T(8,128)(2,1)S(1)} %get-tuple-element.30.refs_1_, bf16[4,512,512]{2,1,0:T(8,128)(2,1)S(1)} %attend.3.refs_2_.refs_1_), custom_call_target="tpu_custom_call" | custom-call | flops 1073741824 | bytes 2097152 | tf_op jit(solution)/shard_map/other_core_both/pallas_call | solution.py:185
  19.1 0.1 collective-permute-start.2
  19.2 0.5 collective-permute-start.1
  19.6 0.0 collective-permute-done.4.refs_3_
  19.7 0.5 first_hop.4.refs_5_
  20.2 1.0 %collective-permute-start.5 = (f32[2,2,256,256]{3,2,1,0:T(8,128)S(1)}, f32[2,2,256,256]{3,2,1,0:T(8,128)S(1)}, u32[]{:S(2)}, u32[]{:S(2)}) collective-permute-start(f32[2,2,256,256]{3,2,1,0:T(8,128)S(1)} %first_hop.4.refs_5_), channel_id=1, source_target_pairs={{0,16},{1,3},{2,18},{3,1},{16,0},{17,19},{18,2},{19,17},{4,20},{5,... | collective-permute-start | bytes 3145736 | tf_op jit(solution)/shard_map/ppermute | solution.py:503
  21.2 1.0 %head_terms.4.refs_4_ = f32[512,512]{1,0:T(8,128)S(1)} custom-call(s32[1]{0:T(128)} %bitcast.number_ref.refs_0_, bf16[4,512,512]{2,1,0:T(8,128)(2,1)S(1)} %attend.3.refs_2_.refs_1_, bf16[2048,512]{1,0:T(8,128)(2,1)S(1)} %get-tuple-element.31.refs_2_, bf16[2048,512]{1,0:T(8,128)(2,1)S(1)} %get-tuple-element.32.refs_3_, ...), custom_call_target="tpu_custom_call" | custom-call | flops 805306368 | bytes 2097152 | tf_op jit(solution)/shard_map/head_terms/pallas_call | solution.py:185
  22.2 1.7 %collective-permute-start.7 = (f32[512,512]{1,0:T(8,128)S(1)}, f32[512,512]{1,0:T(8,128)S(1)}, u32[]{:S(2)}, u32[]{:S(2)}) collective-permute-start(f32[512,512]{1,0:T(8,128)S(1)} %head_terms.4.refs_4_), channel_id=1, source_target_pairs={{0,4},{4,0},{8,12},{12,8},{1,5},{5,1},{9,13},{13,9},{2,6},{6,2},{1... | collective-permute-start | bytes 3145736 | tf_op jit(solution)/shard_map/ppermute | solution.py:453
  23.9 0.0 collective-permute-done.3.refs_3_
  23.9 0.5 first_hop.5.refs_4_
  24.4 1.6 %collective-permute-start.9 = (f32[2,2,256,256]{3,2,1,0:T(8,128)S(1)}, f32[2,2,256,256]{3,2,1,0:T(8,128)S(1)}, u32[]{:S(2)}, u32[]{:S(2)}) collective-permute-start(f32[2,2,256,256]{3,2,1,0:T(8,128)S(1)} %first_hop.5.refs_4_), channel_id=1, source_target_pairs={{0,2},{1,17},{2,0},{3,19},{16,18},{17,1},{18,16},{19,3},{4,6},{5,2... | collective-permute-start | bytes 3145736 | tf_op jit(solution)/shard_map/ppermute | solution.py:503
  26.0 0.0 collective-permute-done.2.refs_3_.refs_4_
  26.0 0.5 first_hop.6.refs_4_
  26.6 1.1 %collective-permute-start.11 = (f32[2,2,256,256]{3,2,1,0:T(8,128)S(1)}, f32[2,2,256,256]{3,2,1,0:T(8,128)S(1)}, u32[]{:S(2)}, u32[]{:S(2)}) collective-permute-start(f32[2,2,256,256]{3,2,1,0:T(8,128)S(1)} %first_hop.6.refs_4_), channel_id=1, source_target_pairs={{0,16},{1,3},{2,18},{3,1},{16,0},{17,19},{18,2},{19,17},{4,20},{5,... | collective-permute-start | bytes 3145736 | tf_op jit(solution)/shard_map/ppermute | solution.py:503
  27.7 0.4 collective-permute-done.1.refs_3_.refs_4_
  28.1 0.5 first_hop.7.refs_5_
  28.6 1.6 %collective-permute-start.10 = (f32[2,2,256,256]{3,2,1,0:T(8,128)S(1)}, f32[2,2,256,256]{3,2,1,0:T(8,128)S(1)}, u32[]{:S(2)}, u32[]{:S(2)}) collective-permute-start(f32[2,2,256,256]{3,2,1,0:T(8,128)S(1)} %first_hop.7.refs_5_), channel_id=1, source_target_pairs={{0,2},{1,17},{2,0},{3,19},{16,18},{17,1},{18,16},{19,3},{4,6},{5,2... | collective-permute-start | bytes 3145736 | tf_op jit(solution)/shard_map/ppermute | solution.py:503
  30.2 1.0 %head_terms.5.refs_5_.refs_0_ = f32[512,512]{1,0:T(8,128)S(1)} custom-call(s32[1]{0:T(128)} %bitcast.number_ref.refs_0_, bf16[4,512,512]{2,1,0:T(8,128)(2,1)S(1)} %attend.3.refs_2_.refs_1_, bf16[2048,512]{1,0:T(8,128)(2,1)S(1)} %get-tuple-element.31.refs_2_, bf16[2048,512]{1,0:T(8,128)(2,1)S(1)} %get-tuple-element.32.refs_3_, ...), custom_call_target="tpu_custom_call" | custom-call | flops 805306368 | bytes 2097152 | tf_op jit(solution)/shard_map/head_terms/pallas_call | solution.py:185
  31.2 1.0 %head_terms.6.refs_5_.refs_0_ = f32[512,512]{1,0:T(8,128)S(1)} custom-call(s32[1]{0:T(128)} %bitcast.number_ref.refs_0_, bf16[4,512,512]{2,1,0:T(8,128)(2,1)S(1)} %attend.3.refs_2_.refs_1_, bf16[2048,512]{1,0:T(8,128)(2,1)S(1)} %get-tuple-element.31.refs_2_, bf16[2048,512]{1,0:T(8,128)(2,1)S(1)} %get-tuple-element.32.refs_3_, ...), custom_call_target="tpu_custom_call" | custom-call | flops 805306368 | bytes 2097152 | tf_op jit(solution)/shard_map/head_terms/pallas_call | solution.py:185
  32.3 10.6 %collective-permute-done.5.refs_6_.refs_5_ = f32[2,2,256,256]{3,2,1,0:T(8,128)S(1)} collective-permute-done((f32[2,2,256,256]{3,2,1,0:T(8,128)S(1)}, f32[2,2,256,256]{3,2,1,0:T(8,128)S(1)}, u32[]{:S(2)}, u32[]{:S(2)}) %collective-permute-start.5) | collective-permute-done | bytes 1048608 | tf_op jit(solution)/shard_map/ppermute | solution.py:503
  42.9 1.0 %head_terms.7.refs_2_ = f32[512,512]{1,0:T(8,128)S(1)} custom-call(s32[1]{0:T(128)} %bitcast.number_ref.refs_0_, bf16[4,512,512]{2,1,0:T(8,128)(2,1)S(1)} %attend.3.refs_2_.refs_1_, bf16[2048,512]{1,0:T(8,128)(2,1)S(1)} %get-tuple-element.31.refs_2_, bf16[2048,512]{1,0:T(8,128)(2,1)S(1)} %get-tuple-element.32.refs_3_, ...), custom_call_target="tpu_custom_call" | custom-call | flops 805306368 | bytes 2097152 | tf_op jit(solution)/shard_map/head_terms/pallas_call | solution.py:185
  43.9 2.8 %collective-permute-start.6 = (f32[512,512]{1,0:T(8,128)S(1)}, f32[512,512]{1,0:T(8,128)S(1)}, u32[]{:S(2)}, u32[]{:S(2)}) collective-permute-start(f32[512,512]{1,0:T(8,128)S(1)} %head_terms.7.refs_2_), channel_id=1, source_target_pairs={{0,4},{4,0},{8,12},{12,8},{1,5},{5,1},{9,13},{13,9},{2,6},{6,2},{1... | collective-permute-start | bytes 3145736 | tf_op jit(solution)/shard_map/ppermute | solution.py:453
  46.7 1.6 %collective-permute-done.7.refs_1_ = f32[512,512]{1,0:T(8,128)S(1)} collective-permute-done((f32[512,512]{1,0:T(8,128)S(1)}, f32[512,512]{1,0:T(8,128)S(1)}, u32[]{:S(2)}, u32[]{:S(2)}) %collective-permute-start.7) | collective-permute-done | bytes 1048608 | tf_op jit(solution)/shard_map/ppermute | solution.py:453
  48.3 0.2 add.9.refs_7_
  48.4 2.7 %collective-permute-start.8 = (f32[512,512]{1,0:T(8,128)S(1)}, f32[512,512]{1,0:T(8,128)S(1)}, u32[]{:S(2)}, u32[]{:S(2)}) collective-permute-start(f32[512,512]{1,0:T(8,128)S(1)} %add.9.refs_7_), channel_id=1, source_target_pairs={{0,8},{4,12},{8,0},{12,4},{1,9},{5,13},{9,1},{13,5},{2,10},{6,14},... | collective-permute-start | bytes 3145736 | tf_op jit(solution)/shard_map/ppermute | solution.py:453
  51.1 0.0 collective-permute-done.9.refs_8_.refs_5_
  51.1 14.3 %collective-permute-done.11.refs_6_ = f32[2,2,256,256]{3,2,1,0:T(8,128)S(1)} collective-permute-done((f32[2,2,256,256]{3,2,1,0:T(8,128)S(1)}, f32[2,2,256,256]{3,2,1,0:T(8,128)S(1)}, u32[]{:S(2)}, u32[]{:S(2)}) %collective-permute-start.11) | collective-permute-done | bytes 1048608 | tf_op jit(solution)/shard_map/ppermute | solution.py:503
  65.4 1.2 %second_hop.2 = (f32[2,2,256,256]{3,2,1,0:T(8,128)S(1)}, f32[2,2,256,256]{3,2,1,0:T(8,128)S(1)}) custom-call(s32[1]{0:T(128)} %bitcast.number_ref.refs_0_, bf16[2,512,2048]{2,1,0:T(8,128)(2,1)S(1)} %get-tuple-element.30.refs_1_, bf16[4,512,512]{2,1,0:T(8,128)(2,1)S(1)} %attend.3.refs_2_.refs_1_, f32[4,2,256,256]{3,2,1,0:T(8,128)S(1)} %collective-permute-done.4.refs_3_, ...), custom_call_target="tpu_custom_call" | custom-call | flops 536870912 | bytes 2097152 | tf_op jit(solution)/shard_map/second_hop/pallas_call | solution.py:185
  66.6 2.6 %collective-permute-start.13 = (f32[2,2,256,256]{3,2,1,0:T(8,128)S(1)}, f32[2,2,256,256]{3,2,1,0:T(8,128)S(1)}, u32[]{:S(2)}, u32[]{:S(2)}) collective-permute-start(f32[2,2,256,256]{3,2,1,0:T(8,128)S(1)} %get-tuple-element.43), channel_id=1, source_target_pairs={{0,2},{1,17},{2,0},{3,19},{16,18},{17,1},{18,16},{19,3},{4,6},{5,2... | collective-permute-start | bytes 3145736 | tf_op jit(solution)/shard_map/ppermute | solution.py:503
  69.2 0.0 collective-permute-done.10.refs_6_
  69.2 1.2 %second_hop.3 = (f32[2,2,256,256]{3,2,1,0:T(8,128)S(1)}, f32[2,2,256,256]{3,2,1,0:T(8,128)S(1)}) custom-call(s32[1]{0:T(128)} %bitcast.number_ref.refs_0_, bf16[2,512,2048]{2,1,0:T(8,128)(2,1)S(1)} %get-tuple-element.30.refs_1_, bf16[4,512,512]{2,1,0:T(8,128)(2,1)S(1)} %attend.3.refs_2_.refs_1_, f32[4,2,256,256]{3,2,1,0:T(8,128)S(1)} %collective-permute-done.3.refs_3_, ...), custom_call_target="tpu_custom_call" | custom-call | flops 536870912 | bytes 2097152 | tf_op jit(solution)/shard_map/second_hop/pallas_call | solution.py:185
  70.4 1.0 %collective-permute-start.12 = (f32[2,2,256,256]{3,2,1,0:T(8,128)S(1)}, f32[2,2,256,256]{3,2,1,0:T(8,128)S(1)}, u32[]{:S(2)}, u32[]{:S(2)}) collective-permute-start(f32[2,2,256,256]{3,2,1,0:T(8,128)S(1)} %get-tuple-element.42), channel_id=1, source_target_pairs={{0,16},{1,3},{2,18},{3,1},{16,0},{17,19},{18,2},{19,17},{4,20},{5,... | collective-permute-start | bytes 3145736 | tf_op jit(solution)/shard_map/ppermute | solution.py:503
  71.4 19.8 %collective-permute-done.13.moved_ref = f32[2,2,256,256]{3,2,1,0:T(8,128)S(1)} collective-permute-done((f32[2,2,256,256]{3,2,1,0:T(8,128)S(1)}, f32[2,2,256,256]{3,2,1,0:T(8,128)S(1)}, u32[]{:S(2)}, u32[]{:S(2)}) %collective-permute-start.13) | collective-permute-done | bytes 1048608 | tf_op jit(solution)/shard_map/ppermute | solution.py:503
  91.2 1.0 %settle.1 = (f32[256,512]{1,0:T(8,128)}, f32[256,512]{1,0:T(8,128)}, f32[256,512]{1,0:T(8,128)}, f32[512,256]{1,0:T(8,128)}) custom-call(s32[1]{0:T(128)} %bitcast.number_ref.refs_0_, f32[2,2,256,256]{3,2,1,0:T(8,128)S(1)} %get-tuple-element.40.refs_7_.kept_ref, f32[2,2,256,256]{3,2,1,0:T(8,128)S(1)} %collective-permute-done.13.moved_ref, ...), custom_call_target="tpu_custom_call" | custom-call | bytes 2097152 | tf_op jit(solution)/shard_map/settle/pallas_call | solution.py:421
  92.2 3.7 %collective-permute-done.8.refs_2_ = f32[512,512]{1,0:T(8,128)S(1)} collective-permute-done((f32[512,512]{1,0:T(8,128)S(1)}, f32[512,512]{1,0:T(8,128)S(1)}, u32[]{:S(2)}, u32[]{:S(2)}) %collective-permute-start.8) | collective-permute-done | bytes 1048608 | tf_op jit(solution)/shard_map/ppermute | solution.py:453
  96.0 0.0 collective-permute-done.6.refs_1_
  96.0 0.0 collective-permute-done.12.refs_4_
  96.0 1.5 %finish.1 = (bf16[512,512]{1,0:T(8,128)(2,1)}, f32[256,512]{1,0:T(8,128)}, f32[256,512]{1,0:T(8,128)}, f32[256,512]{1,0:T(8,128)}, f32[512,256]{1,0:T(8,128)}) custom-call(s32[1]{0:T(128)} %bitcast.number_ref.refs_0_, f32[512,512]{1,0:T(8,128)S(1)} %head_terms.6.refs_5_.refs_0_, ...), custom_call_target="tpu_custom_call", output_to_operand_aliasing={{1}: (6, {}), {2}: (7, {}), {3}: (8, {}), {4}: (9, {})} | custom-call | bytes 2097152 | tf_op jit(solution)/shard_map/finish/pallas_call | solution.py:431
Async XLA Ops:
  5.8 10.5 %collective-permute-start = (f32[4,128,128]{2,1,0:T(8,128)S(1)}, f32[4,128,128]{2,1,0:T(8,128)S(1)}, u32[]{:S(2)}, u32[]{:S(2)}) collective-permute-start(f32[4,128,128]{2,1,0:T(8,128)S(1)} %get-tuple-element.35), channel_id=1, source_target_pairs={{0,16},{16,0},{1,17},{17,1},{2,18},{18,2},{3,19},{19,3},{4,20},{20... | collective-permute-start | bytes 786440 | tf_op jit(solution)/shard_map/ppermute | solution.py:453
  14.9 4.8 %collective-permute-start.4 = (f32[4,2,256,256]{3,2,1,0:T(8,128)S(1)}, f32[4,2,256,256]{3,2,1,0:T(8,128)S(1)}, u32[]{:S(2)}, u32[]{:S(2)}) collective-permute-start(f32[4,2,256,256]{3,2,1,0:T(8,128)S(1)} %other_core.2.refs_3_), channel_id=1, source_target_pairs={{0,1},{1,0},{2,3},{3,2},{4,5},{5,4},{6,7},{7,6},{8,9},{9,8},{10,11... | collective-permute-start | bytes 6291464 | tf_op jit(solution)/shard_map/ppermute | solution.py:453
  15.8 8.1 %collective-permute-start.3 = (f32[4,2,256,256]{3,2,1,0:T(8,128)S(1)}, f32[4,2,256,256]{3,2,1,0:T(8,128)S(1)}, u32[]{:S(2)}, u32[]{:S(2)}) collective-permute-start(f32[4,2,256,256]{3,2,1,0:T(8,128)S(1)} %other_core.3.refs_6_), channel_id=1, source_target_pairs={{0,1},{1,0},{2,3},{3,2},{4,5},{5,4},{6,7},{7,6},{8,9},{9,8},{10,11... | collective-permute-start | bytes 6291464 | tf_op jit(solution)/shard_map/ppermute | solution.py:453
  19.1 7.0 %collective-permute-start.2 = (f32[4,2,256,256]{3,2,1,0:T(8,128)S(1)}, f32[4,2,256,256]{3,2,1,0:T(8,128)S(1)}, u32[]{:S(2)}, u32[]{:S(2)}) collective-permute-start(f32[4,2,256,256]{3,2,1,0:T(8,128)S(1)} %get-tuple-element.39.refs_4_), channel_id=1, source_target_pairs={{0,1},{1,0},{2,3},{3,2},{4,5},{5,4},{6,7},{7,6},{8,9},{9,8},{10,11... | collective-permute-start | bytes 6291464 | tf_op jit(solution)/shard_map/ppermute | solution.py:453
  19.2 8.9 %collective-permute-start.1 = (f32[4,2,256,256]{3,2,1,0:T(8,128)S(1)}, f32[4,2,256,256]{3,2,1,0:T(8,128)S(1)}, u32[]{:S(2)}, u32[]{:S(2)}) collective-permute-start(f32[4,2,256,256]{3,2,1,0:T(8,128)S(1)} %get-tuple-element.38), channel_id=1, source_target_pairs={{0,1},{1,0},{2,3},{3,2},{4,5},{5,4},{6,7},{7,6},{8,9},{9,8},{10,11... | collective-permute-start | bytes 6291464 | tf_op jit(solution)/shard_map/ppermute | solution.py:453
  20.2 22.7 %collective-permute-start.5 = (f32[2,2,256,256]{3,2,1,0:T(8,128)S(1)}, f32[2,2,256,256]{3,2,1,0:T(8,128)S(1)}, u32[]{:S(2)}, u32[]{:S(2)}) collective-permute-start(f32[2,2,256,256]{3,2,1,0:T(8,128)S(1)} %first_hop.4.refs_5_), channel_id=1, source_target_pairs={{0,16},{1,3},{2,18},{3,1},{16,0},{17,19},{18,2},{19,17},{4,20},{5,... | collective-permute-start | bytes 3145736 | tf_op jit(solution)/shard_map/ppermute | solution.py:503
  22.2 26.1 %collective-permute-start.7 = (f32[512,512]{1,0:T(8,128)S(1)}, f32[512,512]{1,0:T(8,128)S(1)}, u32[]{:S(2)}, u32[]{:S(2)}) collective-permute-start(f32[512,512]{1,0:T(8,128)S(1)} %head_terms.4.refs_4_), channel_id=1, source_target_pairs={{0,4},{4,0},{8,12},{12,8},{1,5},{5,1},{9,13},{13,9},{2,6},{6,2},{1... | collective-permute-start | bytes 3145736 | tf_op jit(solution)/shard_map/ppermute | solution.py:453
  24.4 26.7 %collective-permute-start.9 = (f32[2,2,256,256]{3,2,1,0:T(8,128)S(1)}, f32[2,2,256,256]{3,2,1,0:T(8,128)S(1)}, u32[]{:S(2)}, u32[]{:S(2)}) collective-permute-start(f32[2,2,256,256]{3,2,1,0:T(8,128)S(1)} %first_hop.5.refs_4_), channel_id=1, source_target_pairs={{0,2},{1,17},{2,0},{3,19},{16,18},{17,1},{18,16},{19,3},{4,6},{5,2... | collective-permute-start | bytes 3145736 | tf_op jit(solution)/shard_map/ppermute | solution.py:503
  26.6 38.8 %collective-permute-start.11 = (f32[2,2,256,256]{3,2,1,0:T(8,128)S(1)}, f32[2,2,256,256]{3,2,1,0:T(8,128)S(1)}, u32[]{:S(2)}, u32[]{:S(2)}) collective-permute-start(f32[2,2,256,256]{3,2,1,0:T(8,128)S(1)} %first_hop.6.refs_4_), channel_id=1, source_target_pairs={{0,16},{1,3},{2,18},{3,1},{16,0},{17,19},{18,2},{19,17},{4,20},{5,... | collective-permute-start | bytes 3145736 | tf_op jit(solution)/shard_map/ppermute | solution.py:503
  28.6 40.6 %collective-permute-start.10 = (f32[2,2,256,256]{3,2,1,0:T(8,128)S(1)}, f32[2,2,256,256]{3,2,1,0:T(8,128)S(1)}, u32[]{:S(2)}, u32[]{:S(2)}) collective-permute-start(f32[2,2,256,256]{3,2,1,0:T(8,128)S(1)} %first_hop.7.refs_5_), channel_id=1, source_target_pairs={{0,2},{1,17},{2,0},{3,19},{16,18},{17,1},{18,16},{19,3},{4,6},{5,2... | collective-permute-start | bytes 3145736 | tf_op jit(solution)/shard_map/ppermute | solution.py:503
  43.9 52.1 %collective-permute-start.6 = (f32[512,512]{1,0:T(8,128)S(1)}, f32[512,512]{1,0:T(8,128)S(1)}, u32[]{:S(2)}, u32[]{:S(2)}) collective-permute-start(f32[512,512]{1,0:T(8,128)S(1)} %head_terms.7.refs_2_), channel_id=1, source_target_pairs={{0,4},{4,0},{8,12},{12,8},{1,5},{5,1},{9,13},{13,9},{2,6},{6,2},{1... | collective-permute-start | bytes 3145736 | tf_op jit(solution)/shard_map/ppermute | solution.py:453
  48.4 47.6 %collective-permute-start.8 = (f32[512,512]{1,0:T(8,128)S(1)}, f32[512,512]{1,0:T(8,128)S(1)}, u32[]{:S(2)}, u32[]{:S(2)}) collective-permute-start(f32[512,512]{1,0:T(8,128)S(1)} %add.9.refs_7_), channel_id=1, source_target_pairs={{0,8},{4,12},{8,0},{12,4},{1,9},{5,13},{9,1},{13,5},{2,10},{6,14},... | collective-permute-start | bytes 3145736 | tf_op jit(solution)/shard_map/ppermute | solution.py:453
  66.6 24.6 %collective-permute-start.13 = (f32[2,2,256,256]{3,2,1,0:T(8,128)S(1)}, f32[2,2,256,256]{3,2,1,0:T(8,128)S(1)}, u32[]{:S(2)}, u32[]{:S(2)}) collective-permute-start(f32[2,2,256,256]{3,2,1,0:T(8,128)S(1)} %get-tuple-element.43), channel_id=1, source_target_pairs={{0,2},{1,17},{2,0},{3,19},{16,18},{17,1},{18,16},{19,3},{4,6},{5,2... | collective-permute-start | bytes 3145736 | tf_op jit(solution)/shard_map/ppermute | solution.py:503
  70.4 25.6 %collective-permute-start.12 = (f32[2,2,256,256]{3,2,1,0:T(8,128)S(1)}, f32[2,2,256,256]{3,2,1,0:T(8,128)S(1)}, u32[]{:S(2)}, u32[]{:S(2)}) collective-permute-start(f32[2,2,256,256]{3,2,1,0:T(8,128)S(1)} %get-tuple-element.42), channel_id=1, source_target_pairs={{0,16},{1,3},{2,18},{3,1},{16,0},{17,19},{18,2},{19,17},{4,20},{5,... | collective-permute-start | bytes 3145736 | tf_op jit(solution)/shard_map/ppermute | solution.py:503

commit v4 on v3

--- a/solution.py
+++ b/solution.py
@@ -196,7 +196,7 @@
 def attend_kernel(place, *refs, which, part_of, again):
     in_refs, rest = refs[:2], refs[2:]
     if again:
-        state_ref, part_ref, scores_ref, out_ref = rest
+        state_ref, scores_ref, out_ref = rest
     else:
         out_ref, scores_ref = rest
     rows, hd = out_ref.shape[1:]
@@ -249,51 +249,54 @@
     def backward():
         def body(h, heads, put):
             k, v, q, g = heads
-            for slot, a, b, c, dims in ((2, q, k, g, NN), (3, g, v, q, NT)):
-                s00, s10, s11 = causal(h, 3 * slot - 6, a, b)
+            for slot, a, b, c, dims in ((0, q, k, g, NN), (1, g, v, q, NT)):
+                s00, s10, s11 = causal(h, 3 * slot, a, b)
                 halves = (dot(s00, c[top], TN) + dot(s10, c[low], TN), dot(s11, c[low], TN))
                 put(slot, halves, b, dims)
 
         per_head(body, part_of(1))
 
     chosen = which(place)
-    if again:
-        for t in (0, 1):
-            out_ref[2 - 2 * chosen + t] = part_ref[2 - 2 * chosen + t]
     pl.when(chosen == 0)(forward)
     pl.when(chosen != 0)(backward)
 
 
 def attend(place, which, part_of, projected, more=(), after=()):
     rows, hd = projected[0].shape[1:]
-    out = shaped((4, rows, hd), BF16)
+    out = shaped((2, rows, hd), BF16)
     scores = shaped((hd // HEAD_DIM, 6, rows // 2, rows // 2), BF16)
     kernel = functools.partial(attend_kernel, which=which, part_of=part_of, again=bool(more))
     outs = out if more else [out, scores]
     return call(kernel, "attend", outs, [*projected, *more], 128 * rows * rows * hd, after, place)
 
 
-def head_terms_kernel(place, d_ref, wq_ref, wk_ref, wv_ref, out_ref, *, shard):
+def head_terms_kernel(place, d0_ref, d1_ref, wq_ref, wk_ref, wv_ref, out_ref, *, which, shard):
     width = out_ref.shape[1]
     step = min(width, 256)
     start = shard(place) * width
-    for i in range(width // step):
-        rows = pl.ds(pl.multiple_of(start + i * step, step), step)
-        out_ref[:, pl.ds(i * step, step)] = (
-            dot(d_ref[1], wq_ref[rows, :], NT)
-            + dot(d_ref[3], wk_ref[rows, :], NT)
-            + dot(d_ref[2], wv_ref[rows, :], NT)
-        )
-
-
-def head_terms(place, results, weights, shard, shards, after=()):
+
+    def fill(forward_ref, backward_ref):
+        for i in range(width // step):
+            rows = pl.ds(pl.multiple_of(start + i * step, step), step)
+            out_ref[:, pl.ds(i * step, step)] = (
+                dot(forward_ref[1], wq_ref[rows, :], NT)
+                + dot(backward_ref[1], wk_ref[rows, :], NT)
+                + dot(backward_ref[0], wv_ref[rows, :], NT)
+            )
+
+    chosen = which(place)
+    pl.when(chosen == 0)(lambda: fill(d0_ref, d1_ref))
+    pl.when(chosen != 0)(lambda: fill(d1_ref, d0_ref))
+
+
+def head_terms(place, which, first, second, weights, shard, shards, after=()):
     width, hd = weights[0].shape
-    rows = results.shape[1]
+    rows = first.shape[1]
     return call(
-        functools.partial(head_terms_kernel, shard=shard),
+        functools.partial(head_terms_kernel, which=which, shard=shard),
         "head_terms",
         shaped((rows, width // shards), F32),
-        [results, *weights],
+        [first, second, *weights],
         6 * rows * width // shards * hd,
         after,
         place,
@@ -315,23 +318,26 @@
     return (place.seq ^ (i // 2 % 2)) * 4 + (place.dp ^ (i % 2 * 2 + i // 4))
 
 
-def fill_tiles(place, xo_ref, d_ref, pair, side, blocks, scale, added, outs):
-    half = d_ref.shape[2] // 2
+def fill_tiles(place, xo_ref, read, half, pair, side, blocks, scale, added, outs):
     block = outs[0].shape[1]
     features = pl.ds(pl.multiple_of(side * half, half), half)
     for i, b in enumerate(blocks):
         columns = pl.ds(pl.multiple_of(column_block(place, b) * block, block), block)
         for t, rows in enumerate((1 - pair, 0)):
-            tile = dot(xo_ref[rows, :, columns], d_ref[2 * pair + t, :, features], TN) * scale
-            for read in added:
-                tile = tile + read(i, t)
+            tile = dot(xo_ref[rows, :, columns], read(t, features), TN) * scale
+            for more in added:
+                tile = tile + more(i, t)
             outs[i][t] = tile
+
+
+def reader(d_ref):
+    return (lambda t, features: d_ref[t, :, features]), d_ref.shape[2] // 2
 
 
 def other_core_kernel(place, xo_ref, d_ref, out_ref, *, early, slot, scale):
     outs = [out_ref.at[i] for i in range(4)]
     pair, side = place.seq ^ early, 1 - place.core ^ slot
-    fill_tiles(place, xo_ref, d_ref, pair, side, (4, 5, 6, 7), scale, (), outs)
+    fill_tiles(place, xo_ref, *reader(d_ref), pair, side, (4, 5, 6, 7), scale, (), outs)
 
 
 def other_core_both_kernel(place, xo_ref, d_ref, *out_refs, early, scale):
@@ -341,7 +347,7 @@
     sides = (1 - place.core, place.core)
     for t, rows in enumerate((1 - pair, 0)):
         features = [pl.ds(pl.multiple_of(side * half, half), half) for side in sides]
-        d = jnp.concatenate([d_ref[2 * pair + t, :, at] for at in features], axis=1)
+        d = jnp.concatenate([d_ref[t, :, at] for at in features], axis=1)
         for i in range(4):
             columns = pl.ds(pl.multiple_of(column_block(place, 4 + i) * block, block), block)
             tile = dot(xo_ref[rows, :, columns], d, TN) * scale
@@ -354,11 +360,11 @@
     blocks = (2 - side, 3)
     outs = [out_ref.at[i] for i in range(2)]
     added = (lambda i, t: far_ref[blocks[i], t],)
-    fill_tiles(place, xo_ref, d_ref, pair, side, blocks, scale, added, outs)
+    fill_tiles(place, xo_ref, *reader(d_ref), pair, side, blocks, scale, added, outs)
 
 
 def second_hop_kernel(
-    place, xo_ref, d_ref, far0_ref, far1_ref, over0_ref, over1_ref, keep_ref, send_ref,
+    place, xo_ref, d0_ref, d1_ref, far0_ref, far1_ref, over0_ref, over1_ref, keep_ref, send_ref,
     *, slot, scale,
 ):
     over = (over0_ref, over1_ref)
@@ -373,9 +379,14 @@
             lambda i, t: jnp.where(side == 0, far(1 - p, i, t), far(p, i, t)),
             lambda i, t: over[p][i, t],
         )
+        late = p ^ 1 - side
+
+        def read(t, features):
+            return jnp.where(late == 0, d0_ref[t, :, features], d1_ref[t, :, features])
+
         pair = place.seq ^ p ^ 1 - side
         outs = (keep_ref.at[p], send_ref.at[p])
-        fill_tiles(place, xo_ref, d_ref, pair, side, blocks, scale, added, outs)
+        fill_tiles(place, xo_ref, read, d0_ref.shape[2] // 2, pair, side, blocks, scale, added, outs)
 
 
 def put_side(place, slot, kept_ref, moved_ref, part_ref, out_refs, sems):
@@ -474,10 +485,10 @@
     if not planned:
         prefix = states_before(state, "seq", False)
         suffix = states_before(more[0], "seq", True)
-        d, scores = attend(place, lambda at: 0, lambda which: 0, projected)
-        d = attend(place, lambda at: 0, lambda which: 0, projected, (prefix, d, scores))
-        d = attend(place, lambda at: 1, lambda which: 0, projected, (suffix, d, scores))
-        terms = head_terms(place, d, weights, lambda at: 0, 1)
+        _, scores = attend(place, lambda at: 0, lambda which: 0, projected)
+        first = attend(place, lambda at: 0, lambda which: 0, projected, (prefix, scores))
+        second = attend(place, lambda at: 1, lambda which: 0, projected, (suffix, scores))
+        terms = head_terms(place, lambda at: 0, first, second, weights, lambda at: 0, 1)
 
         def reduced(rows, d):
             return lax.psum_scatter(
@@ -486,14 +497,16 @@
 
         return (
             lax.psum_scatter(terms, "head", scatter_dimension=1, tiled=True).astype(BF16)[None],
-            reduced(xo[0], d[1]),
-            reduced(xo[0], d[3]),
-            reduced(xo[0], d[2]),
-            reduced(xo[1], d[0]).T,
+            reduced(xo[0], first[1]),
+            reduced(xo[0], second[1]),
+            reduced(xo[0], second[0]),
+            reduced(xo[1], first[0]).T,
         )
 
     def term(flip, after):
-        return head_terms(place, d, weights, lambda at: at.head ^ flip, n_head, after)
+        return head_terms(
+            place, lambda at: at.seq, early, late, weights, lambda at: at.head ^ flip, n_head, after
+        )
 
     def hop(array, slot, second):
         pairs = []
@@ -521,14 +534,14 @@
     def first_hop(early, slot, after):
         kernel = functools.partial(first_hop_kernel, early=early, slot=slot, scale=scale)
         out = shaped((2, *tile), F32)
-        args = [xo, d, far[early][slot]]
+        args = [xo, results[early], far[early][slot]]
         array = call(kernel, "first_hop", out, args, 2 * flops, after, place)
         return array, hop(array, slot, 0)
 
     def second_hop(slot, over, after):
         kernel = functools.partial(second_hop_kernel, slot=slot, scale=scale)
         outs = [shaped((2, *tile), F32)] * 2
-        args = [xo, d, far[0][slot], far[1][slot], *over]
+        args = [xo, *results, far[0][slot], far[1][slot], *over]
         keep, leave = call(kernel, "second_hop", outs, args, 4 * flops, after, place)
         return keep, hop(leave, slot, 1)
 
@@ -536,8 +549,11 @@
     far = ([None, None], [None, None])
     at, far[0][0] = to_core(early, 0, 0, [])
     at, far[0][1] = to_core(early, 0, 1, [at])
-    d = attend(place, lambda at: 1 - at.seq, lambda which: 1 - which, projected, (state, early, scores), [at])
-    at, far[1][:] = both_to_core(d, 1, [])
+    late = attend(
+        place, lambda at: 1 - at.seq, lambda which: 1 - which, projected, (state, scores), [at]
+    )
+    results = (early, late)
+    at, far[1][:] = both_to_core(late, 1, [])
     at, over1 = first_hop(0, 0, [at])
     t3 = term(3, [at])
     t3_in = swap(t3, "head", 1)

time: 97.7 us -> 97.7 us (level)
  transfers between devices with their start and end apart: 14 -> 14, of which waited for: 6 -> 6; matrix products, arithmetic and copies ran while one was open for 0% -> 0% of each run, Pallas kernels for 19% -> 20%
where the time goes in v4:
time: 97.7 us; the launch traced here: 97.6 us
  waiting for transfers between devices  49.9 us (51%)
  Pallas kernels  25.9 us (27%)
  starting transfers between devices  20.7 us (21%)
  between operations  0.98 us (1%)
    ppermute x6, waiting for transfers between devices, hop(): return lax.ppermute(array, ('seq', 'dp'), pairs)  44.4 us
    pallas_call x17, Pallas kernels, call(): pl.pallas_call(body, out_shape=out_shape, in_specs=[IN_SMEM] * len(number...  18.2 us
    ppermute x8, starting transfers between devices, swap(): lax.ppermute(x, axis, [(i, i ^ bit) for i in range(lax.axis_size(axis))])  11.7 us
    ppermute x6, starting transfers between devices, hop(): return lax.ppermute(array, ('seq', 'dp'), pairs)  8.98 us
    ppermute x8, waiting for transfers between devices, swap(): lax.ppermute(x, axis, [(i, i ^ bit) for i in range(lax.axis_size(axis))])  5.56 us
    pallas_call x1, Pallas kernels, load(): pl.pallas_call(functools.partial(load_kernel, sizes=sizes, which=which),...  5.2 us
  transfers between devices with their start and end apart: 14, of which 6 were waited for; matrix products, arithmetic and copies ran while one was open for 0% of the time, Pallas kernels for 20%

profile of v4, /device:TPU:0, one launch (start us, length us, event | category | flops | bytes accessed | tf_op | source)
XLA Modules:
  0.0 97.6 jit_solution(7533326802000415329)
XLA Ops:
  0.6 5.2 %load.1 = (bf16[2,512,512]{2,1,0:T(8,128)(2,1)S(1)}, f32[4,128,128]{2,1,0:T(8,128)S(1)}, bf16[2,512,2048]{2,1,0:T(8,128)(2,1)S(1)}, bf16[2048,512]{1,0:T(8,128)(...) custom-call(s32[1]{0:T(128)} %bitcast.number_ref.refs_0_, ...), custom_call_target="tpu_custom_call" | custom-call | flops 2147483648 | bytes 14680064 | tf_op jit(solution)/shard_map/load/pallas_call | solution.py:139
  5.8 3.4 %collective-permute-start = (f32[4,128,128]{2,1,0:T(8,128)S(1)}, f32[4,128,128]{2,1,0:T(8,128)S(1)}, u32[]{:S(2)}, u32[]{:S(2)}) collective-permute-start(f32[4,128,128]{2,1,0:T(8,128)S(1)} %get-tuple-element.36), channel_id=1, source_target_pairs={{0,16},{16,0},{1,17},{17,1},{2,18},{18,2},{3,19},{19,3},{4,20},{20... | collective-permute-start | bytes 786440 | tf_op jit(solution)/shard_map/ppermute | solution.py:464
  9.2 2.3 %project.1.refs_2_ = bf16[2,512,512]{2,1,0:T(8,128)(2,1)S(1)} custom-call(s32[1]{0:T(128)} %bitcast.number_ref.refs_0_, bf16[2,512,2048]{2,1,0:T(8,128)(2,1)S(1)} %get-tuple-element.30.refs_1_, bf16[2048,512]{1,0:T(8,128)(2,1)S(1)} %get-tuple-element.31.refs_2_.refs_3_, bf16[2048,512]{1,0:T(8,128)(2,1)S(1)} %get-tuple-element.32.refs_3_.refs_4_, ...), custom_call_target="tpu_custom_call" | custom-call | flops 2147483648 | bytes 2097152 | tf_op jit(solution)/shard_map/project/pallas_call | solution.py:185
  11.6 2.5 %attend.2 = (bf16[2,512,512]{2,1,0:T(8,128)(2,1)S(1)}, bf16[4,6,256,256]{3,2,1,0:T(8,128)(2,1)S(1)}) custom-call(s32[1]{0:T(128)} %bitcast.number_ref.refs_0_, bf16[2,512,512]{2,1,0:T(8,128)(2,1)S(1)} %get-tuple-element.29.refs_1_, bf16[2,512,512]{2,1,0:T(8,128)(2,1)S(1)} %project.1.refs_2_), custom_call_target="tpu_custom_call" | custom-call | flops 17179869184 | bytes 2097152 | tf_op jit(solution)/shard_map/attend/pallas_call | solution.py:185
  14.0 0.8 other_core.2.refs_3_
  14.9 0.1 collective-permute-start.4
  15.0 0.9 other_core.3.refs_5_
  15.8 0.5 collective-permute-start.3
  16.4 0.0 collective-permute-done.refs_3_
  16.4 1.3 %attend.3.refs_2_.refs_3_ = bf16[2,512,512]{2,1,0:T(8,128)(2,1)S(1)} custom-call(s32[1]{0:T(128)} %bitcast.number_ref.refs_0_, bf16[2,512,512]{2,1,0:T(8,128)(2,1)S(1)} %get-tuple-element.29.refs_1_, bf16[2,512,512]{2,1,0:T(8,128)(2,1)S(1)} %project.1.refs_2_, f32[4,128,128]{2,1,0:T(8,128)S(1)} %collective-permute-done.refs_3_, ...), custom_call_target="tpu_custom_call" | custom-call | flops 17179869184 | bytes 2097152 | tf_op jit(solution)/shard_map/attend/pallas_call | solution.py:185
  17.7 1.3 %other_core_both.1 = (f32[4,2,256,256]{3,2,1,0:T(8,128)S(1)}, f32[4,2,256,256]{3,2,1,0:T(8,128)S(1)}) custom-call(s32[1]{0:T(128)} %bitcast.number_ref.refs_0_, bf16[2,512,2048]{2,1,0:T(8,128)(2,1)S(1)} %get-tuple-element.30.refs_1_, bf16[2,512,512]{2,1,0:T(8,128)(2,1)S(1)} %attend.3.refs_2_.refs_3_), custom_call_target="tpu_custom_call" | custom-call | flops 1073741824 | bytes 2097152 | tf_op jit(solution)/shard_map/other_core_both/pallas_call | solution.py:185
  19.0 0.1 collective-permute-start.2
  19.1 0.5 collective-permute-start.1
  19.6 0.0 collective-permute-done.4.refs_3_.refs_4_
  19.6 0.5 first_hop.4.refs_6_
  20.1 1.0 %collective-permute-start.5 = (f32[2,2,256,256]{3,2,1,0:T(8,128)S(1)}, f32[2,2,256,256]{3,2,1,0:T(8,128)S(1)}, u32[]{:S(2)}, u32[]{:S(2)}) collective-permute-start(f32[2,2,256,256]{3,2,1,0:T(8,128)S(1)} %first_hop.4.refs_6_), channel_id=1, source_target_pairs={{0,16},{1,3},{2,18},{3,1},{16,0},{17,19},{18,2},{19,17},{4,20},{5,... | collective-permute-start | bytes 3145736 | tf_op jit(solution)/shard_map/ppermute | solution.py:516
  21.1 1.0 %head_terms.4.refs_4_ = f32[512,512]{1,0:T(8,128)S(1)} custom-call(s32[1]{0:T(128)} %bitcast.number_ref.refs_0_, bf16[2,512,512]{2,1,0:T(8,128)(2,1)S(1)} %get-tuple-element.35.refs_2_.refs_1_, bf16[2,512,512]{2,1,0:T(8,128)(2,1)S(1)} %attend.3.refs_2_.refs_3_, bf16[2048,512]{1,0:T(8,128)(2,1)S(1)} %get-tuple-element.31.refs_2_.refs_3_, ...), custom_call_target="tpu_custom_call" | custom-call | flops 805306368 | bytes 2097152 | tf_op jit(solution)/shard_map/head_terms/pallas_call | solution.py:185
  22.1 1.7 %collective-permute-start.7 = (f32[512,512]{1,0:T(8,128)S(1)}, f32[512,512]{1,0:T(8,128)S(1)}, u32[]{:S(2)}, u32[]{:S(2)}) collective-permute-start(f32[512,512]{1,0:T(8,128)S(1)} %head_terms.4.refs_4_), channel_id=1, source_target_pairs={{0,4},{4,0},{8,12},{12,8},{1,5},{5,1},{9,13},{13,9},{2,6},{6,2},{1... | collective-permute-start | bytes 3145736 | tf_op jit(solution)/shard_map/ppermute | solution.py:464
  23.8 0.0 collective-permute-done.3.refs_3_.refs_4_
  23.8 0.5 first_hop.5.refs_4_
  24.4 1.6 %collective-permute-start.9 = (f32[2,2,256,256]{3,2,1,0:T(8,128)S(1)}, f32[2,2,256,256]{3,2,1,0:T(8,128)S(1)}, u32[]{:S(2)}, u32[]{:S(2)}) collective-permute-start(f32[2,2,256,256]{3,2,1,0:T(8,128)S(1)} %first_hop.5.refs_4_), channel_id=1, source_target_pairs={{0,2},{1,17},{2,0},{3,19},{16,18},{17,1},{18,16},{19,3},{4,6},{5,2... | collective-permute-start | bytes 3145736 | tf_op jit(solution)/shard_map/ppermute | solution.py:516
  26.0 0.0 collective-permute-done.2.refs_3_.refs_5_
  26.0 0.5 first_hop.6.refs_4_
  26.5 1.1 %collective-permute-start.11 = (f32[2,2,256,256]{3,2,1,0:T(8,128)S(1)}, f32[2,2,256,256]{3,2,1,0:T(8,128)S(1)}, u32[]{:S(2)}, u32[]{:S(2)}) collective-permute-start(f32[2,2,256,256]{3,2,1,0:T(8,128)S(1)} %first_hop.6.refs_4_), channel_id=1, source_target_pairs={{0,16},{1,3},{2,18},{3,1},{16,0},{17,19},{18,2},{19,17},{4,20},{5,... | collective-permute-start | bytes 3145736 | tf_op jit(solution)/shard_map/ppermute | solution.py:516
  27.6 0.5 collective-permute-done.1.refs_3_.refs_5_
  28.1 0.5 first_hop.7.refs_6_
  28.6 1.6 %collective-permute-start.10 = (f32[2,2,256,256]{3,2,1,0:T(8,128)S(1)}, f32[2,2,256,256]{3,2,1,0:T(8,128)S(1)}, u32[]{:S(2)}, u32[]{:S(2)}) collective-permute-start(f32[2,2,256,256]{3,2,1,0:T(8,128)S(1)} %first_hop.7.refs_6_), channel_id=1, source_target_pairs={{0,2},{1,17},{2,0},{3,19},{16,18},{17,1},{18,16},{19,3},{4,6},{5,2... | collective-permute-start | bytes 3145736 | tf_op jit(solution)/shard_map/ppermute | solution.py:516
  30.2 1.0 %head_terms.5.refs_6_.refs_0_ = f32[512,512]{1,0:T(8,128)S(1)} custom-call(s32[1]{0:T(128)} %bitcast.number_ref.refs_0_, bf16[2,512,512]{2,1,0:T(8,128)(2,1)S(1)} %get-tuple-element.35.refs_2_.refs_1_, bf16[2,512,512]{2,1,0:T(8,128)(2,1)S(1)} %attend.3.refs_2_.refs_3_, bf16[2048,512]{1,0:T(8,128)(2,1)S(1)} %get-tuple-element.31.refs_2_.refs_3_, ...), custom_call_target="tpu_custom_call" | custom-call | flops 805306368 | bytes 2097152 | tf_op jit(solution)/shard_map/head_terms/pallas_call | solution.py:185
  31.2 1.0 %head_terms.6.refs_6_.refs_0_ = f32[512,512]{1,0:T(8,128)S(1)} custom-call(s32[1]{0:T(128)} %bitcast.number_ref.refs_0_, bf16[2,512,512]{2,1,0:T(8,128)(2,1)S(1)} %get-tuple-element.35.refs_2_.refs_1_, bf16[2,512,512]{2,1,0:T(8,128)(2,1)S(1)} %attend.3.refs_2_.refs_3_, bf16[2048,512]{1,0:T(8,128)(2,1)S(1)} %get-tuple-element.31.refs_2_.refs_3_, ...), custom_call_target="tpu_custom_call" | custom-call | flops 805306368 | bytes 2097152 | tf_op jit(solution)/shard_map/head_terms/pallas_call | solution.py:185
  32.3 10.5 %collective-permute-done.5.refs_7_.refs_6_ = f32[2,2,256,256]{3,2,1,0:T(8,128)S(1)} collective-permute-done((f32[2,2,256,256]{3,2,1,0:T(8,128)S(1)}, f32[2,2,256,256]{3,2,1,0:T(8,128)S(1)}, u32[]{:S(2)}, u32[]{:S(2)}) %collective-permute-start.5) | collective-permute-done | bytes 1048608 | tf_op jit(solution)/shard_map/ppermute | solution.py:516
  42.8 1.0 %head_terms.7.refs_2_ = f32[512,512]{1,0:T(8,128)S(1)} custom-call(s32[1]{0:T(128)} %bitcast.number_ref.refs_0_, bf16[2,512,512]{2,1,0:T(8,128)(2,1)S(1)} %get-tuple-element.35.refs_2_.refs_1_, bf16[2,512,512]{2,1,0:T(8,128)(2,1)S(1)} %attend.3.refs_2_.refs_3_, bf16[2048,512]{1,0:T(8,128)(2,1)S(1)} %get-tuple-element.31.refs_2_.refs_3_, ...), custom_call_target="tpu_custom_call" | custom-call | flops 805306368 | bytes 2097152 | tf_op jit(solution)/shard_map/head_terms/pallas_call | solution.py:185
  43.8 2.8 %collective-permute-start.6 = (f32[512,512]{1,0:T(8,128)S(1)}, f32[512,512]{1,0:T(8,128)S(1)}, u32[]{:S(2)}, u32[]{:S(2)}) collective-permute-start(f32[512,512]{1,0:T(8,128)S(1)} %head_terms.7.refs_2_), channel_id=1, source_target_pairs={{0,4},{4,0},{8,12},{12,8},{1,5},{5,1},{9,13},{13,9},{2,6},{6,2},{1... | collective-permute-start | bytes 3145736 | tf_op jit(solution)/shard_map/ppermute | solution.py:464
  46.6 1.6 %collective-permute-done.7.refs_1_ = f32[512,512]{1,0:T(8,128)S(1)} collective-permute-done((f32[512,512]{1,0:T(8,128)S(1)}, f32[512,512]{1,0:T(8,128)S(1)}, u32[]{:S(2)}, u32[]{:S(2)}) %collective-permute-start.7) | collective-permute-done | bytes 1048608 | tf_op jit(solution)/shard_map/ppermute | solution.py:464
  48.2 0.2 add.9.refs_8_
  48.4 2.7 %collective-permute-start.8 = (f32[512,512]{1,0:T(8,128)S(1)}, f32[512,512]{1,0:T(8,128)S(1)}, u32[]{:S(2)}, u32[]{:S(2)}) collective-permute-start(f32[512,512]{1,0:T(8,128)S(1)} %add.9.refs_8_), channel_id=1, source_target_pairs={{0,8},{4,12},{8,0},{12,4},{1,9},{5,13},{9,1},{13,5},{2,10},{6,14},... | collective-permute-start | bytes 3145736 | tf_op jit(solution)/shard_map/ppermute | solution.py:464
  51.1 0.0 collective-permute-done.9.refs_9_.refs_6_
  51.1 14.2 %collective-permute-done.11.refs_7_ = f32[2,2,256,256]{3,2,1,0:T(8,128)S(1)} collective-permute-done((f32[2,2,256,256]{3,2,1,0:T(8,128)S(1)}, f32[2,2,256,256]{3,2,1,0:T(8,128)S(1)}, u32[]{:S(2)}, u32[]{:S(2)}) %collective-permute-start.11) | collective-permute-done | bytes 1048608 | tf_op jit(solution)/shard_map/ppermute | solution.py:516
  65.3 1.4 %second_hop.2 = (f32[2,2,256,256]{3,2,1,0:T(8,128)S(1)}, f32[2,2,256,256]{3,2,1,0:T(8,128)S(1)}) custom-call(s32[1]{0:T(128)} %bitcast.number_ref.refs_0_, bf16[2,512,2048]{2,1,0:T(8,128)(2,1)S(1)} %get-tuple-element.30.refs_1_, bf16[2,512,512]{2,1,0:T(8,128)(2,1)S(1)} %get-tuple-element.35.refs_2_.refs_1_, bf16[2,512,512]{2,1,0:T(8,128)(2,1)S(1)} %attend.3.refs_2_.refs_3_, ...), custom_call_target="tpu_custom_call" | custom-call | flops 536870912 | bytes 2097152 | tf_op jit(solution)/shard_map/second_hop/pallas_call | solution.py:185
  66.7 2.7 %collective-permute-start.13 = (f32[2,2,256,256]{3,2,1,0:T(8,128)S(1)}, f32[2,2,256,256]{3,2,1,0:T(8,128)S(1)}, u32[]{:S(2)}, u32[]{:S(2)}) collective-permute-start(f32[2,2,256,256]{3,2,1,0:T(8,128)S(1)} %get-tuple-element.43), channel_id=1, source_target_pairs={{0,2},{1,17},{2,0},{3,19},{16,18},{17,1},{18,16},{19,3},{4,6},{5,2... | collective-permute-start | bytes 3145736 | tf_op jit(solution)/shard_map/ppermute | solution.py:516
  69.4 0.0 collective-permute-done.10.refs_7_
  69.4 1.4 %second_hop.3 = (f32[2,2,256,256]{3,2,1,0:T(8,128)S(1)}, f32[2,2,256,256]{3,2,1,0:T(8,128)S(1)}) custom-call(s32[1]{0:T(128)} %bitcast.number_ref.refs_0_, bf16[2,512,2048]{2,1,0:T(8,128)(2,1)S(1)} %get-tuple-element.30.refs_1_, bf16[2,512,512]{2,1,0:T(8,128)(2,1)S(1)} %get-tuple-element.35.refs_2_.refs_1_, bf16[2,512,512]{2,1,0:T(8,128)(2,1)S(1)} %attend.3.refs_2_.refs_3_, ...), custom_call_target="tpu_custom_call" | custom-call | flops 536870912 | bytes 2097152 | tf_op jit(solution)/shard_map/second_hop/pallas_call | solution.py:185
  70.7 1.0 %collective-permute-start.12 = (f32[2,2,256,256]{3,2,1,0:T(8,128)S(1)}, f32[2,2,256,256]{3,2,1,0:T(8,128)S(1)}, u32[]{:S(2)}, u32[]{:S(2)}) collective-permute-start(f32[2,2,256,256]{3,2,1,0:T(8,128)S(1)} %get-tuple-element.42), channel_id=1, source_target_pairs={{0,16},{1,3},{2,18},{3,1},{16,0},{17,19},{18,2},{19,17},{4,20},{5,... | collective-permute-start | bytes 3145736 | tf_op jit(solution)/shard_map/ppermute | solution.py:516
  71.8 19.6 %collective-permute-done.13.moved_ref = f32[2,2,256,256]{3,2,1,0:T(8,128)S(1)} collective-permute-done((f32[2,2,256,256]{3,2,1,0:T(8,128)S(1)}, f32[2,2,256,256]{3,2,1,0:T(8,128)S(1)}, u32[]{:S(2)}, u32[]{:S(2)}) %collective-permute-start.13) | collective-permute-done | bytes 1048608 | tf_op jit(solution)/shard_map/ppermute | solution.py:516
  91.4 1.0 %settle.1 = (f32[256,512]{1,0:T(8,128)}, f32[256,512]{1,0:T(8,128)}, f32[256,512]{1,0:T(8,128)}, f32[512,256]{1,0:T(8,128)}) custom-call(s32[1]{0:T(128)} %bitcast.number_ref.refs_0_, f32[2,2,256,256]{3,2,1,0:T(8,128)S(1)} %get-tuple-element.40.refs_8_.kept_ref, f32[2,2,256,256]{3,2,1,0:T(8,128)S(1)} %collective-permute-done.13.moved_ref, ...), custom_call_target="tpu_custom_call" | custom-call | bytes 2097152 | tf_op jit(solution)/shard_map/settle/pallas_call | solution.py:432
  92.5 3.5 %collective-permute-done.8.refs_2_ = f32[512,512]{1,0:T(8,128)S(1)} collective-permute-done((f32[512,512]{1,0:T(8,128)S(1)}, f32[512,512]{1,0:T(8,128)S(1)}, u32[]{:S(2)}, u32[]{:S(2)}) %collective-permute-start.8) | collective-permute-done | bytes 1048608 | tf_op jit(solution)/shard_map/ppermute | solution.py:464
  95.9 0.0 collective-permute-done.6.refs_1_
  95.9 0.0 collective-permute-done.12.refs_4_
  95.9 1.5 %finish.1 = (bf16[512,512]{1,0:T(8,128)(2,1)}, f32[256,512]{1,0:T(8,128)}, f32[256,512]{1,0:T(8,128)}, f32[256,512]{1,0:T(8,128)}, f32[512,256]{1,0:T(8,128)}) custom-call(s32[1]{0:T(128)} %bitcast.number_ref.refs_0_, f32[512,512]{1,0:T(8,128)S(1)} %head_terms.6.refs_6_.refs_0_, ...), custom_call_target="tpu_custom_call", output_to_operand_aliasing={{1}: (6, {}), {2}: (7, {}), {3}: (8, {}), {4}: (9, {})} | custom-call | bytes 2097152 | tf_op jit(solution)/shard_map/finish/pallas_call | solution.py:442
Async XLA Ops:
  5.8 10.5 %collective-permute-start = (f32[4,128,128]{2,1,0:T(8,128)S(1)}, f32[4,128,128]{2,1,0:T(8,128)S(1)}, u32[]{:S(2)}, u32[]{:S(2)}) collective-permute-start(f32[4,128,128]{2,1,0:T(8,128)S(1)} %get-tuple-element.36), channel_id=1, source_target_pairs={{0,16},{16,0},{1,17},{17,1},{2,18},{18,2},{3,19},{19,3},{4,20},{20... | collective-permute-start | bytes 786440 | tf_op jit(solution)/shard_map/ppermute | solution.py:464
  14.9 4.7 %collective-permute-start.4 = (f32[4,2,256,256]{3,2,1,0:T(8,128)S(1)}, f32[4,2,256,256]{3,2,1,0:T(8,128)S(1)}, u32[]{:S(2)}, u32[]{:S(2)}) collective-permute-start(f32[4,2,256,256]{3,2,1,0:T(8,128)S(1)} %other_core.2.refs_3_), channel_id=1, source_target_pairs={{0,1},{1,0},{2,3},{3,2},{4,5},{5,4},{6,7},{7,6},{8,9},{9,8},{10,11... | collective-permute-start | bytes 6291464 | tf_op jit(solution)/shard_map/ppermute | solution.py:464
  15.8 8.0 %collective-permute-start.3 = (f32[4,2,256,256]{3,2,1,0:T(8,128)S(1)}, f32[4,2,256,256]{3,2,1,0:T(8,128)S(1)}, u32[]{:S(2)}, u32[]{:S(2)}) collective-permute-start(f32[4,2,256,256]{3,2,1,0:T(8,128)S(1)} %other_core.3.refs_5_), channel_id=1, source_target_pairs={{0,1},{1,0},{2,3},{3,2},{4,5},{5,4},{6,7},{7,6},{8,9},{9,8},{10,11... | collective-permute-start | bytes 6291464 | tf_op jit(solution)/shard_map/ppermute | solution.py:464
  19.0 7.0 %collective-permute-start.2 = (f32[4,2,256,256]{3,2,1,0:T(8,128)S(1)}, f32[4,2,256,256]{3,2,1,0:T(8,128)S(1)}, u32[]{:S(2)}, u32[]{:S(2)}) collective-permute-start(f32[4,2,256,256]{3,2,1,0:T(8,128)S(1)} %get-tuple-element.39.refs_4_), channel_id=1, source_target_pairs={{0,1},{1,0},{2,3},{3,2},{4,5},{5,4},{6,7},{7,6},{8,9},{9,8},{10,11... | collective-permute-start | bytes 6291464 | tf_op jit(solution)/shard_map/ppermute | solution.py:464
  19.1 9.0 %collective-permute-start.1 = (f32[4,2,256,256]{3,2,1,0:T(8,128)S(1)}, f32[4,2,256,256]{3,2,1,0:T(8,128)S(1)}, u32[]{:S(2)}, u32[]{:S(2)}) collective-permute-start(f32[4,2,256,256]{3,2,1,0:T(8,128)S(1)} %get-tuple-element.38), channel_id=1, source_target_pairs={{0,1},{1,0},{2,3},{3,2},{4,5},{5,4},{6,7},{7,6},{8,9},{9,8},{10,11... | collective-permute-start | bytes 6291464 | tf_op jit(solution)/shard_map/ppermute | solution.py:464
  20.1 22.7 %collective-permute-start.5 = (f32[2,2,256,256]{3,2,1,0:T(8,128)S(1)}, f32[2,2,256,256]{3,2,1,0:T(8,128)S(1)}, u32[]{:S(2)}, u32[]{:S(2)}) collective-permute-start(f32[2,2,256,256]{3,2,1,0:T(8,128)S(1)} %first_hop.4.refs_6_), channel_id=1, source_target_pairs={{0,16},{1,3},{2,18},{3,1},{16,0},{17,19},{18,2},{19,17},{4,20},{5,... | collective-permute-start | bytes 3145736 | tf_op jit(solution)/shard_map/ppermute | solution.py:516
  22.1 26.1 %collective-permute-start.7 = (f32[512,512]{1,0:T(8,128)S(1)}, f32[512,512]{1,0:T(8,128)S(1)}, u32[]{:S(2)}, u32[]{:S(2)}) collective-permute-start(f32[512,512]{1,0:T(8,128)S(1)} %head_terms.4.refs_4_), channel_id=1, source_target_pairs={{0,4},{4,0},{8,12},{12,8},{1,5},{5,1},{9,13},{13,9},{2,6},{6,2},{1... | collective-permute-start | bytes 3145736 | tf_op jit(solution)/shard_map/ppermute | solution.py:464
  24.4 26.7 %collective-permute-start.9 = (f32[2,2,256,256]{3,2,1,0:T(8,128)S(1)}, f32[2,2,256,256]{3,2,1,0:T(8,128)S(1)}, u32[]{:S(2)}, u32[]{:S(2)}) collective-permute-start(f32[2,2,256,256]{3,2,1,0:T(8,128)S(1)} %first_hop.5.refs_4_), channel_id=1, source_target_pairs={{0,2},{1,17},{2,0},{3,19},{16,18},{17,1},{18,16},{19,3},{4,6},{5,2... | collective-permute-start | bytes 3145736 | tf_op jit(solution)/shard_map/ppermute | solution.py:516
  26.5 38.7 %collective-permute-start.11 = (f32[2,2,256,256]{3,2,1,0:T(8,128)S(1)}, f32[2,2,256,256]{3,2,1,0:T(8,128)S(1)}, u32[]{:S(2)}, u32[]{:S(2)}) collective-permute-start(f32[2,2,256,256]{3,2,1,0:T(8,128)S(1)} %first_hop.6.refs_4_), channel_id=1, source_target_pairs={{0,16},{1,3},{2,18},{3,1},{16,0},{17,19},{18,2},{19,17},{4,20},{5,... | collective-permute-start | bytes 3145736 | tf_op jit(solution)/shard_map/ppermute | solution.py:516
  28.6 40.7 %collective-permute-start.10 = (f32[2,2,256,256]{3,2,1,0:T(8,128)S(1)}, f32[2,2,256,256]{3,2,1,0:T(8,128)S(1)}, u32[]{:S(2)}, u32[]{:S(2)}) collective-permute-start(f32[2,2,256,256]{3,2,1,0:T(8,128)S(1)} %first_hop.7.refs_6_), channel_id=1, source_target_pairs={{0,2},{1,17},{2,0},{3,19},{16,18},{17,1},{18,16},{19,3},{4,6},{5,2... | collective-permute-start | bytes 3145736 | tf_op jit(solution)/shard_map/ppermute | solution.py:516
  43.8 52.1 %collective-permute-start.6 = (f32[512,512]{1,0:T(8,128)S(1)}, f32[512,512]{1,0:T(8,128)S(1)}, u32[]{:S(2)}, u32[]{:S(2)}) collective-permute-start(f32[512,512]{1,0:T(8,128)S(1)} %head_terms.7.refs_2_), channel_id=1, source_target_pairs={{0,4},{4,0},{8,12},{12,8},{1,5},{5,1},{9,13},{13,9},{2,6},{6,2},{1... | collective-permute-start | bytes 3145736 | tf_op jit(solution)/shard_map/ppermute | solution.py:464
  48.4 47.6 %collective-permute-start.8 = (f32[512,512]{1,0:T(8,128)S(1)}, f32[512,512]{1,0:T(8,128)S(1)}, u32[]{:S(2)}, u32[]{:S(2)}) collective-permute-start(f32[512,512]{1,0:T(8,128)S(1)} %add.9.refs_8_), channel_id=1, source_target_pairs={{0,8},{4,12},{8,0},{12,4},{1,9},{5,13},{9,1},{13,5},{2,10},{6,14},... | collective-permute-start | bytes 3145736 | tf_op jit(solution)/shard_map/ppermute | solution.py:464
  66.7 24.7 %collective-permute-start.13 = (f32[2,2,256,256]{3,2,1,0:T(8,128)S(1)}, f32[2,2,256,256]{3,2,1,0:T(8,128)S(1)}, u32[]{:S(2)}, u32[]{:S(2)}) collective-permute-start(f32[2,2,256,256]{3,2,1,0:T(8,128)S(1)} %get-tuple-element.43), channel_id=1, source_target_pairs={{0,2},{1,17},{2,0},{3,19},{16,18},{17,1},{18,16},{19,3},{4,6},{5,2... | collective-permute-start | bytes 3145736 | tf_op jit(solution)/shard_map/ppermute | solution.py:516
  70.7 25.2 %collective-permute-start.12 = (f32[2,2,256,256]{3,2,1,0:T(8,128)S(1)}, f32[2,2,256,256]{3,2,1,0:T(8,128)S(1)}, u32[]{:S(2)}, u32[]{:S(2)}) collective-permute-start(f32[2,2,256,256]{3,2,1,0:T(8,128)S(1)} %get-tuple-element.42), channel_id=1, source_target_pairs={{0,16},{1,3},{2,18},{3,1},{16,0},{17,19},{18,2},{19,17},{4,20},{5,... | collective-permute-start | bytes 3145736 | tf_op jit(solution)/shard_map/ppermute | solution.py:516

commit v5 on v3

--- a/solution.py
+++ b/solution.py
@@ -404,12 +404,15 @@
     line, (kept_ref, moved_ref) = refs[:3], refs[3:5]
     input_out, out_refs, (part_ref, input_ref, sems) = refs[9], refs[10:14], refs[14:]
     place = Place(number_ref[0], sizes)
-    input_ref[...] = (line[0][...] + line[1][...] + line[2][...]).astype(BF16)
-    last = pltpu.make_async_copy(input_ref, input_out, sems.at[4])
-    last.start()
-    for c in put_side(place, 1, kept_ref, moved_ref, part_ref, out_refs, sems):
+    copies = put_side(place, 1, kept_ref, moved_ref, part_ref, out_refs, sems)
+    rows = input_ref.shape[0] // 2
+    for i in (0, 1):
+        at = pl.ds(i * rows, rows)
+        input_ref[at] = (line[0][at] + line[1][at] + line[2][at]).astype(BF16)
+        copies.append(pltpu.make_async_copy(input_ref.at[at], input_out.at[at], sems.at[4 + i]))
+        copies[-1].start()
+    for c in copies:
         c.wait()
-    last.wait()
 
 
 def finish(place, line, kept, moved):
@@ -434,7 +437,7 @@
         in_specs=[IN_SMEM] + [IN_VMEM] * 5 + [ANYWHERE] * 4,
         out_specs=[ANYWHERE] * 5,
         input_output_aliases={6 + i: 1 + i for i in range(4)},
-        scratch_shapes=[parts, pltpu.VMEM(line[0].shape, BF16), pltpu.SemaphoreType.DMA((5,))],
+        scratch_shapes=[parts, pltpu.VMEM(line[0].shape, BF16), pltpu.SemaphoreType.DMA((6,))],
         compiler_params=params(16),
         cost_estimate=cost(0, 2 * MIB),
         name="finish",

time: 97.7 us -> 97.5 us (level)
  no operation moved by 1% of the time
where the time goes in v5:
time: 97.5 us; the launch traced here: 97.4 us
  waiting for transfers between devices  50.4 us (52%)
  Pallas kernels  25.4 us (26%)
  starting transfers between devices  20.6 us (21%)
    ppermute x6, waiting for transfers between devices, hop(): return lax.ppermute(array, ('seq', 'dp'), pairs)  44.7 us
    pallas_call x17, Pallas kernels, call(): pl.pallas_call(body, out_shape=out_shape, in_specs=[IN_SMEM] * len(number...  17.9 us
    ppermute x8, starting transfers between devices, swap(): lax.ppermute(x, axis, [(i, i ^ bit) for i in range(lax.axis_size(axis))])  11.7 us
    ppermute x6, starting transfers between devices, hop(): return lax.ppermute(array, ('seq', 'dp'), pairs)  8.88 us
    ppermute x8, waiting for transfers between devices, swap(): lax.ppermute(x, axis, [(i, i ^ bit) for i in range(lax.axis_size(axis))])  5.75 us
    pallas_call x1, Pallas kernels, load(): pl.pallas_call(functools.partial(load_kernel, sizes=sizes, which=which),...  5.2 us
  transfers between devices with their start and end apart: 14, of which 6 were waited for; matrix products, arithmetic and copies ran while one was open for 0% of the time, Pallas kernels for 19%

profile of v5, /device:TPU:0, one launch (start us, length us, event | category | flops | bytes accessed | tf_op | source)
XLA Modules:
  0.0 97.4 jit_solution(18292664675151556915)
XLA Ops:
  0.6 5.2 %load.1 = (bf16[2,512,512]{2,1,0:T(8,128)(2,1)S(1)}, f32[4,128,128]{2,1,0:T(8,128)S(1)}, bf16[2,512,2048]{2,1,0:T(8,128)(2,1)S(1)}, bf16[2048,512]{1,0:T(8,128)(...) custom-call(s32[1]{0:T(128)} %bitcast.number_ref.refs_0_, ...), custom_call_target="tpu_custom_call" | custom-call | flops 2147483648 | bytes 14680064 | tf_op jit(solution)/shard_map/load/pallas_call | solution.py:139
  5.8 3.4 %collective-permute-start = (f32[4,128,128]{2,1,0:T(8,128)S(1)}, f32[4,128,128]{2,1,0:T(8,128)S(1)}, u32[]{:S(2)}, u32[]{:S(2)}) collective-permute-start(f32[4,128,128]{2,1,0:T(8,128)S(1)} %get-tuple-element.35), channel_id=1, source_target_pairs={{0,16},{16,0},{1,17},{17,1},{2,18},{18,2},{3,19},{19,3},{4,20},{20... | collective-permute-start | bytes 786440 | tf_op jit(solution)/shard_map/ppermute | solution.py:456
  9.2 2.3 %project.1.refs_2_ = bf16[2,512,512]{2,1,0:T(8,128)(2,1)S(1)} custom-call(s32[1]{0:T(128)} %bitcast.number_ref.refs_0_, bf16[2,512,2048]{2,1,0:T(8,128)(2,1)S(1)} %get-tuple-element.30.refs_1_, bf16[2048,512]{1,0:T(8,128)(2,1)S(1)} %get-tuple-element.31.refs_2_, bf16[2048,512]{1,0:T(8,128)(2,1)S(1)} %get-tuple-element.32.refs_3_, ...), custom_call_target="tpu_custom_call" | custom-call | flops 2147483648 | bytes 2097152 | tf_op jit(solution)/shard_map/project/pallas_call | solution.py:185
  11.6 2.5 %attend.2 = (bf16[4,512,512]{2,1,0:T(8,128)(2,1)S(1)}, bf16[4,6,256,256]{3,2,1,0:T(8,128)(2,1)S(1)}) custom-call(s32[1]{0:T(128)} %bitcast.number_ref.refs_0_, bf16[2,512,512]{2,1,0:T(8,128)(2,1)S(1)} %get-tuple-element.29.refs_1_, bf16[2,512,512]{2,1,0:T(8,128)(2,1)S(1)} %project.1.refs_2_), custom_call_target="tpu_custom_call" | custom-call | flops 17179869184 | bytes 2097152 | tf_op jit(solution)/shard_map/attend/pallas_call | solution.py:185
  14.0 0.8 other_core.2.refs_3_
  14.9 0.1 collective-permute-start.4
  15.0 0.9 other_core.3.refs_6_
  15.8 0.5 collective-permute-start.3
  16.4 0.0 collective-permute-done.refs_3_
  16.4 1.4 %attend.3.refs_2_.refs_1_ = bf16[4,512,512]{2,1,0:T(8,128)(2,1)S(1)} custom-call(s32[1]{0:T(128)} %bitcast.number_ref.refs_0_, bf16[2,512,512]{2,1,0:T(8,128)(2,1)S(1)} %get-tuple-element.29.refs_1_, bf16[2,512,512]{2,1,0:T(8,128)(2,1)S(1)} %project.1.refs_2_, f32[4,128,128]{2,1,0:T(8,128)S(1)} %collective-permute-done.refs_3_, ...), custom_call_target="tpu_custom_call" | custom-call | flops 17179869184 | bytes 2097152 | tf_op jit(solution)/shard_map/attend/pallas_call | solution.py:185
  17.8 1.3 %other_core_both.1 = (f32[4,2,256,256]{3,2,1,0:T(8,128)S(1)}, f32[4,2,256,256]{3,2,1,0:T(8,128)S(1)}) custom-call(s32[1]{0:T(128)} %bitcast.number_ref.refs_0_, bf16[2,512,2048]{2,1,0:T(8,128)(2,1)S(1)} %get-tuple-element.30.refs_1_, bf16[4,512,512]{2,1,0:T(8,128)(2,1)S(1)} %attend.3.refs_2_.refs_1_), custom_call_target="tpu_custom_call" | custom-call | flops 1073741824 | bytes 2097152 | tf_op jit(solution)/shard_map/other_core_both/pallas_call | solution.py:185
  19.1 0.1 collective-permute-start.2
  19.2 0.5 collective-permute-start.1
  19.6 0.0 collective-permute-done.4.refs_3_
  19.7 0.5 first_hop.4.refs_5_
  20.2 1.0 %collective-permute-start.5 = (f32[2,2,256,256]{3,2,1,0:T(8,128)S(1)}, f32[2,2,256,256]{3,2,1,0:T(8,128)S(1)}, u32[]{:S(2)}, u32[]{:S(2)}) collective-permute-start(f32[2,2,256,256]{3,2,1,0:T(8,128)S(1)} %first_hop.4.refs_5_), channel_id=1, source_target_pairs={{0,16},{1,3},{2,18},{3,1},{16,0},{17,19},{18,2},{19,17},{4,20},{5,... | collective-permute-start | bytes 3145736 | tf_op jit(solution)/shard_map/ppermute | solution.py:506
  21.2 1.0 %head_terms.4.refs_4_ = f32[512,512]{1,0:T(8,128)S(1)} custom-call(s32[1]{0:T(128)} %bitcast.number_ref.refs_0_, bf16[4,512,512]{2,1,0:T(8,128)(2,1)S(1)} %attend.3.refs_2_.refs_1_, bf16[2048,512]{1,0:T(8,128)(2,1)S(1)} %get-tuple-element.31.refs_2_, bf16[2048,512]{1,0:T(8,128)(2,1)S(1)} %get-tuple-element.32.refs_3_, ...), custom_call_target="tpu_custom_call" | custom-call | flops 805306368 | bytes 2097152 | tf_op jit(solution)/shard_map/head_terms/pallas_call | solution.py:185
  22.2 1.7 %collective-permute-start.7 = (f32[512,512]{1,0:T(8,128)S(1)}, f32[512,512]{1,0:T(8,128)S(1)}, u32[]{:S(2)}, u32[]{:S(2)}) collective-permute-start(f32[512,512]{1,0:T(8,128)S(1)} %head_terms.4.refs_4_), channel_id=1, source_target_pairs={{0,4},{4,0},{8,12},{12,8},{1,5},{5,1},{9,13},{13,9},{2,6},{6,2},{1... | collective-permute-start | bytes 3145736 | tf_op jit(solution)/shard_map/ppermute | solution.py:456
  23.9 0.0 collective-permute-done.3.refs_3_
  23.9 0.5 first_hop.5.refs_4_
  24.4 1.6 %collective-permute-start.9 = (f32[2,2,256,256]{3,2,1,0:T(8,128)S(1)}, f32[2,2,256,256]{3,2,1,0:T(8,128)S(1)}, u32[]{:S(2)}, u32[]{:S(2)}) collective-permute-start(f32[2,2,256,256]{3,2,1,0:T(8,128)S(1)} %first_hop.5.refs_4_), channel_id=1, source_target_pairs={{0,2},{1,17},{2,0},{3,19},{16,18},{17,1},{18,16},{19,3},{4,6},{5,2... | collective-permute-start | bytes 3145736 | tf_op jit(solution)/shard_map/ppermute | solution.py:506
  26.0 0.0 collective-permute-done.2.refs_3_.refs_4_
  26.0 0.5 first_hop.6.refs_4_
  26.6 1.1 %collective-permute-start.11 = (f32[2,2,256,256]{3,2,1,0:T(8,128)S(1)}, f32[2,2,256,256]{3,2,1,0:T(8,128)S(1)}, u32[]{:S(2)}, u32[]{:S(2)}) collective-permute-start(f32[2,2,256,256]{3,2,1,0:T(8,128)S(1)} %first_hop.6.refs_4_), channel_id=1, source_target_pairs={{0,16},{1,3},{2,18},{3,1},{16,0},{17,19},{18,2},{19,17},{4,20},{5,... | collective-permute-start | bytes 3145736 | tf_op jit(solution)/shard_map/ppermute | solution.py:506
  27.7 0.4 collective-permute-done.1.refs_3_.refs_4_
  28.1 0.5 first_hop.7.refs_5_
  28.6 1.6 %collective-permute-start.10 = (f32[2,2,256,256]{3,2,1,0:T(8,128)S(1)}, f32[2,2,256,256]{3,2,1,0:T(8,128)S(1)}, u32[]{:S(2)}, u32[]{:S(2)}) collective-permute-start(f32[2,2,256,256]{3,2,1,0:T(8,128)S(1)} %first_hop.7.refs_5_), channel_id=1, source_target_pairs={{0,2},{1,17},{2,0},{3,19},{16,18},{17,1},{18,16},{19,3},{4,6},{5,2... | collective-permute-start | bytes 3145736 | tf_op jit(solution)/shard_map/ppermute | solution.py:506
  30.2 1.0 %head_terms.5.refs_5_.refs_0_ = f32[512,512]{1,0:T(8,128)S(1)} custom-call(s32[1]{0:T(128)} %bitcast.number_ref.refs_0_, bf16[4,512,512]{2,1,0:T(8,128)(2,1)S(1)} %attend.3.refs_2_.refs_1_, bf16[2048,512]{1,0:T(8,128)(2,1)S(1)} %get-tuple-element.31.refs_2_, bf16[2048,512]{1,0:T(8,128)(2,1)S(1)} %get-tuple-element.32.refs_3_, ...), custom_call_target="tpu_custom_call" | custom-call | flops 805306368 | bytes 2097152 | tf_op jit(solution)/shard_map/head_terms/pallas_call | solution.py:185
  31.2 1.0 %head_terms.6.refs_5_.refs_0_ = f32[512,512]{1,0:T(8,128)S(1)} custom-call(s32[1]{0:T(128)} %bitcast.number_ref.refs_0_, bf16[4,512,512]{2,1,0:T(8,128)(2,1)S(1)} %attend.3.refs_2_.refs_1_, bf16[2048,512]{1,0:T(8,128)(2,1)S(1)} %get-tuple-element.31.refs_2_, bf16[2048,512]{1,0:T(8,128)(2,1)S(1)} %get-tuple-element.32.refs_3_, ...), custom_call_target="tpu_custom_call" | custom-call | flops 805306368 | bytes 2097152 | tf_op jit(solution)/shard_map/head_terms/pallas_call | solution.py:185
  32.3 10.6 %collective-permute-done.5.refs_6_.refs_5_ = f32[2,2,256,256]{3,2,1,0:T(8,128)S(1)} collective-permute-done((f32[2,2,256,256]{3,2,1,0:T(8,128)S(1)}, f32[2,2,256,256]{3,2,1,0:T(8,128)S(1)}, u32[]{:S(2)}, u32[]{:S(2)}) %collective-permute-start.5) | collective-permute-done | bytes 1048608 | tf_op jit(solution)/shard_map/ppermute | solution.py:506
  42.9 1.0 %head_terms.7.refs_2_ = f32[512,512]{1,0:T(8,128)S(1)} custom-call(s32[1]{0:T(128)} %bitcast.number_ref.refs_0_, bf16[4,512,512]{2,1,0:T(8,128)(2,1)S(1)} %attend.3.refs_2_.refs_1_, bf16[2048,512]{1,0:T(8,128)(2,1)S(1)} %get-tuple-element.31.refs_2_, bf16[2048,512]{1,0:T(8,128)(2,1)S(1)} %get-tuple-element.32.refs_3_, ...), custom_call_target="tpu_custom_call" | custom-call | flops 805306368 | bytes 2097152 | tf_op jit(solution)/shard_map/head_terms/pallas_call | solution.py:185
  43.9 2.8 %collective-permute-start.6 = (f32[512,512]{1,0:T(8,128)S(1)}, f32[512,512]{1,0:T(8,128)S(1)}, u32[]{:S(2)}, u32[]{:S(2)}) collective-permute-start(f32[512,512]{1,0:T(8,128)S(1)} %head_terms.7.refs_2_), channel_id=1, source_target_pairs={{0,4},{4,0},{8,12},{12,8},{1,5},{5,1},{9,13},{13,9},{2,6},{6,2},{1... | collective-permute-start | bytes 3145736 | tf_op jit(solution)/shard_map/ppermute | solution.py:456
  46.7 1.6 %collective-permute-done.7.refs_1_ = f32[512,512]{1,0:T(8,128)S(1)} collective-permute-done((f32[512,512]{1,0:T(8,128)S(1)}, f32[512,512]{1,0:T(8,128)S(1)}, u32[]{:S(2)}, u32[]{:S(2)}) %collective-permute-start.7) | collective-permute-done | bytes 1048608 | tf_op jit(solution)/shard_map/ppermute | solution.py:456
  48.3 0.2 add.9.refs_7_
  48.4 2.7 %collective-permute-start.8 = (f32[512,512]{1,0:T(8,128)S(1)}, f32[512,512]{1,0:T(8,128)S(1)}, u32[]{:S(2)}, u32[]{:S(2)}) collective-permute-start(f32[512,512]{1,0:T(8,128)S(1)} %add.9.refs_7_), channel_id=1, source_target_pairs={{0,8},{4,12},{8,0},{12,4},{1,9},{5,13},{9,1},{13,5},{2,10},{6,14},... | collective-permute-start | bytes 3145736 | tf_op jit(solution)/shard_map/ppermute | solution.py:456
  51.1 0.0 collective-permute-done.9.refs_8_.refs_5_
  51.1 14.3 %collective-permute-done.11.refs_6_ = f32[2,2,256,256]{3,2,1,0:T(8,128)S(1)} collective-permute-done((f32[2,2,256,256]{3,2,1,0:T(8,128)S(1)}, f32[2,2,256,256]{3,2,1,0:T(8,128)S(1)}, u32[]{:S(2)}, u32[]{:S(2)}) %collective-permute-start.11) | collective-permute-done | bytes 1048608 | tf_op jit(solution)/shard_map/ppermute | solution.py:506
  65.4 1.2 %second_hop.2 = (f32[2,2,256,256]{3,2,1,0:T(8,128)S(1)}, f32[2,2,256,256]{3,2,1,0:T(8,128)S(1)}) custom-call(s32[1]{0:T(128)} %bitcast.number_ref.refs_0_, bf16[2,512,2048]{2,1,0:T(8,128)(2,1)S(1)} %get-tuple-element.30.refs_1_, bf16[4,512,512]{2,1,0:T(8,128)(2,1)S(1)} %attend.3.refs_2_.refs_1_, f32[4,2,256,256]{3,2,1,0:T(8,128)S(1)} %collective-permute-done.4.refs_3_, ...), custom_call_target="tpu_custom_call" | custom-call | flops 536870912 | bytes 2097152 | tf_op jit(solution)/shard_map/second_hop/pallas_call | solution.py:185
  66.6 2.6 %collective-permute-start.13 = (f32[2,2,256,256]{3,2,1,0:T(8,128)S(1)}, f32[2,2,256,256]{3,2,1,0:T(8,128)S(1)}, u32[]{:S(2)}, u32[]{:S(2)}) collective-permute-start(f32[2,2,256,256]{3,2,1,0:T(8,128)S(1)} %get-tuple-element.43), channel_id=1, source_target_pairs={{0,2},{1,17},{2,0},{3,19},{16,18},{17,1},{18,16},{19,3},{4,6},{5,2... | collective-permute-start | bytes 3145736 | tf_op jit(solution)/shard_map/ppermute | solution.py:506
  69.2 0.0 collective-permute-done.10.refs_6_
  69.2 1.2 %second_hop.3 = (f32[2,2,256,256]{3,2,1,0:T(8,128)S(1)}, f32[2,2,256,256]{3,2,1,0:T(8,128)S(1)}) custom-call(s32[1]{0:T(128)} %bitcast.number_ref.refs_0_, bf16[2,512,2048]{2,1,0:T(8,128)(2,1)S(1)} %get-tuple-element.30.refs_1_, bf16[4,512,512]{2,1,0:T(8,128)(2,1)S(1)} %attend.3.refs_2_.refs_1_, f32[4,2,256,256]{3,2,1,0:T(8,128)S(1)} %collective-permute-done.3.refs_3_, ...), custom_call_target="tpu_custom_call" | custom-call | flops 536870912 | bytes 2097152 | tf_op jit(solution)/shard_map/second_hop/pallas_call | solution.py:185
  70.4 1.0 %collective-permute-start.12 = (f32[2,2,256,256]{3,2,1,0:T(8,128)S(1)}, f32[2,2,256,256]{3,2,1,0:T(8,128)S(1)}, u32[]{:S(2)}, u32[]{:S(2)}) collective-permute-start(f32[2,2,256,256]{3,2,1,0:T(8,128)S(1)} %get-tuple-element.42), channel_id=1, source_target_pairs={{0,16},{1,3},{2,18},{3,1},{16,0},{17,19},{18,2},{19,17},{4,20},{5,... | collective-permute-start | bytes 3145736 | tf_op jit(solution)/shard_map/ppermute | solution.py:506
  71.4 19.8 %collective-permute-done.13.moved_ref = f32[2,2,256,256]{3,2,1,0:T(8,128)S(1)} collective-permute-done((f32[2,2,256,256]{3,2,1,0:T(8,128)S(1)}, f32[2,2,256,256]{3,2,1,0:T(8,128)S(1)}, u32[]{:S(2)}, u32[]{:S(2)}) %collective-permute-start.13) | collective-permute-done | bytes 1048608 | tf_op jit(solution)/shard_map/ppermute | solution.py:506
  91.2 1.0 %settle.1 = (f32[256,512]{1,0:T(8,128)}, f32[256,512]{1,0:T(8,128)}, f32[256,512]{1,0:T(8,128)}, f32[512,256]{1,0:T(8,128)}) custom-call(s32[1]{0:T(128)} %bitcast.number_ref.refs_0_, f32[2,2,256,256]{3,2,1,0:T(8,128)S(1)} %get-tuple-element.40.refs_7_.kept_ref, f32[2,2,256,256]{3,2,1,0:T(8,128)S(1)} %collective-permute-done.13.moved_ref, ...), custom_call_target="tpu_custom_call" | custom-call | bytes 2097152 | tf_op jit(solution)/shard_map/settle/pallas_call | solution.py:424
  92.2 3.7 %collective-permute-done.8.refs_2_ = f32[512,512]{1,0:T(8,128)S(1)} collective-permute-done((f32[512,512]{1,0:T(8,128)S(1)}, f32[512,512]{1,0:T(8,128)S(1)}, u32[]{:S(2)}, u32[]{:S(2)}) %collective-permute-start.8) | collective-permute-done | bytes 1048608 | tf_op jit(solution)/shard_map/ppermute | solution.py:456
  96.0 0.0 collective-permute-done.6.refs_1_
  96.0 0.0 collective-permute-done.12.refs_4_
  96.0 1.2 %finish.1 = (bf16[512,512]{1,0:T(8,128)(2,1)}, f32[256,512]{1,0:T(8,128)}, f32[256,512]{1,0:T(8,128)}, f32[256,512]{1,0:T(8,128)}, f32[512,256]{1,0:T(8,128)}) custom-call(s32[1]{0:T(128)} %bitcast.number_ref.refs_0_, f32[512,512]{1,0:T(8,128)S(1)} %head_terms.6.refs_5_.refs_0_, ...), custom_call_target="tpu_custom_call", output_to_operand_aliasing={{1}: (6, {}), {2}: (7, {}), {3}: (8, {}), {4}: (9, {})} | custom-call | bytes 2097152 | tf_op jit(solution)/shard_map/finish/pallas_call | solution.py:434
Async XLA Ops:
  5.8 10.5 %collective-permute-start = (f32[4,128,128]{2,1,0:T(8,128)S(1)}, f32[4,128,128]{2,1,0:T(8,128)S(1)}, u32[]{:S(2)}, u32[]{:S(2)}) collective-permute-start(f32[4,128,128]{2,1,0:T(8,128)S(1)} %get-tuple-element.35), channel_id=1, source_target_pairs={{0,16},{16,0},{1,17},{17,1},{2,18},{18,2},{3,19},{19,3},{4,20},{20... | collective-permute-start | bytes 786440 | tf_op jit(solution)/shard_map/ppermute | solution.py:456
  14.9 4.8 %collective-permute-start.4 = (f32[4,2,256,256]{3,2,1,0:T(8,128)S(1)}, f32[4,2,256,256]{3,2,1,0:T(8,128)S(1)}, u32[]{:S(2)}, u32[]{:S(2)}) collective-permute-start(f32[4,2,256,256]{3,2,1,0:T(8,128)S(1)} %other_core.2.refs_3_), channel_id=1, source_target_pairs={{0,1},{1,0},{2,3},{3,2},{4,5},{5,4},{6,7},{7,6},{8,9},{9,8},{10,11... | collective-permute-start | bytes 6291464 | tf_op jit(solution)/shard_map/ppermute | solution.py:456
  15.8 8.1 %collective-permute-start.3 = (f32[4,2,256,256]{3,2,1,0:T(8,128)S(1)}, f32[4,2,256,256]{3,2,1,0:T(8,128)S(1)}, u32[]{:S(2)}, u32[]{:S(2)}) collective-permute-start(f32[4,2,256,256]{3,2,1,0:T(8,128)S(1)} %other_core.3.refs_6_), channel_id=1, source_target_pairs={{0,1},{1,0},{2,3},{3,2},{4,5},{5,4},{6,7},{7,6},{8,9},{9,8},{10,11... | collective-permute-start | bytes 6291464 | tf_op jit(solution)/shard_map/ppermute | solution.py:456
  19.1 7.0 %collective-permute-start.2 = (f32[4,2,256,256]{3,2,1,0:T(8,128)S(1)}, f32[4,2,256,256]{3,2,1,0:T(8,128)S(1)}, u32[]{:S(2)}, u32[]{:S(2)}) collective-permute-start(f32[4,2,256,256]{3,2,1,0:T(8,128)S(1)} %get-tuple-element.39.refs_4_), channel_id=1, source_target_pairs={{0,1},{1,0},{2,3},{3,2},{4,5},{5,4},{6,7},{7,6},{8,9},{9,8},{10,11... | collective-permute-start | bytes 6291464 | tf_op jit(solution)/shard_map/ppermute | solution.py:456
  19.2 8.9 %collective-permute-start.1 = (f32[4,2,256,256]{3,2,1,0:T(8,128)S(1)}, f32[4,2,256,256]{3,2,1,0:T(8,128)S(1)}, u32[]{:S(2)}, u32[]{:S(2)}) collective-permute-start(f32[4,2,256,256]{3,2,1,0:T(8,128)S(1)} %get-tuple-element.38), channel_id=1, source_target_pairs={{0,1},{1,0},{2,3},{3,2},{4,5},{5,4},{6,7},{7,6},{8,9},{9,8},{10,11... | collective-permute-start | bytes 6291464 | tf_op jit(solution)/shard_map/ppermute | solution.py:456
  20.2 22.7 %collective-permute-start.5 = (f32[2,2,256,256]{3,2,1,0:T(8,128)S(1)}, f32[2,2,256,256]{3,2,1,0:T(8,128)S(1)}, u32[]{:S(2)}, u32[]{:S(2)}) collective-permute-start(f32[2,2,256,256]{3,2,1,0:T(8,128)S(1)} %first_hop.4.refs_5_), channel_id=1, source_target_pairs={{0,16},{1,3},{2,18},{3,1},{16,0},{17,19},{18,2},{19,17},{4,20},{5,... | collective-permute-start | bytes 3145736 | tf_op jit(solution)/shard_map/ppermute | solution.py:506
  22.2 26.1 %collective-permute-start.7 = (f32[512,512]{1,0:T(8,128)S(1)}, f32[512,512]{1,0:T(8,128)S(1)}, u32[]{:S(2)}, u32[]{:S(2)}) collective-permute-start(f32[512,512]{1,0:T(8,128)S(1)} %head_terms.4.refs_4_), channel_id=1, source_target_pairs={{0,4},{4,0},{8,12},{12,8},{1,5},{5,1},{9,13},{13,9},{2,6},{6,2},{1... | collective-permute-start | bytes 3145736 | tf_op jit(solution)/shard_map/ppermute | solution.py:456
  24.4 26.7 %collective-permute-start.9 = (f32[2,2,256,256]{3,2,1,0:T(8,128)S(1)}, f32[2,2,256,256]{3,2,1,0:T(8,128)S(1)}, u32[]{:S(2)}, u32[]{:S(2)}) collective-permute-start(f32[2,2,256,256]{3,2,1,0:T(8,128)S(1)} %first_hop.5.refs_4_), channel_id=1, source_target_pairs={{0,2},{1,17},{2,0},{3,19},{16,18},{17,1},{18,16},{19,3},{4,6},{5,2... | collective-permute-start | bytes 3145736 | tf_op jit(solution)/shard_map/ppermute | solution.py:506
  26.6 38.8 %collective-permute-start.11 = (f32[2,2,256,256]{3,2,1,0:T(8,128)S(1)}, f32[2,2,256,256]{3,2,1,0:T(8,128)S(1)}, u32[]{:S(2)}, u32[]{:S(2)}) collective-permute-start(f32[2,2,256,256]{3,2,1,0:T(8,128)S(1)} %first_hop.6.refs_4_), channel_id=1, source_target_pairs={{0,16},{1,3},{2,18},{3,1},{16,0},{17,19},{18,2},{19,17},{4,20},{5,... | collective-permute-start | bytes 3145736 | tf_op jit(solution)/shard_map/ppermute | solution.py:506
  28.6 40.6 %collective-permute-start.10 = (f32[2,2,256,256]{3,2,1,0:T(8,128)S(1)}, f32[2,2,256,256]{3,2,1,0:T(8,128)S(1)}, u32[]{:S(2)}, u32[]{:S(2)}) collective-permute-start(f32[2,2,256,256]{3,2,1,0:T(8,128)S(1)} %first_hop.7.refs_5_), channel_id=1, source_target_pairs={{0,2},{1,17},{2,0},{3,19},{16,18},{17,1},{18,16},{19,3},{4,6},{5,2... | collective-permute-start | bytes 3145736 | tf_op jit(solution)/shard_map/ppermute | solution.py:506
  43.9 52.1 %collective-permute-start.6 = (f32[512,512]{1,0:T(8,128)S(1)}, f32[512,512]{1,0:T(8,128)S(1)}, u32[]{:S(2)}, u32[]{:S(2)}) collective-permute-start(f32[512,512]{1,0:T(8,128)S(1)} %head_terms.7.refs_2_), channel_id=1, source_target_pairs={{0,4},{4,0},{8,12},{12,8},{1,5},{5,1},{9,13},{13,9},{2,6},{6,2},{1... | collective-permute-start | bytes 3145736 | tf_op jit(solution)/shard_map/ppermute | solution.py:456
  48.4 47.6 %collective-permute-start.8 = (f32[512,512]{1,0:T(8,128)S(1)}, f32[512,512]{1,0:T(8,128)S(1)}, u32[]{:S(2)}, u32[]{:S(2)}) collective-permute-start(f32[512,512]{1,0:T(8,128)S(1)} %add.9.refs_7_), channel_id=1, source_target_pairs={{0,8},{4,12},{8,0},{12,4},{1,9},{5,13},{9,1},{13,5},{2,10},{6,14},... | collective-permute-start | bytes 3145736 | tf_op jit(solution)/shard_map/ppermute | solution.py:456
  66.6 24.6 %collective-permute-start.13 = (f32[2,2,256,256]{3,2,1,0:T(8,128)S(1)}, f32[2,2,256,256]{3,2,1,0:T(8,128)S(1)}, u32[]{:S(2)}, u32[]{:S(2)}) collective-permute-start(f32[2,2,256,256]{3,2,1,0:T(8,128)S(1)} %get-tuple-element.43), channel_id=1, source_target_pairs={{0,2},{1,17},{2,0},{3,19},{16,18},{17,1},{18,16},{19,3},{4,6},{5,2... | collective-permute-start | bytes 3145736 | tf_op jit(solution)/shard_map/ppermute | solution.py:506
  70.4 25.6 %collective-permute-start.12 = (f32[2,2,256,256]{3,2,1,0:T(8,128)S(1)}, f32[2,2,256,256]{3,2,1,0:T(8,128)S(1)}, u32[]{:S(2)}, u32[]{:S(2)}) collective-permute-start(f32[2,2,256,256]{3,2,1,0:T(8,128)S(1)} %get-tuple-element.42), channel_id=1, source_target_pairs={{0,16},{1,3},{2,18},{3,1},{16,0},{17,19},{18,2},{19,17},{4,20},{5,... | collective-permute-start | bytes 3145736 | tf_op jit(solution)/shard_map/ppermute | solution.py:506

commit v6 on v5

--- a/solution.py
+++ b/solution.py
@@ -541,10 +541,10 @@
     at, far[0][1] = to_core(early, 0, 1, [at])
     d = attend(place, lambda at: 1 - at.seq, lambda which: 1 - which, projected, (state, early, scores), [at])
     at, far[1][:] = both_to_core(d, 1, [])
-    at, over1 = first_hop(0, 0, [at])
     t3 = term(3, [at])
     t3_in = swap(t3, "head", 1)
-    at, over2 = first_hop(0, 1, [t3])
+    at, over1 = first_hop(0, 0, [t3])
+    at, over2 = first_hop(0, 1, [at])
     at, over3 = first_hop(1, 0, [at])
     at, over4 = first_hop(1, 1, [at])
     t2 = term(2, [at])

time: 97.5 us -> 97.5 us (level)
    ppermute x8, waiting for transfers between devices: 5.75 us -> 0.79 us  [swap(): lax.ppermute(x, axis, [(i, i ^ bit) for i in range(lax.axis_size(axis))])]
    ppermute x6, waiting for transfers between devices: 44.7 us -> 49.5 us  [hop(): return lax.ppermute(array, ('seq', 'dp'), pairs)]
  transfers between devices with their start and end apart: 14 -> 14, of which waited for: 6 -> 5; matrix products, arithmetic and copies ran while one was open for 0% -> 0% of each run, Pallas kernels for 19% -> 20%
where the time goes in v6:
time: 97.5 us; the launch traced here: 97.3 us
  waiting for transfers between devices  50.3 us (52%)
  Pallas kernels  25.4 us (26%)
  starting transfers between devices  20.6 us (21%)
    ppermute x6, waiting for transfers between devices, hop(): return lax.ppermute(array, ('seq', 'dp'), pairs)  49.5 us
    pallas_call x17, Pallas kernels, call(): pl.pallas_call(body, out_shape=out_shape, in_specs=[IN_SMEM] * len(number...  17.9 us
    ppermute x8, starting transfers between devices, swap(): lax.ppermute(x, axis, [(i, i ^ bit) for i in range(lax.axis_size(axis))])  11.7 us
    ppermute x6, starting transfers between devices, hop(): return lax.ppermute(array, ('seq', 'dp'), pairs)  8.94 us
    pallas_call x1, Pallas kernels, load(): pl.pallas_call(functools.partial(load_kernel, sizes=sizes, which=which),...  5.2 us
  transfers between devices with their start and end apart: 14, of which 5 were waited for; matrix products, arithmetic and copies ran while one was open for 0% of the time, Pallas kernels for 20%

profile of v6, /device:TPU:0, one launch (start us, length us, event | category | flops | bytes accessed | tf_op | source)
XLA Modules:
  0.0 97.3 jit_solution(601263524131985862)
XLA Ops:
  0.6 5.2 %load.1 = (bf16[2,512,512]{2,1,0:T(8,128)(2,1)S(1)}, f32[4,128,128]{2,1,0:T(8,128)S(1)}, bf16[2,512,2048]{2,1,0:T(8,128)(2,1)S(1)}, bf16[2048,512]{1,0:T(8,128)(...) custom-call(s32[1]{0:T(128)} %bitcast.number_ref.refs_0_, ...), custom_call_target="tpu_custom_call" | custom-call | flops 2147483648 | bytes 14680064 | tf_op jit(solution)/shard_map/load/pallas_call | solution.py:139
  5.8 3.4 %collective-permute-start = (f32[4,128,128]{2,1,0:T(8,128)S(1)}, f32[4,128,128]{2,1,0:T(8,128)S(1)}, u32[]{:S(2)}, u32[]{:S(2)}) collective-permute-start(f32[4,128,128]{2,1,0:T(8,128)S(1)} %get-tuple-element.35), channel_id=1, source_target_pairs={{0,16},{16,0},{1,17},{17,1},{2,18},{18,2},{3,19},{19,3},{4,20},{20... | collective-permute-start | bytes 786440 | tf_op jit(solution)/shard_map/ppermute | solution.py:456
  9.2 2.3 %project.1.refs_2_ = bf16[2,512,512]{2,1,0:T(8,128)(2,1)S(1)} custom-call(s32[1]{0:T(128)} %bitcast.number_ref.refs_0_, bf16[2,512,2048]{2,1,0:T(8,128)(2,1)S(1)} %get-tuple-element.30.refs_1_, bf16[2048,512]{1,0:T(8,128)(2,1)S(1)} %get-tuple-element.31.refs_2_, bf16[2048,512]{1,0:T(8,128)(2,1)S(1)} %get-tuple-element.32.refs_3_, ...), custom_call_target="tpu_custom_call" | custom-call | flops 2147483648 | bytes 2097152 | tf_op jit(solution)/shard_map/project/pallas_call | solution.py:185
  11.6 2.5 %attend.2 = (bf16[4,512,512]{2,1,0:T(8,128)(2,1)S(1)}, bf16[4,6,256,256]{3,2,1,0:T(8,128)(2,1)S(1)}) custom-call(s32[1]{0:T(128)} %bitcast.number_ref.refs_0_, bf16[2,512,512]{2,1,0:T(8,128)(2,1)S(1)} %get-tuple-element.29.refs_1_, bf16[2,512,512]{2,1,0:T(8,128)(2,1)S(1)} %project.1.refs_2_), custom_call_target="tpu_custom_call" | custom-call | flops 17179869184 | bytes 2097152 | tf_op jit(solution)/shard_map/attend/pallas_call | solution.py:185
  14.0 0.8 other_core.2.refs_3_
  14.9 0.1 collective-permute-start.4
  15.0 0.9 other_core.3.refs_6_
  15.8 0.5 collective-permute-start.3
  16.4 0.0 collective-permute-done.refs_3_
  16.4 1.4 %attend.3.refs_2_.refs_1_ = bf16[4,512,512]{2,1,0:T(8,128)(2,1)S(1)} custom-call(s32[1]{0:T(128)} %bitcast.number_ref.refs_0_, bf16[2,512,512]{2,1,0:T(8,128)(2,1)S(1)} %get-tuple-element.29.refs_1_, bf16[2,512,512]{2,1,0:T(8,128)(2,1)S(1)} %project.1.refs_2_, f32[4,128,128]{2,1,0:T(8,128)S(1)} %collective-permute-done.refs_3_, ...), custom_call_target="tpu_custom_call" | custom-call | flops 17179869184 | bytes 2097152 | tf_op jit(solution)/shard_map/attend/pallas_call | solution.py:185
  17.8 1.3 %other_core_both.1 = (f32[4,2,256,256]{3,2,1,0:T(8,128)S(1)}, f32[4,2,256,256]{3,2,1,0:T(8,128)S(1)}) custom-call(s32[1]{0:T(128)} %bitcast.number_ref.refs_0_, bf16[2,512,2048]{2,1,0:T(8,128)(2,1)S(1)} %get-tuple-element.30.refs_1_, bf16[4,512,512]{2,1,0:T(8,128)(2,1)S(1)} %attend.3.refs_2_.refs_1_), custom_call_target="tpu_custom_call" | custom-call | flops 1073741824 | bytes 2097152 | tf_op jit(solution)/shard_map/other_core_both/pallas_call | solution.py:185
  19.1 0.1 collective-permute-start.2
  19.2 0.5 collective-permute-start.1
  19.6 1.0 %head_terms.4.refs_4_ = f32[512,512]{1,0:T(8,128)S(1)} custom-call(s32[1]{0:T(128)} %bitcast.number_ref.refs_0_, bf16[4,512,512]{2,1,0:T(8,128)(2,1)S(1)} %attend.3.refs_2_.refs_1_, bf16[2048,512]{1,0:T(8,128)(2,1)S(1)} %get-tuple-element.31.refs_2_, bf16[2048,512]{1,0:T(8,128)(2,1)S(1)} %get-tuple-element.32.refs_3_, ...), custom_call_target="tpu_custom_call" | custom-call | flops 805306368 | bytes 2097152 | tf_op jit(solution)/shard_map/head_terms/pallas_call | solution.py:185
  20.7 0.0 collective-permute-done.4.refs_3_
  20.7 0.6 first_hop.4.refs_4_
  21.2 1.0 %collective-permute-start.5 = (f32[2,2,256,256]{3,2,1,0:T(8,128)S(1)}, f32[2,2,256,256]{3,2,1,0:T(8,128)S(1)}, u32[]{:S(2)}, u32[]{:S(2)}) collective-permute-start(f32[2,2,256,256]{3,2,1,0:T(8,128)S(1)} %first_hop.4.refs_4_), channel_id=1, source_target_pairs={{0,16},{1,3},{2,18},{3,1},{16,0},{17,19},{18,2},{19,17},{4,20},{5,... | collective-permute-start | bytes 3145736 | tf_op jit(solution)/shard_map/ppermute | solution.py:506
  22.2 1.6 %collective-permute-start.7 = (f32[512,512]{1,0:T(8,128)S(1)}, f32[512,512]{1,0:T(8,128)S(1)}, u32[]{:S(2)}, u32[]{:S(2)}) collective-permute-start(f32[512,512]{1,0:T(8,128)S(1)} %head_terms.4.refs_4_), channel_id=1, source_target_pairs={{0,4},{4,0},{8,12},{12,8},{1,5},{5,1},{9,13},{13,9},{2,6},{6,2},{1... | collective-permute-start | bytes 3145736 | tf_op jit(solution)/shard_map/ppermute | solution.py:456
  23.9 0.0 collective-permute-done.3.refs_3_
  23.9 0.5 first_hop.5.refs_4_
  24.4 1.6 %collective-permute-start.9 = (f32[2,2,256,256]{3,2,1,0:T(8,128)S(1)}, f32[2,2,256,256]{3,2,1,0:T(8,128)S(1)}, u32[]{:S(2)}, u32[]{:S(2)}) collective-permute-start(f32[2,2,256,256]{3,2,1,0:T(8,128)S(1)} %first_hop.5.refs_4_), channel_id=1, source_target_pairs={{0,2},{1,17},{2,0},{3,19},{16,18},{17,1},{18,16},{19,3},{4,6},{5,2... | collective-permute-start | bytes 3145736 | tf_op jit(solution)/shard_map/ppermute | solution.py:506
  26.0 0.0 collective-permute-done.2.refs_3_.refs_4_
  26.0 0.5 first_hop.6.refs_4_
  26.5 1.1 %collective-permute-start.11 = (f32[2,2,256,256]{3,2,1,0:T(8,128)S(1)}, f32[2,2,256,256]{3,2,1,0:T(8,128)S(1)}, u32[]{:S(2)}, u32[]{:S(2)}) collective-permute-start(f32[2,2,256,256]{3,2,1,0:T(8,128)S(1)} %first_hop.6.refs_4_), channel_id=1, source_target_pairs={{0,16},{1,3},{2,18},{3,1},{16,0},{17,19},{18,2},{19,17},{4,20},{5,... | collective-permute-start | bytes 3145736 | tf_op jit(solution)/shard_map/ppermute | solution.py:506
  27.6 0.5 collective-permute-done.1.refs_3_.refs_4_
  28.1 0.5 first_hop.7.refs_5_
  28.6 1.6 %collective-permute-start.10 = (f32[2,2,256,256]{3,2,1,0:T(8,128)S(1)}, f32[2,2,256,256]{3,2,1,0:T(8,128)S(1)}, u32[]{:S(2)}, u32[]{:S(2)}) collective-permute-start(f32[2,2,256,256]{3,2,1,0:T(8,128)S(1)} %first_hop.7.refs_5_), channel_id=1, source_target_pairs={{0,2},{1,17},{2,0},{3,19},{16,18},{17,1},{18,16},{19,3},{4,6},{5,2... | collective-permute-start | bytes 3145736 | tf_op jit(solution)/shard_map/ppermute | solution.py:506
  30.2 1.0 %head_terms.5.refs_5_.refs_0_ = f32[512,512]{1,0:T(8,128)S(1)} custom-call(s32[1]{0:T(128)} %bitcast.number_ref.refs_0_, bf16[4,512,512]{2,1,0:T(8,128)(2,1)S(1)} %attend.3.refs_2_.refs_1_, bf16[2048,512]{1,0:T(8,128)(2,1)S(1)} %get-tuple-element.31.refs_2_, bf16[2048,512]{1,0:T(8,128)(2,1)S(1)} %get-tuple-element.32.refs_3_, ...), custom_call_target="tpu_custom_call" | custom-call | flops 805306368 | bytes 2097152 | tf_op jit(solution)/shard_map/head_terms/pallas_call | solution.py:185
  31.2 1.0 %head_terms.6.refs_5_.refs_0_ = f32[512,512]{1,0:T(8,128)S(1)} custom-call(s32[1]{0:T(128)} %bitcast.number_ref.refs_0_, bf16[4,512,512]{2,1,0:T(8,128)(2,1)S(1)} %attend.3.refs_2_.refs_1_, bf16[2048,512]{1,0:T(8,128)(2,1)S(1)} %get-tuple-element.31.refs_2_, bf16[2048,512]{1,0:T(8,128)(2,1)S(1)} %get-tuple-element.32.refs_3_, ...), custom_call_target="tpu_custom_call" | custom-call | flops 805306368 | bytes 2097152 | tf_op jit(solution)/shard_map/head_terms/pallas_call | solution.py:185
  32.3 12.7 %collective-permute-done.5.refs_6_.refs_5_ = f32[2,2,256,256]{3,2,1,0:T(8,128)S(1)} collective-permute-done((f32[2,2,256,256]{3,2,1,0:T(8,128)S(1)}, f32[2,2,256,256]{3,2,1,0:T(8,128)S(1)}, u32[]{:S(2)}, u32[]{:S(2)}) %collective-permute-start.5) | collective-permute-done | bytes 1048608 | tf_op jit(solution)/shard_map/ppermute | solution.py:506
  45.0 1.0 %head_terms.7.refs_2_ = f32[512,512]{1,0:T(8,128)S(1)} custom-call(s32[1]{0:T(128)} %bitcast.number_ref.refs_0_, bf16[4,512,512]{2,1,0:T(8,128)(2,1)S(1)} %attend.3.refs_2_.refs_1_, bf16[2048,512]{1,0:T(8,128)(2,1)S(1)} %get-tuple-element.31.refs_2_, bf16[2048,512]{1,0:T(8,128)(2,1)S(1)} %get-tuple-element.32.refs_3_, ...), custom_call_target="tpu_custom_call" | custom-call | flops 805306368 | bytes 2097152 | tf_op jit(solution)/shard_map/head_terms/pallas_call | solution.py:185
  46.0 2.8 %collective-permute-start.6 = (f32[512,512]{1,0:T(8,128)S(1)}, f32[512,512]{1,0:T(8,128)S(1)}, u32[]{:S(2)}, u32[]{:S(2)}) collective-permute-start(f32[512,512]{1,0:T(8,128)S(1)} %head_terms.7.refs_2_), channel_id=1, source_target_pairs={{0,4},{4,0},{8,12},{12,8},{1,5},{5,1},{9,13},{13,9},{2,6},{6,2},{1... | collective-permute-start | bytes 3145736 | tf_op jit(solution)/shard_map/ppermute | solution.py:456
  48.8 0.0 collective-permute-done.7.refs_1_
  48.9 0.2 add.9.refs_7_
  49.0 2.7 %collective-permute-start.8 = (f32[512,512]{1,0:T(8,128)S(1)}, f32[512,512]{1,0:T(8,128)S(1)}, u32[]{:S(2)}, u32[]{:S(2)}) collective-permute-start(f32[512,512]{1,0:T(8,128)S(1)} %add.9.refs_7_), channel_id=1, source_target_pairs={{0,8},{4,12},{8,0},{12,4},{1,9},{5,13},{9,1},{13,5},{2,10},{6,14},... | collective-permute-start | bytes 3145736 | tf_op jit(solution)/shard_map/ppermute | solution.py:456
  51.7 0.0 collective-permute-done.9.refs_8_.refs_5_
  51.7 15.8 %collective-permute-done.11.refs_6_ = f32[2,2,256,256]{3,2,1,0:T(8,128)S(1)} collective-permute-done((f32[2,2,256,256]{3,2,1,0:T(8,128)S(1)}, f32[2,2,256,256]{3,2,1,0:T(8,128)S(1)}, u32[]{:S(2)}, u32[]{:S(2)}) %collective-permute-start.11) | collective-permute-done | bytes 1048608 | tf_op jit(solution)/shard_map/ppermute | solution.py:506
  67.5 1.2 %second_hop.2 = (f32[2,2,256,256]{3,2,1,0:T(8,128)S(1)}, f32[2,2,256,256]{3,2,1,0:T(8,128)S(1)}) custom-call(s32[1]{0:T(128)} %bitcast.number_ref.refs_0_, bf16[2,512,2048]{2,1,0:T(8,128)(2,1)S(1)} %get-tuple-element.30.refs_1_, bf16[4,512,512]{2,1,0:T(8,128)(2,1)S(1)} %attend.3.refs_2_.refs_1_, f32[4,2,256,256]{3,2,1,0:T(8,128)S(1)} %collective-permute-done.4.refs_3_, ...), custom_call_target="tpu_custom_call" | custom-call | flops 536870912 | bytes 2097152 | tf_op jit(solution)/shard_map/second_hop/pallas_call | solution.py:185
  68.7 2.6 %collective-permute-start.13 = (f32[2,2,256,256]{3,2,1,0:T(8,128)S(1)}, f32[2,2,256,256]{3,2,1,0:T(8,128)S(1)}, u32[]{:S(2)}, u32[]{:S(2)}) collective-permute-start(f32[2,2,256,256]{3,2,1,0:T(8,128)S(1)} %get-tuple-element.43), channel_id=1, source_target_pairs={{0,2},{1,17},{2,0},{3,19},{16,18},{17,1},{18,16},{19,3},{4,6},{5,2... | collective-permute-start | bytes 3145736 | tf_op jit(solution)/shard_map/ppermute | solution.py:506
  71.3 0.0 collective-permute-done.10.refs_6_
  71.3 1.2 %second_hop.3 = (f32[2,2,256,256]{3,2,1,0:T(8,128)S(1)}, f32[2,2,256,256]{3,2,1,0:T(8,128)S(1)}) custom-call(s32[1]{0:T(128)} %bitcast.number_ref.refs_0_, bf16[2,512,2048]{2,1,0:T(8,128)(2,1)S(1)} %get-tuple-element.30.refs_1_, bf16[4,512,512]{2,1,0:T(8,128)(2,1)S(1)} %attend.3.refs_2_.refs_1_, f32[4,2,256,256]{3,2,1,0:T(8,128)S(1)} %collective-permute-done.3.refs_3_, ...), custom_call_target="tpu_custom_call" | custom-call | flops 536870912 | bytes 2097152 | tf_op jit(solution)/shard_map/second_hop/pallas_call | solution.py:185
  72.5 1.1 %collective-permute-start.12 = (f32[2,2,256,256]{3,2,1,0:T(8,128)S(1)}, f32[2,2,256,256]{3,2,1,0:T(8,128)S(1)}, u32[]{:S(2)}, u32[]{:S(2)}) collective-permute-start(f32[2,2,256,256]{3,2,1,0:T(8,128)S(1)} %get-tuple-element.42), channel_id=1, source_target_pairs={{0,16},{1,3},{2,18},{3,1},{16,0},{17,19},{18,2},{19,17},{4,20},{5,... | collective-permute-start | bytes 3145736 | tf_op jit(solution)/shard_map/ppermute | solution.py:506
  73.6 21.0 %collective-permute-done.13.moved_ref = f32[2,2,256,256]{3,2,1,0:T(8,128)S(1)} collective-permute-done((f32[2,2,256,256]{3,2,1,0:T(8,128)S(1)}, f32[2,2,256,256]{3,2,1,0:T(8,128)S(1)}, u32[]{:S(2)}, u32[]{:S(2)}) %collective-permute-start.13) | collective-permute-done | bytes 1048608 | tf_op jit(solution)/shard_map/ppermute | solution.py:506
  94.6 1.0 %settle.1 = (f32[256,512]{1,0:T(8,128)}, f32[256,512]{1,0:T(8,128)}, f32[256,512]{1,0:T(8,128)}, f32[512,256]{1,0:T(8,128)}) custom-call(s32[1]{0:T(128)} %bitcast.number_ref.refs_0_, f32[2,2,256,256]{3,2,1,0:T(8,128)S(1)} %get-tuple-element.40.refs_7_.kept_ref, f32[2,2,256,256]{3,2,1,0:T(8,128)S(1)} %collective-permute-done.13.moved_ref, ...), custom_call_target="tpu_custom_call" | custom-call | bytes 2097152 | tf_op jit(solution)/shard_map/settle/pallas_call | solution.py:424
  95.6 0.3 collective-permute-done.8.refs_2_
  95.9 0.0 collective-permute-done.6.refs_1_
  95.9 0.0 collective-permute-done.12.refs_4_
  95.9 1.2 %finish.1 = (bf16[512,512]{1,0:T(8,128)(2,1)}, f32[256,512]{1,0:T(8,128)}, f32[256,512]{1,0:T(8,128)}, f32[256,512]{1,0:T(8,128)}, f32[512,256]{1,0:T(8,128)}) custom-call(s32[1]{0:T(128)} %bitcast.number_ref.refs_0_, f32[512,512]{1,0:T(8,128)S(1)} %head_terms.6.refs_5_.refs_0_, ...), custom_call_target="tpu_custom_call", output_to_operand_aliasing={{1}: (6, {}), {2}: (7, {}), {3}: (8, {}), {4}: (9, {})} | custom-call | bytes 2097152 | tf_op jit(solution)/shard_map/finish/pallas_call | solution.py:434
Async XLA Ops:
  5.8 10.5 %collective-permute-start = (f32[4,128,128]{2,1,0:T(8,128)S(1)}, f32[4,128,128]{2,1,0:T(8,128)S(1)}, u32[]{:S(2)}, u32[]{:S(2)}) collective-permute-start(f32[4,128,128]{2,1,0:T(8,128)S(1)} %get-tuple-element.35), channel_id=1, source_target_pairs={{0,16},{16,0},{1,17},{17,1},{2,18},{18,2},{3,19},{19,3},{4,20},{20... | collective-permute-start | bytes 786440 | tf_op jit(solution)/shard_map/ppermute | solution.py:456
  14.9 5.8 %collective-permute-start.4 = (f32[4,2,256,256]{3,2,1,0:T(8,128)S(1)}, f32[4,2,256,256]{3,2,1,0:T(8,128)S(1)}, u32[]{:S(2)}, u32[]{:S(2)}) collective-permute-start(f32[4,2,256,256]{3,2,1,0:T(8,128)S(1)} %other_core.2.refs_3_), channel_id=1, source_target_pairs={{0,1},{1,0},{2,3},{3,2},{4,5},{5,4},{6,7},{7,6},{8,9},{9,8},{10,11... | collective-permute-start | bytes 6291464 | tf_op jit(solution)/shard_map/ppermute | solution.py:456
  15.8 8.0 %collective-permute-start.3 = (f32[4,2,256,256]{3,2,1,0:T(8,128)S(1)}, f32[4,2,256,256]{3,2,1,0:T(8,128)S(1)}, u32[]{:S(2)}, u32[]{:S(2)}) collective-permute-start(f32[4,2,256,256]{3,2,1,0:T(8,128)S(1)} %other_core.3.refs_6_), channel_id=1, source_target_pairs={{0,1},{1,0},{2,3},{3,2},{4,5},{5,4},{6,7},{7,6},{8,9},{9,8},{10,11... | collective-permute-start | bytes 6291464 | tf_op jit(solution)/shard_map/ppermute | solution.py:456
  19.1 6.9 %collective-permute-start.2 = (f32[4,2,256,256]{3,2,1,0:T(8,128)S(1)}, f32[4,2,256,256]{3,2,1,0:T(8,128)S(1)}, u32[]{:S(2)}, u32[]{:S(2)}) collective-permute-start(f32[4,2,256,256]{3,2,1,0:T(8,128)S(1)} %get-tuple-element.39.refs_5_), channel_id=1, source_target_pairs={{0,1},{1,0},{2,3},{3,2},{4,5},{5,4},{6,7},{7,6},{8,9},{9,8},{10,11... | collective-permute-start | bytes 6291464 | tf_op jit(solution)/shard_map/ppermute | solution.py:456
  19.2 8.9 %collective-permute-start.1 = (f32[4,2,256,256]{3,2,1,0:T(8,128)S(1)}, f32[4,2,256,256]{3,2,1,0:T(8,128)S(1)}, u32[]{:S(2)}, u32[]{:S(2)}) collective-permute-start(f32[4,2,256,256]{3,2,1,0:T(8,128)S(1)} %get-tuple-element.38), channel_id=1, source_target_pairs={{0,1},{1,0},{2,3},{3,2},{4,5},{5,4},{6,7},{7,6},{8,9},{9,8},{10,11... | collective-permute-start | bytes 6291464 | tf_op jit(solution)/shard_map/ppermute | solution.py:456
  21.2 23.8 %collective-permute-start.5 = (f32[2,2,256,256]{3,2,1,0:T(8,128)S(1)}, f32[2,2,256,256]{3,2,1,0:T(8,128)S(1)}, u32[]{:S(2)}, u32[]{:S(2)}) collective-permute-start(f32[2,2,256,256]{3,2,1,0:T(8,128)S(1)} %first_hop.4.refs_4_), channel_id=1, source_target_pairs={{0,16},{1,3},{2,18},{3,1},{16,0},{17,19},{18,2},{19,17},{4,20},{5,... | collective-permute-start | bytes 3145736 | tf_op jit(solution)/shard_map/ppermute | solution.py:506
  22.2 26.6 %collective-permute-start.7 = (f32[512,512]{1,0:T(8,128)S(1)}, f32[512,512]{1,0:T(8,128)S(1)}, u32[]{:S(2)}, u32[]{:S(2)}) collective-permute-start(f32[512,512]{1,0:T(8,128)S(1)} %head_terms.4.refs_4_), channel_id=1, source_target_pairs={{0,4},{4,0},{8,12},{12,8},{1,5},{5,1},{9,13},{13,9},{2,6},{6,2},{1... | collective-permute-start | bytes 3145736 | tf_op jit(solution)/shard_map/ppermute | solution.py:456
  24.4 27.3 %collective-permute-start.9 = (f32[2,2,256,256]{3,2,1,0:T(8,128)S(1)}, f32[2,2,256,256]{3,2,1,0:T(8,128)S(1)}, u32[]{:S(2)}, u32[]{:S(2)}) collective-permute-start(f32[2,2,256,256]{3,2,1,0:T(8,128)S(1)} %first_hop.5.refs_4_), channel_id=1, source_target_pairs={{0,2},{1,17},{2,0},{3,19},{16,18},{17,1},{18,16},{19,3},{4,6},{5,2... | collective-permute-start | bytes 3145736 | tf_op jit(solution)/shard_map/ppermute | solution.py:506
  26.5 40.9 %collective-permute-start.11 = (f32[2,2,256,256]{3,2,1,0:T(8,128)S(1)}, f32[2,2,256,256]{3,2,1,0:T(8,128)S(1)}, u32[]{:S(2)}, u32[]{:S(2)}) collective-permute-start(f32[2,2,256,256]{3,2,1,0:T(8,128)S(1)} %first_hop.6.refs_4_), channel_id=1, source_target_pairs={{0,16},{1,3},{2,18},{3,1},{16,0},{17,19},{18,2},{19,17},{4,20},{5,... | collective-permute-start | bytes 3145736 | tf_op jit(solution)/shard_map/ppermute | solution.py:506
  28.6 42.7 %collective-permute-start.10 = (f32[2,2,256,256]{3,2,1,0:T(8,128)S(1)}, f32[2,2,256,256]{3,2,1,0:T(8,128)S(1)}, u32[]{:S(2)}, u32[]{:S(2)}) collective-permute-start(f32[2,2,256,256]{3,2,1,0:T(8,128)S(1)} %first_hop.7.refs_5_), channel_id=1, source_target_pairs={{0,2},{1,17},{2,0},{3,19},{16,18},{17,1},{18,16},{19,3},{4,6},{5,2... | collective-permute-start | bytes 3145736 | tf_op jit(solution)/shard_map/ppermute | solution.py:506
  46.0 49.9 %collective-permute-start.6 = (f32[512,512]{1,0:T(8,128)S(1)}, f32[512,512]{1,0:T(8,128)S(1)}, u32[]{:S(2)}, u32[]{:S(2)}) collective-permute-start(f32[512,512]{1,0:T(8,128)S(1)} %head_terms.7.refs_2_), channel_id=1, source_target_pairs={{0,4},{4,0},{8,12},{12,8},{1,5},{5,1},{9,13},{13,9},{2,6},{6,2},{1... | collective-permute-start | bytes 3145736 | tf_op jit(solution)/shard_map/ppermute | solution.py:456
  49.0 46.9 %collective-permute-start.8 = (f32[512,512]{1,0:T(8,128)S(1)}, f32[512,512]{1,0:T(8,128)S(1)}, u32[]{:S(2)}, u32[]{:S(2)}) collective-permute-start(f32[512,512]{1,0:T(8,128)S(1)} %add.9.refs_7_), channel_id=1, source_target_pairs={{0,8},{4,12},{8,0},{12,4},{1,9},{5,13},{9,1},{13,5},{2,10},{6,14},... | collective-permute-start | bytes 3145736 | tf_op jit(solution)/shard_map/ppermute | solution.py:456
  68.7 25.9 %collective-permute-start.13 = (f32[2,2,256,256]{3,2,1,0:T(8,128)S(1)}, f32[2,2,256,256]{3,2,1,0:T(8,128)S(1)}, u32[]{:S(2)}, u32[]{:S(2)}) collective-permute-start(f32[2,2,256,256]{3,2,1,0:T(8,128)S(1)} %get-tuple-element.43), channel_id=1, source_target_pairs={{0,2},{1,17},{2,0},{3,19},{16,18},{17,1},{18,16},{19,3},{4,6},{5,2... | collective-permute-start | bytes 3145736 | tf_op jit(solution)/shard_map/ppermute | solution.py:506
  72.5 23.4 %collective-permute-start.12 = (f32[2,2,256,256]{3,2,1,0:T(8,128)S(1)}, f32[2,2,256,256]{3,2,1,0:T(8,128)S(1)}, u32[]{:S(2)}, u32[]{:S(2)}) collective-permute-start(f32[2,2,256,256]{3,2,1,0:T(8,128)S(1)} %get-tuple-element.42), channel_id=1, source_target_pairs={{0,16},{1,3},{2,18},{3,1},{16,0},{17,19},{18,2},{19,17},{4,20},{5,... | collective-permute-start | bytes 3145736 | tf_op jit(solution)/shard_map/ppermute | solution.py:506
